TPU v7x, 32 devices: a whole 2x2x4 slice. The times are simulated.
32 devices in a mesh: rep: 4 (over z), shard: 8 (over y, x, core).
Axes of the slice: x: 2, y: 2, z: 4, core: 2. Of those that a mesh axis runs over, the one named last changes fastest.
Arguments:
- inputs: bfloat16 [8192, 1024], P(('rep', 'shard')), may hold values from -6 to 6
- cotangent: bfloat16 [8192, 1024], P(('rep', 'shard')), may hold values from -6 to 6
- segments: int32 [32, 256], P(('rep', 'shard')), may hold values from 0 to 7, never falling along the last dimension, each value on 1 to 128 neighbouring positions
- w_qkv: bfloat16 [2, 1024, 3072], P(None, 'shard'), may hold values from -0.1875 to 0.1875
- w_out: bfloat16 [2, 1024, 1024], P(None, 'shard'), may hold values from -1 to 1
- w_up: bfloat16 [2, 1024, 4096], P(None, 'shard'), may hold values from -0.1875 to 0.1875
- w_down: bfloat16 [2, 4096, 1024], P(None, 'shard'), may hold values from -0.09375 to 0.09375
- bias_query: bfloat16 [2, 1024], P(None, 'shard'), may hold values from -3 to 3
- bias_value: bfloat16 [2, 1024], P(None, 'shard'), may hold values from -3 to 3
- bias_out: bfloat16 [2, 1024], P(None, 'shard'), may hold values from -2 to 2
- bias_up: bfloat16 [2, 4096], P(None, 'shard'), may hold values from -3 to 3
- bias_down: bfloat16 [2, 1024], P(None, 'shard'), may hold values from -2 to 2
- norm1_gain: bfloat16 [2, 1024], P(None, 'shard'), may hold values from 0.5 to 1.5
- norm1_bias: bfloat16 [2, 1024], P(None, 'shard'), may hold values from -2 to 2
- norm2_gain: bfloat16 [2, 1024], P(None, 'shard'), may hold values from 0.5 to 1.5
- norm2_bias: bfloat16 [2, 1024], P(None, 'shard'), may hold values from -2 to 2
- tau: float32 [2, 16], replicated, may hold values from 3 to 12
Outputs:
- output: bfloat16 [8192, 1024], P(('rep', 'shard'))
- input_grad: float32 [8192, 1024], P(('rep', 'shard'))
- grad_w_qkv: float32 [2, 1024, 3072], P(None, 'shard')
- grad_w_out: float32 [2, 1024, 1024], P(None, 'shard')
- grad_w_up: float32 [2, 1024, 4096], P(None, 'shard')
- grad_w_down: float32 [2, 4096, 1024], P(None, 'shard')
- grad_bias_query: float32 [2, 1024], P(None, 'shard')
- grad_bias_value: float32 [2, 1024], P(None, 'shard')
- grad_bias_out: float32 [2, 1024], P(None, 'shard')
- grad_bias_up: float32 [2, 4096], P(None, 'shard')
- grad_bias_down: float32 [2, 1024], P(None, 'shard')
- grad_norm1_gain: float32 [2, 1024], P(None, 'shard')
- grad_norm1_bias: float32 [2, 1024], P(None, 'shard')
- grad_norm2_gain: float32 [2, 1024], P(None, 'shard')
- grad_norm2_bias: float32 [2, 1024], P(None, 'shard')
- clipped_qk: float32 [2, 1024, 2048], P(None, 'shard')
- clipped_bias_query: float32 [2, 1024], P(None, 'shard')
Inputs may be any that keep to these rules, and one draw needn't show every extreme that they name: `segments`: segment numbers never fall along a sequence, so each document's tokens are consecutive.
All inputs are finite; a program needn't handle non-finite values.
Results may differ from a plain program's by a relative error of at most 0.019.
Values may be sent and summed in bfloat16 or wider, within the bound.
A program may use at most 256 MiB of HBM per device.

v0:
```python
import math

import jax
import jax.numpy as jnp
from jax import lax
from jax.sharding import PartitionSpec as P

HEADS = 16


epsilon = 1e-05
neg_large = -1e30


def normalize(values):
    centred = values - jnp.mean(values, axis=-1, keepdims=True)
    rstd = lax.rsqrt(jnp.mean(centred * centred, axis=-1, keepdims=True) + epsilon)
    return (centred * rstd, rstd)


def norm_back(grad_norm, normed, rstd):
    inner = jnp.mean(grad_norm * normed, axis=-1, keepdims=True)
    return rstd * (grad_norm - jnp.mean(grad_norm, axis=-1, keepdims=True) - normed * inner)


def gelu_slope(pre):
    cdf = 0.5 * (1.0 + lax.erf(pre * (1.0 / math.sqrt(2.0))))
    return cdf + pre * jnp.exp(-0.5 * pre * pre) * (1.0 / math.sqrt(2.0 * math.pi))


def masked_scores(query, key_rows, same):
    scale = 1.0 / math.sqrt(query.shape[-1])
    scores = jnp.einsum("qhd,khd->hqk", query, key_rows, preferred_element_type=jnp.float32) * scale
    return jnp.where(same[None], scores, neg_large)


def fetch_forward(pieces):
    (
        w_qkv,
        w_out,
        w_up,
        w_down,
        bias_query,
        bias_value,
        bias_out,
        bias_up,
        bias_down,
        gain_first,
        shift_first,
        gain_second,
        shift_second,
    ) = pieces
    return (
        lax.all_gather(w_qkv, "shard", axis=0, tiled=True),
        lax.all_gather(w_out, "shard", axis=0, tiled=True),
        lax.all_gather(w_up, "shard", axis=0, tiled=True),
        lax.all_gather(w_down, "shard", axis=0, tiled=True),
        lax.all_gather(bias_query, "shard", axis=0, tiled=True),
        lax.all_gather(bias_value, "shard", axis=0, tiled=True),
        lax.all_gather(bias_out, "shard", axis=0, tiled=True),
        lax.all_gather(bias_up, "shard", axis=0, tiled=True),
        lax.all_gather(bias_down, "shard", axis=0, tiled=True),
        lax.all_gather(gain_first, "shard", axis=0, tiled=True),
        lax.all_gather(shift_first, "shard", axis=0, tiled=True),
        lax.all_gather(gain_second, "shard", axis=0, tiled=True),
        lax.all_gather(shift_second, "shard", axis=0, tiled=True),
    )


def fetch_backward(pieces):
    (
        w_qkv,
        w_out,
        w_up,
        w_down,
        bias_query,
        bias_value,
        bias_out,
        bias_up,
        bias_down,
        gain_first,
        shift_first,
        gain_second,
        shift_second,
    ) = pieces
    return (
        lax.all_gather(w_qkv, "shard", axis=0, tiled=True),
        lax.all_gather(w_out, "shard", axis=0, tiled=True),
        lax.all_gather(w_up, "shard", axis=0, tiled=True),
        lax.all_gather(w_down, "shard", axis=0, tiled=True),
        lax.all_gather(bias_query, "shard", axis=0, tiled=True),
        lax.all_gather(bias_value, "shard", axis=0, tiled=True),
        lax.all_gather(bias_out, "shard", axis=0, tiled=True),
        lax.all_gather(bias_up, "shard", axis=0, tiled=True),
        lax.all_gather(bias_down, "shard", axis=0, tiled=True),
        lax.all_gather(gain_first, "shard", axis=0, tiled=True),
        lax.all_gather(shift_first, "shard", axis=0, tiled=True),
        lax.all_gather(gain_second, "shard", axis=0, tiled=True),
        lax.all_gather(shift_second, "shard", axis=0, tiled=True),
    )


def forward_layer(hidden, fetched, same):
    (
        w_qkv,
        w_out,
        w_up,
        w_down,
        bias_query,
        bias_value,
        bias_out,
        bias_up,
        bias_down,
        gain_first,
        shift_first,
        gain_second,
        shift_second,
    ) = fetched
    tokens_here, width = hidden.shape
    head_dim = width // HEADS
    hidden_low = hidden.astype(jnp.bfloat16)
    bias_row = jnp.concatenate(
        [
            bias_query.astype(jnp.float32),
            jnp.zeros((width,), jnp.float32),
            bias_value.astype(jnp.float32),
        ]
    )
    qkv = (jnp.dot(hidden_low, w_qkv, preferred_element_type=jnp.float32) + bias_row).astype(
        jnp.bfloat16
    )
    query = qkv[:, :width].reshape(tokens_here, HEADS, head_dim)
    key_rows = qkv[:, width : 2 * width].reshape(tokens_here, HEADS, head_dim)
    value_rows = qkv[:, 2 * width :].reshape(tokens_here, HEADS, head_dim)
    masked = masked_scores(query, key_rows, same)
    top = jnp.max(masked, axis=2, keepdims=True)
    expo = jnp.exp(masked - top)
    total = jnp.sum(expo, axis=2, keepdims=True)
    probs = (expo / total).astype(jnp.bfloat16)
    log_total = top + jnp.log(total)
    head_top = jnp.max(top[:, :, 0], axis=1)
    attended = jnp.einsum("hqk,khd->qhd", probs, value_rows, preferred_element_type=jnp.float32)
    attended = attended.reshape(tokens_here, width).astype(jnp.bfloat16)
    summed_one = (
        hidden
        + jnp.dot(attended, w_out, preferred_element_type=jnp.float32)
        + bias_out.astype(jnp.float32)
    )
    normed_one, rstd_one = normalize(summed_one)
    first = normed_one * gain_first.astype(jnp.float32) + shift_first.astype(jnp.float32)
    first_low = first.astype(jnp.bfloat16)
    pre = jnp.dot(first_low, w_up, preferred_element_type=jnp.float32) + bias_up.astype(jnp.float32)
    activation = jax.nn.gelu(pre, approximate=False).astype(jnp.bfloat16)
    summed_two = (
        first
        + jnp.dot(activation, w_down, preferred_element_type=jnp.float32)
        + bias_down.astype(jnp.float32)
    )
    normed_two, rstd_two = normalize(summed_two)
    result = normed_two * gain_second.astype(jnp.float32) + shift_second.astype(jnp.float32)
    saved = (
        hidden_low,
        qkv,
        log_total,
        attended,
        normed_one,
        rstd_one,
        first_low,
        pre,
        activation,
        normed_two,
        rstd_two,
    )
    return (result, head_top, saved)


def column_sums(values):
    return jnp.sum(values.astype(jnp.float32), axis=0)


def backward_layer(grad_out, fetched, same, saved):
    (
        w_qkv,
        w_out,
        w_up,
        w_down,
        bias_query,
        bias_value,
        bias_out,
        bias_up,
        bias_down,
        gain_first,
        shift_first,
        gain_second,
        shift_second,
    ) = fetched
    (
        hidden_low,
        qkv,
        log_total,
        attended,
        normed_one,
        rstd_one,
        first_low,
        pre,
        activation,
        normed_two,
        rstd_two,
    ) = saved
    tokens_here, width = hidden_low.shape
    head_dim = width // HEADS
    scale = 1.0 / math.sqrt(head_dim)
    grad_gain_second = jnp.sum(grad_out * normed_two, axis=0)
    grad_shift_second = jnp.sum(grad_out, axis=0)
    grad_sum_two = norm_back(grad_out * gain_second.astype(jnp.float32), normed_two, rstd_two)
    branch_two = grad_sum_two.astype(jnp.bfloat16)
    grad_bias_down = column_sums(branch_two)
    grad_w_down = jnp.einsum(
        "tf,td->fd", activation, branch_two, preferred_element_type=jnp.float32
    )
    grad_act = jnp.einsum("td,fd->tf", branch_two, w_down, preferred_element_type=jnp.float32)
    branch_pre = (grad_act * gelu_slope(pre)).astype(jnp.bfloat16)
    grad_bias_up = column_sums(branch_pre)
    grad_w_up = jnp.einsum("td,tf->df", first_low, branch_pre, preferred_element_type=jnp.float32)
    grad_first = grad_sum_two + jnp.einsum(
        "tf,df->td", branch_pre, w_up, preferred_element_type=jnp.float32
    )
    grad_gain_first = jnp.sum(grad_first * normed_one, axis=0)
    grad_shift_first = jnp.sum(grad_first, axis=0)
    grad_sum_one = norm_back(grad_first * gain_first.astype(jnp.float32), normed_one, rstd_one)
    branch_one = grad_sum_one.astype(jnp.bfloat16)
    grad_bias_out = column_sums(branch_one)
    grad_w_out = jnp.einsum("ti,to->io", attended, branch_one, preferred_element_type=jnp.float32)
    grad_attended = jnp.einsum("to,io->ti", branch_one, w_out, preferred_element_type=jnp.float32)
    grad_attended = grad_attended.astype(jnp.bfloat16).reshape(tokens_here, HEADS, head_dim)
    query = qkv[:, :width].reshape(tokens_here, HEADS, head_dim)
    key_rows = qkv[:, width : 2 * width].reshape(tokens_here, HEADS, head_dim)
    value_rows = qkv[:, 2 * width :].reshape(tokens_here, HEADS, head_dim)
    masked = masked_scores(query, key_rows, same)
    probs = jnp.exp(masked - log_total)
    grad_value = jnp.einsum(
        "hqk,qhd->khd",
        probs.astype(jnp.bfloat16),
        grad_attended,
        preferred_element_type=jnp.float32,
    )
    grad_probs = jnp.einsum(
        "qhd,khd->hqk", grad_attended, value_rows, preferred_element_type=jnp.float32
    )
    row_inner = jnp.sum(probs * grad_probs, axis=2, keepdims=True)
    grad_scores = (probs * (grad_probs - row_inner)).astype(jnp.bfloat16)
    grad_query = (
        jnp.einsum("hqk,khd->qhd", grad_scores, key_rows, preferred_element_type=jnp.float32)
        * scale
    )
    grad_key = (
        jnp.einsum("hqk,qhd->khd", grad_scores, query, preferred_element_type=jnp.float32) * scale
    )
    grad_qkv = jnp.concatenate(
        [
            grad_query.reshape(tokens_here, width),
            grad_key.reshape(tokens_here, width),
            grad_value.reshape(tokens_here, width),
        ],
        axis=1,
    ).astype(jnp.bfloat16)
    grad_bias_query = column_sums(grad_qkv[:, :width])
    grad_bias_value = column_sums(grad_qkv[:, 2 * width :])
    grad_w_qkv = jnp.einsum("ti,tj->ij", hidden_low, grad_qkv, preferred_element_type=jnp.float32)
    grad_hidden = grad_sum_one + jnp.einsum(
        "tj,ij->ti", grad_qkv, w_qkv, preferred_element_type=jnp.float32
    )
    terms = (
        grad_w_qkv,
        grad_w_out,
        grad_w_up,
        grad_w_down,
        grad_bias_query,
        grad_bias_value,
        grad_bias_out,
        grad_bias_up,
        grad_bias_down,
        grad_gain_first,
        grad_shift_first,
        grad_gain_second,
        grad_shift_second,
    )
    return (grad_hidden, terms)


def reduce_group(terms):
    (
        term_qkv,
        term_out,
        term_up,
        term_down,
        term_query,
        term_value,
        term_attend,
        term_hidden,
        term_final,
        gain_first,
        shift_first,
        gain_second,
        shift_second,
    ) = terms
    owned = (
        lax.psum_scatter(term_qkv, "shard", scatter_dimension=0, tiled=True),
        lax.psum_scatter(term_out, "shard", scatter_dimension=0, tiled=True),
        lax.psum_scatter(term_up, "shard", scatter_dimension=0, tiled=True),
        lax.psum_scatter(term_down, "shard", scatter_dimension=0, tiled=True),
        lax.psum_scatter(term_query, "shard", scatter_dimension=0, tiled=True),
        lax.psum_scatter(term_value, "shard", scatter_dimension=0, tiled=True),
        lax.psum_scatter(term_attend, "shard", scatter_dimension=0, tiled=True),
        lax.psum_scatter(term_hidden, "shard", scatter_dimension=0, tiled=True),
        lax.psum_scatter(term_final, "shard", scatter_dimension=0, tiled=True),
        lax.psum_scatter(gain_first, "shard", scatter_dimension=0, tiled=True),
        lax.psum_scatter(shift_first, "shard", scatter_dimension=0, tiled=True),
        lax.psum_scatter(gain_second, "shard", scatter_dimension=0, tiled=True),
        lax.psum_scatter(shift_second, "shard", scatter_dimension=0, tiled=True),
    )
    (
        term_qkv,
        term_out,
        term_up,
        term_down,
        term_query,
        term_value,
        term_attend,
        term_hidden,
        term_final,
        gain_first,
        shift_first,
        gain_second,
        shift_second,
    ) = owned
    return (
        lax.psum(term_qkv.astype(jnp.bfloat16), "rep").astype(jnp.float32),
        lax.psum(term_out.astype(jnp.bfloat16), "rep").astype(jnp.float32),
        lax.psum(term_up.astype(jnp.bfloat16), "rep").astype(jnp.float32),
        lax.psum(term_down.astype(jnp.bfloat16), "rep").astype(jnp.float32),
        lax.psum(term_query.astype(jnp.bfloat16), "rep").astype(jnp.float32),
        lax.psum(term_value.astype(jnp.bfloat16), "rep").astype(jnp.float32),
        lax.psum(term_attend.astype(jnp.bfloat16), "rep").astype(jnp.float32),
        lax.psum(term_hidden.astype(jnp.bfloat16), "rep").astype(jnp.float32),
        lax.psum(term_final.astype(jnp.bfloat16), "rep").astype(jnp.float32),
        lax.psum(gain_first.astype(jnp.bfloat16), "rep").astype(jnp.float32),
        lax.psum(shift_first.astype(jnp.bfloat16), "rep").astype(jnp.float32),
        lax.psum(gain_second.astype(jnp.bfloat16), "rep").astype(jnp.float32),
        lax.psum(shift_second.astype(jnp.bfloat16), "rep").astype(jnp.float32),
    )


def shards(
    inputs,
    cotangent,
    segments,
    w_qkv,
    w_out,
    w_up,
    w_down,
    bias_query,
    bias_value,
    bias_out,
    bias_up,
    bias_down,
    norm1_gain,
    norm1_bias,
    norm2_gain,
    norm2_bias,
    tau,
):
    layer_count = w_qkv.shape[0]
    stacked = (
        w_qkv,
        w_out,
        w_up,
        w_down,
        bias_query,
        bias_value,
        bias_out,
        bias_up,
        bias_down,
        norm1_gain,
        norm1_bias,
        norm2_gain,
        norm2_bias,
    )
    seg_row = segments[0]
    same = seg_row[:, None] == seg_row[None, :]
    hidden = inputs.astype(jnp.float32)
    saved_all = []
    fetched_all = []
    tops = []
    for layer_index in range(layer_count):
        fetched = fetch_forward(tuple((weight[layer_index] for weight in stacked)))
        hidden, head_top, saved = forward_layer(hidden, fetched, same)
        saved_all.append(saved)
        fetched_all.append(fetched)
        tops.append(head_top)
    output = hidden.astype(jnp.bfloat16)
    peak = lax.pmax(jnp.stack(tops), ("rep", "shard"))
    grad_flow = cotangent.astype(jnp.float32)
    collected = [None] * layer_count
    for layer_index in reversed(range(layer_count)):
        fetched = fetch_backward(tuple((weight[layer_index] for weight in stacked)))
        grad_flow, terms = backward_layer(grad_flow, fetched, same, saved_all[layer_index])
        collected[layer_index] = reduce_group(terms)
    gradients = tuple(
        (
            jnp.stack([collected[layer_index][member] for layer_index in range(layer_count)])
            for member in range(13)
        )
    )
    width = w_qkv.shape[2] // 3
    head_dim = width // HEADS
    factor = jnp.sqrt(tau / jnp.maximum(peak, tau))
    column_scale = jnp.repeat(factor, head_dim, axis=1)
    both_scale = jnp.concatenate([column_scale, column_scale], axis=1)
    clipped_qk = w_qkv[:, :, : 2 * width].astype(jnp.float32) * both_scale[:, None, :]
    rows_here = bias_query.shape[1]
    start = lax.axis_index("shard") * rows_here
    scale_here = lax.dynamic_slice_in_dim(column_scale, start, rows_here, 1)
    clipped_bias_query = bias_query.astype(jnp.float32) * scale_here
    return (
        output,
        grad_flow,
        gradients[0],
        gradients[1],
        gradients[2],
        gradients[3],
        gradients[4],
        gradients[5],
        gradients[6],
        gradients[7],
        gradients[8],
        gradients[9],
        gradients[10],
        gradients[11],
        gradients[12],
        clipped_qk,
        clipped_bias_query,
    )


def solution(mesh):
    in_specs = (
        P(("rep", "shard"), None),
        P(("rep", "shard"), None),
        P(("rep", "shard"), None),
        P(None, "shard", None),
        P(None, "shard", None),
        P(None, "shard", None),
        P(None, "shard", None),
        P(None, "shard"),
        P(None, "shard"),
        P(None, "shard"),
        P(None, "shard"),
        P(None, "shard"),
        P(None, "shard"),
        P(None, "shard"),
        P(None, "shard"),
        P(None, "shard"),
        P(),
    )
    out_specs = (
        P(("rep", "shard"), None),
        P(("rep", "shard"), None),
        P(None, "shard", None),
        P(None, "shard", None),
        P(None, "shard", None),
        P(None, "shard", None),
        P(None, "shard"),
        P(None, "shard"),
        P(None, "shard"),
        P(None, "shard"),
        P(None, "shard"),
        P(None, "shard"),
        P(None, "shard"),
        P(None, "shard"),
        P(None, "shard"),
        P(None, "shard", None),
        P(None, "shard"),
    )
    return jax.shard_map(shards, mesh=mesh, in_specs=in_specs, out_specs=out_specs, check_vma=False)
```

profile of v0, /device:TPU:0, one launch (start us, length us, event | category | flops | bytes accessed | tf_op | source)
XLA Modules:
  0.0 1444.9 jit_solution(7468149867409905691)
XLA Ops:
  7.3 2.8 fusion.217
  12.7 3.1 fusion.213
  18.7 10.2 all-gather.1
  28.9 8.7 all-gather.25
  37.6 7.8 all-gather.24
  45.4 8.7 all-gather.19
  54.1 7.8 all-gather.18
  61.9 8.7 all-gather.23
  70.6 7.8 all-gather.17
  78.4 8.7 all-gather.2
  87.1 7.8 all-gather.14
  94.8 8.7 all-gather.12
  103.6 7.8 all-gather.11
  111.3 8.7 all-gather.6
  120.0 7.8 all-gather.5
  127.8 8.7 all-gather.10
  136.5 7.8 all-gather.4
  144.3 8.7 all-gather.15
  153.0 7.9 all-gather.8
  161.0 9.1 all-gather.21
  170.3 4.6 fusion.79
  182.4 15.5 %fusion.44 = (bf16[256,4096]{1,0:T(8,128)(2,1)}, f32[256,4096]{1,0:T(8,128)}) fusion(f32[4096]{0:T(1024)S(1)} %bitcast.314, bf16[1,1024,4096]{2,1,0:T(8,128)(2,1)} %all-gather.39.cloned.1.call-done, f32[256,1024]{1,0:T(8,128)S(1)} %get-tuple-element.178, f32[1024]{0:T(1024)S(1)} %bitcast.297, f32[1024]{0:T(1024)S(1)} %bitcast.289, ...), kind=kOutput, calls=%fused_computation.37 | convolution fusion | flops 2218000384 | bytes 15755264 | tf_op jit(solution)/shard_map/dot_general | solution.py:152
  197.9 5.1 all-gather.41.cloned.1.call-done
  203.0 6.5 fusion.230
  209.7 41.1 %all-gather.43.cloned.1.call-done = bf16[1,1024,3072]{2,1,0:T(8,128)(2,1)} async-done(((bf16[1,128,3072]{2,1,0:T(8,128)(2,1)}), bf16[1,1024,3072]{2,1,0:T(8,128)(2,1)}) %all-gather.43.cloned.1.call-update) | async-done | bytes 6291472 | tf_op jit(solution)/shard_map/all_gather | solution.py:54
  250.8 4.7 fusion.76
  265.0 15.4 %all-gather.45.cloned.1.call-done = bf16[1,1024,1024]{2,1,0:T(8,128)(2,1)} async-done(((bf16[1,128,1024]{2,1,0:T(8,128)(2,1)}), bf16[1,1024,1024]{2,1,0:T(8,128)(2,1)}) %all-gather.45.cloned.1.call-update) | async-done | bytes 2097168 | tf_op jit(solution)/shard_map/all_gather | solution.py:55
  283.4 53.9 %all-gather.47.cloned.1.call-done = bf16[1,1024,4096]{2,1,0:T(8,128)(2,1)} async-done(((bf16[1,128,4096]{2,1,0:T(8,128)(2,1)}), bf16[1,1024,4096]{2,1,0:T(8,128)(2,1)}) %all-gather.47.cloned.1.call-update) | async-done | bytes 8388624 | tf_op jit(solution)/shard_map/all_gather | solution.py:56
  337.4 15.7 %fusion.47 = (bf16[256,4096]{1,0:T(8,128)(2,1)}, f32[256,4096]{1,0:T(8,128)}) fusion(f32[4096]{0:T(1024)S(1)} %bitcast.313, bf16[1,1024,4096]{2,1,0:T(8,128)(2,1)} %all-gather.47.cloned.1.call-done, f32[256,1024]{1,0:T(8,128)S(1)} %get-tuple-element.186, f32[1024]{0:T(1024)S(1)} %bitcast.294, f32[1024]{0:T(1024)S(1)} %bitcast.284, ...), kind=kOutput, calls=%fused_computation.40 | convolution fusion | flops 2218000384 | bytes 15755264 | tf_op jit(solution)/shard_map/dot_general | solution.py:152
  353.1 40.6 %all-gather.49.cloned.1.call-done = bf16[1,4096,1024]{2,1,0:T(8,128)(2,1)} async-done(((bf16[1,512,1024]{2,1,0:T(8,128)(2,1)}), bf16[1,4096,1024]{2,1,0:T(8,128)(2,1)}) %all-gather.49.cloned.1.call-update) | async-done | bytes 8388624 | tf_op jit(solution)/shard_map/all_gather | solution.py:57
  393.7 6.6 fusion.233
  402.5 4.3 convert_reduce_fusion
  406.9 2.7 multiply_reduce_fusion.3
  411.0 2.7 fusion.196
  413.7 3.5 fusion.150
  419.3 3.9 fusion.211
  426.4 6.9 multiply_reduce_fusion.2
  433.7 6.2 convert_reduce_fusion.1
  440.0 2.7 multiply_reduce_fusion.4
  444.0 2.7 fusion.190
  446.8 7.8 fusion.166
  455.9 3.2 fusion.147
  461.2 4.0 fusion.210
  469.1 6.3 convolution_bitcast_fusion
  475.5 11.4 fusion.193
  486.9 10.2 fusion.207
  497.4 9.9 fusion.202
  508.5 10.0 fusion.199
  520.3 5.9 reduce-scatter.13.cloned.1.call-done
  528.0 94.1 %reduce-scatter.11.cloned.1.call-done = f32[128,3072]{0,1:T(8,128)} async-done(((f32[1024,3072]{0,1:T(8,128)}), f32[128,3072]{0,1:T(8,128)}) %reduce-scatter.11.cloned.1.call-update) | async-done | bytes 1572880 | tf_op jit(solution)/shard_map/reduce_scatter | solution.py:308
  624.6 93.4 %reduce-scatter.9.cloned.1.call-done = f32[128,3072]{0,1:T(8,128)} async-done(((f32[1024,3072]{0,1:T(8,128)}), f32[128,3072]{0,1:T(8,128)}) %reduce-scatter.9.cloned.1.call-update) | async-done | bytes 1572880 | tf_op jit(solution)/shard_map/reduce_scatter | solution.py:308
  720.3 117.2 %reduce-scatter.21.cloned.1.call-done = f32[512,1024]{1,0:T(8,128)} async-done(((f32[4096,1024]{1,0:T(8,128)}), f32[512,1024]{1,0:T(8,128)}) %reduce-scatter.21.cloned.1.call-update) | async-done | bytes 2097168 | tf_op jit(solution)/shard_map/reduce_scatter | solution.py:311
  837.5 2.7 convert_bitcast_fusion.1
  840.3 116.7 %reduce-scatter.17.cloned.1.call-done = f32[128,4096]{1,0:T(8,128)} async-done(((f32[1024,4096]{1,0:T(8,128)}), f32[128,4096]{1,0:T(8,128)}) %reduce-scatter.17.cloned.1.call-update) | async-done | bytes 2097168 | tf_op jit(solution)/shard_map/reduce_scatter | solution.py:310
  959.7 116.7 %reduce-scatter.19.cloned.1.call-done = f32[128,4096]{1,0:T(8,128)} async-done(((f32[1024,4096]{1,0:T(8,128)}), f32[128,4096]{1,0:T(8,128)}) %reduce-scatter.19.cloned.1.call-update) | async-done | bytes 2097168 | tf_op jit(solution)/shard_map/reduce_scatter | solution.py:310
  1079.1 116.7 %reduce-scatter.23.cloned.1.call-done = f32[512,1024]{1,0:T(8,128)} async-done(((f32[4096,1024]{1,0:T(8,128)}), f32[512,1024]{1,0:T(8,128)}) %reduce-scatter.23.cloned.1.call-update) | async-done | bytes 2097168 | tf_op jit(solution)/shard_map/reduce_scatter | solution.py:311
  1195.8 2.7 convert_bitcast_fusion
  1200.5 44.9 %pmax.7 = f32[2,16]{1,0:T(2,128)S(1)} all-reduce(f32[2,16]{1,0:T(2,128)S(1)} %pad_maximum_fusion.9), channel_id=1, replica_groups=mesh['rep'=4,'shard'=8] {'rep','shard'}, use_global_device_ids=true, to_apply=%region_94.95 | all-reduce | flops 32 | bytes 256 | tf_op jit(solution)/shard_map/pmax | solution.py:402
  1246.4 25.8 %all-reduce.18 = (bf16[1024]{0:T(1024)(128)(2,1)S(1)}, bf16[1024]{0:T(1024)(128)(2,1)S(1)}, bf16[1024]{0:T(1024)(128)(2,1)S(1)}, bf16[1024]{0:T(1024)(128)(2,1)S...) all-reduce(f32[1024]{0:T(1024)S(1)} %convert_reduce_fusion.9, ...), channel_id=37, replica_groups=mesh['rep'=4,'shard'=8] {'shard'}, use_global_device_ids=true, to_apply=%region_42.43.clone | all-reduce | flops 24576 | bytes 147456
  1273.8 24.1 %all-reduce.19 = (bf16[1,128]{1,0:T(2,128)(2,1)S(1)}, bf16[1,128]{1,0:T(2,128)(2,1)S(1)}, bf16[1,128]{1,0:T(2,128)(2,1)S(1)}, bf16[1,128]{1,0:T(2,128)(2,1)S(1)}...) all-reduce(bf16[1,128]{1,0:T(2,128)(2,1)S(1)} %fusion.184, ...), channel_id=1, replica_groups=mesh['rep'=4,'shard'=8] {'rep'}, use_global_device_ids=true, to_apply=%region_43.44 | all-reduce | flops 3072 | bytes 12288 | tf_op jit(solution)/shard_map/psum | solution.py:342
  1303.6 2.9 convert_multiply_fusion
  1306.5 5.6 fusion.117
  1312.1 113.9 %all-reduce.23.cloned.1.call-done = (bf16[1,128,3072]{1,2,0:T(8,128)(2,1)}, bf16[1,128,3072]{1,2,0:T(8,128)(2,1)}, bf16[1,128,1024]{2,1,0:T(8,128)(2,1)}, bf16[1...) async-done(((bf16[1,128,3072]{1,2,0:T(8,128)(2,1)}, ...) | async-done | bytes 6291472 | tf_op jit(solution)/shard_map/psum | solution.py:338
  1432.1 3.8 maximum_convert_fusion
  (322 shorter events, 75.6 us)
Async XLA Ops:
  7.2 2.9 copy-start.45
  7.2 3.8 copy-start.33
  7.2 163.0 %all-gather.35.cloned.1.call-start = ((), (), s32[]{:S(2)}) async-start(), calls=%async_computation.16 | async-start | bytes 7077888 | tf_op jit(solution)/shard_map/all_gather | solution.py:54
  10.0 169.4 %all-gather.37.cloned.1.call-start = ((), (), s32[]{:S(2)}) async-start(), calls=%async_computation.17 | async-start | bytes 2359296 | tf_op jit(solution)/shard_map/all_gather | solution.py:55
  10.9 171.4 %all-gather.39.cloned.1.call-start = ((), (), s32[]{:S(2)}) async-start(), calls=%async_computation.18 | async-start | bytes 9437184 | tf_op jit(solution)/shard_map/all_gather | solution.py:56
  12.5 6.0 copy-start.55
  12.5 6.0 copy-start.56
  12.5 6.0 copy-start.57
  12.5 6.1 copy-start.58
  12.5 6.1 copy-start.59
  12.5 6.1 copy-start.60
  12.6 6.1 copy-start.61
  12.6 6.1 copy-start.52
  12.6 140.4 %copy-start.51 = (bf16[2,512]{1,0:T(2,128)(2,1)S(1)}, bf16[2,512]{1,0:T(2,128)(2,1)}, u32[]{:S(2)}) copy-start(bf16[2,512]{1,0:T(2,128)(2,1)} %param.27) | copy-start | bytes 6148
  12.6 157.5 %copy-start.54 = (s32[1,256]{1,0:T(1,128)S(1)}, s32[1,256]{1,0:T(1,128)}, u32[]{:S(2)}) copy-start(s32[1,256]{1,0:T(1,128)} %param.19) | copy-start | bytes 3076
  12.6 157.7 %copy-start.29 = (bf16[256,1024]{1,0:T(8,128)(2,1)S(1)}, bf16[256,1024]{1,0:T(8,128)(2,1)}, u32[]{:S(2)}) copy-start(bf16[256,1024]{1,0:T(8,128)(2,1)} %param.17) | copy-start | bytes 1572868
  12.6 190.3 %all-gather.41.cloned.1.call-start = ((), (), s32[]{:S(2)}) async-start(), calls=%async_computation.19 | async-start | bytes 9437184 | tf_op jit(solution)/shard_map/all_gather | solution.py:57
  15.8 235.0 %all-gather.43.cloned.1.call-start = ((), (), s32[]{:S(2)}) async-start(), calls=%async_computation.20 | async-start | bytes 7077888 | tf_op jit(solution)/shard_map/all_gather | solution.py:54
  16.4 264.1 %all-gather.45.cloned.1.call-start = ((), (), s32[]{:S(2)}) async-start(), calls=%async_computation.21 | async-start | bytes 2359296 | tf_op jit(solution)/shard_map/all_gather | solution.py:55
  17.0 320.4 %all-gather.47.cloned.1.call-start = ((), (), s32[]{:S(2)}) async-start(), calls=%async_computation.22 | async-start | bytes 9437184 | tf_op jit(solution)/shard_map/all_gather | solution.py:56
  17.7 376.0 %all-gather.49.cloned.1.call-start = ((), (), s32[]{:S(2)}) async-start(), calls=%async_computation.23 | async-start | bytes 9437184 | tf_op jit(solution)/shard_map/all_gather | solution.py:57
  18.5 500.1 %reduce-scatter.15.cloned.1.call-start = ((), (), s32[]{:S(2)}) async-start(), calls=%async_computation.11 | async-start | bytes 4718592 | tf_op jit(solution)/shard_map/reduce_scatter | solution.py:309
  176.5 2.9 copy-start.47
  179.4 18.5 %copy-start.38 = (bf16[16,64,256]{2,1,0:T(8,128)(2,1)}, bf16[16,64,256]{2,1,0:T(8,128)(2,1)S(1)}, u32[]{:S(2)}) copy-start(bf16[16,64,256]{2,1,0:T(8,128)(2,1)S(1)} %fusion.158) | copy-start | bytes 1572868
  256.8 5.2 copy-start.22
  258.2 3.7 copy-start.24
  260.5 2.9 copy-start.32
  393.7 8.8 slice-start.6
  393.7 6.9 copy-start.34
  393.7 8.8 slice-start.7
  401.2 5.7 slice-start.4
  402.4 4.4 copy-start.26
  402.5 4.4 slice-start.5
  406.9 2.8 copy-start.40
  406.9 4.1 copy-start.42
  419.3 107.0 %reduce-scatter.13.cloned.1.call-start = ((), (), s32[]{:S(2)}) async-start(), calls=%async_computation.10 | async-start | bytes 4718592 | tf_op jit(solution)/shard_map/reduce_scatter | solution.py:309
  419.3 3.9 copy-start.3
  425.6 7.7 copy-start.37
  425.6 8.1 slice-start.2
  426.4 6.9 copy-start.10
  426.4 7.3 slice-start.3
  426.4 13.5 slice-start
  433.7 6.3 copy-start.28
  433.7 6.2 slice-start.1
  439.9 2.8 copy-start.41
  440.0 4.1 copy-start.39
  446.8 175.4 %reduce-scatter.11.cloned.1.call-start = ((), (), s32[]{:S(2)}) async-start(), calls=%async_computation.9 | async-start | bytes 14155776 | tf_op jit(solution)/shard_map/reduce_scatter | solution.py:308
  454.7 263.3 %reduce-scatter.9.cloned.1.call-start = ((), (), s32[]{:S(2)}) async-start(), calls=%async_computation.8 | async-start | bytes 14155776 | tf_op jit(solution)/shard_map/reduce_scatter | solution.py:308
  461.2 4.0 copy-start.1
  475.4 362.1 %reduce-scatter.21.cloned.1.call-start = ((), (), s32[]{:S(2)}) async-start(), calls=%async_computation.14 | async-start | bytes 18874368 | tf_op jit(solution)/shard_map/reduce_scatter | solution.py:311
  486.9 470.1 %reduce-scatter.17.cloned.1.call-start = ((), (), s32[]{:S(2)}) async-start(), calls=%async_computation.12 | async-start | bytes 18874368 | tf_op jit(solution)/shard_map/reduce_scatter | solution.py:310
  497.2 579.2 %reduce-scatter.19.cloned.1.call-start = ((), (), s32[]{:S(2)}) async-start(), calls=%async_computation.13 | async-start | bytes 18874368 | tf_op jit(solution)/shard_map/reduce_scatter | solution.py:310
  507.3 688.5 %reduce-scatter.23.cloned.1.call-start = ((), (), s32[]{:S(2)}) async-start(), calls=%async_computation.15 | async-start | bytes 18874368 | tf_op jit(solution)/shard_map/reduce_scatter | solution.py:311
  518.5 907.5 %all-reduce.23.cloned.1.call-start = ((), (), s32[]{:S(2)}) async-start(), calls=%async_computation.24 | async-start | bytes 12582912 | tf_op jit(solution)/shard_map/psum | solution.py:338
  1079.1 119.5 %copy-start.63 = (u32[32]{0:T(128)S(1)}, u32[32]{0:T(128)}, u32[]{:S(2)}) copy-start(u32[32]{0:T(128)} %constant.106) | copy-start | bytes 388
  1079.1 166.4 %copy-start.11 = (bf16[16,64,256]{2,1,0:T(8,128)(2,1)S(1)}, bf16[16,64,256]{2,1,0:T(8,128)(2,1)}, u32[]{:S(2)}) copy-start(bf16[16,64,256]{2,1,0:T(8,128)(2,1)} %copy-done.10) | copy-start | bytes 1572868
  1198.5 47.1 %copy-start.17 = (bf16[16,64,256]{2,1,0:T(8,128)(2,1)S(1)}, bf16[16,64,256]{2,1,0:T(8,128)(2,1)}, u32[]{:S(2)}) copy-start(bf16[16,64,256]{2,1,0:T(8,128)(2,1)} %copy-done.16) | copy-start | bytes 1572868
  1198.5 47.4 %copy-start.9 = (bf16[16,64,256]{2,1,0:T(8,128)(2,1)S(1)}, bf16[16,64,256]{2,1,0:T(8,128)(2,1)}, u32[]{:S(2)}) copy-start(bf16[16,64,256]{2,1,0:T(8,128)(2,1)} %copy-done.8) | copy-start | bytes 1572868
  1198.5 47.6 %copy-start.15 = (bf16[16,64,256]{2,1,0:T(8,128)(2,1)S(1)}, bf16[16,64,256]{2,1,0:T(8,128)(2,1)}, u32[]{:S(2)}) copy-start(bf16[16,64,256]{2,1,0:T(8,128)(2,1)} %copy-done.14) | copy-start | bytes 1572868
  1198.5 73.9 %copy-start.62 = (f32[2,16]{1,0:T(2,128)S(1)}, f32[2,16]{1,0:T(2,128)}, u32[]{:S(2)}) copy-start(f32[2,16]{1,0:T(2,128)} %param.33) | copy-start | bytes 388
  1198.5 104.5 %copy-start.53 = (bf16[2,128]{1,0:T(2,128)(2,1)S(1)}, bf16[2,128]{1,0:T(2,128)(2,1)}, u32[]{:S(2)}) copy-start(bf16[2,128]{1,0:T(2,128)(2,1)} %param.24) | copy-start | bytes 1540
  1245.7 60.8 %copy-start.36 = (bf16[16,64,256]{2,1,0:T(8,128)(2,1)S(1)}, bf16[16,64,256]{2,1,0:T(8,128)(2,1)}, u32[]{:S(2)}) copy-start(bf16[16,64,256]{2,1,0:T(8,128)(2,1)} %copy-done.35) | copy-start | bytes 1572868
  1429.9 6.0 copy-start.43
  1429.9 6.0 copy-start.44
  (26 other events, 38.4 us)
Sparse Core Ops, SparseCore 0:
  10.5 48.2 all-gather.34
  61.3 27.9 all-gather.36
  91.7 54.4 all-gather.38
  148.4 54.4 all-gather.40
  205.3 45.5 all-gather.42
  252.6 27.8 all-gather.44
  283.0 54.3 all-gather.46
  339.3 54.3 all-gather.48
  419.4 51.3 reduce-scatter.14
  474.9 51.3 reduce-scatter.12
  529.8 92.3 reduce-scatter.10
  625.5 92.3 reduce-scatter.8
  721.5 115.9 reduce-scatter.20
  841.0 115.9 reduce-scatter.16
  960.4 115.9 reduce-scatter.18
  1079.8 115.9 reduce-scatter.22
  1199.2 226.7 all-reduce.22
where the time goes:
time: 1450 us; the launch traced here: 1440 us
  waiting for transfers between devices  934 us (64%)
  blocking collectives  246 us (17%)
  matrix products  171 us (12%)
  other arithmetic  45.8 us (3%)
  local copies, waits for them, and re-layouts  30.3 us (2%)
  between operations  16.9 us (1%)
    reduce_scatter x2, waiting for transfers between devices, reduce_group(): lax.psum_scatter(term_down, 'shard', scatter_dimension=0, tiled=True)  234 us
    reduce_scatter x2, waiting for transfers between devices, reduce_group(): lax.psum_scatter(term_up, 'shard', scatter_dimension=0, tiled=True)  233 us
    reduce_scatter x2, waiting for transfers between devices, reduce_group(): lax.psum_scatter(term_qkv, 'shard', scatter_dimension=0, tiled=True)  188 us
    psum x1, waiting for transfers between devices, reduce_group(): lax.psum(term_qkv.astype(jnp.bfloat16), 'rep').astype(jnp.float32)  114 us
    all_gather x2, waiting for transfers between devices, fetch_forward(): lax.all_gather(w_up, 'shard', axis=0, tiled=True)  54 us
    all_gather x2, waiting for transfers between devices, fetch_forward(): lax.all_gather(w_down, 'shard', axis=0, tiled=True)  45.7 us
    pmax x1, blocking collectives, shards(): peak = lax.pmax(jnp.stack(tops), ('rep', 'shard'))  44.9 us
    all_gather x2, waiting for transfers between devices, fetch_forward(): lax.all_gather(w_qkv, 'shard', axis=0, tiled=True)  41.1 us
  transfers between devices with their start and end apart: 17, of which 13 were waited for; matrix products, arithmetic and copies ran while one was open for 14% of the time, Pallas kernels for 0%

commit v1 on v0

v1 whole, which is shorter than its diff:
```python
import math

import jax
import jax.numpy as jnp
from jax import lax
from jax.sharding import PartitionSpec as P

HEADS = 16


epsilon = 1e-05
neg_large = -1e30
low = jnp.bfloat16
wide = jnp.float32


def normalize(values):
    centred = values - jnp.mean(values, axis=-1, keepdims=True)
    rstd = lax.rsqrt(jnp.mean(centred * centred, axis=-1, keepdims=True) + epsilon)
    return (centred * rstd, rstd)


def norm_back(grad_norm, normed, rstd):
    inner = jnp.mean(grad_norm * normed, axis=-1, keepdims=True)
    return rstd * (grad_norm - jnp.mean(grad_norm, axis=-1, keepdims=True) - normed * inner)


def gelu_slope(pre):
    cdf = 0.5 * (1.0 + lax.erf(pre * (1.0 / math.sqrt(2.0))))
    return cdf + pre * jnp.exp(-0.5 * pre * pre) * (1.0 / math.sqrt(2.0 * math.pi))


def column_sums(values):
    return jnp.sum(values.astype(wide), axis=0)


class Net:
    def __init__(self, shards, reps, step):
        self.shards = shards
        self.reps = reps
        self.step = step
        self.pairs = shards // 2
        self.high = shards // (2 * step)
        self.bits = self.pairs.bit_length() - 1
        self.me = lax.axis_index("shard")
        self.core = (self.me // step) % 2
        self.rep = lax.axis_index("rep")

    def over_core(self, value):
        return lax.ppermute(value, "shard", [(i, i ^ self.step) for i in range(self.shards)])

    def stride(self, bit):
        return (1 << bit) if (1 << bit) < self.step else (2 << bit)

    def over_bit(self, value, bit):
        step = self.stride(bit)
        return lax.ppermute(value, "shard", [(i, i ^ step) for i in range(self.shards)])

    def chip_bit(self, bit):
        return (self.me // self.stride(bit)) % 2

    def rows_in_order(self, value):
        rest = value.shape[2:]
        value = value.reshape((self.high, self.step, 2) + rest)
        return jnp.swapaxes(value, 1, 2).reshape((self.shards,) + rest)

    def rows_by_pair(self, value):
        rest = value.shape[1:]
        value = value.reshape((self.high, 2, self.step) + rest)
        return jnp.swapaxes(value, 1, 2).reshape((self.pairs, 2) + rest)

    def in_order(self, mine, other, place):
        first = place == 0
        return jnp.stack([jnp.where(first, mine, other), jnp.where(first, other, mine)])

    def gather_chips(self, piece, order):
        shape = piece.shape
        for bit in order:
            piece = self.in_order(piece, self.over_bit(piece, bit), self.chip_bit(bit))
        axes = list(reversed(order))
        natural = [axes.index(bit) for bit in reversed(range(self.bits))]
        rest = list(range(self.bits, self.bits + len(shape)))
        return piece.transpose(natural + rest).reshape((self.pairs,) + shape)

    def scatter_chips(self, value, order):
        rest = value.shape[1:]
        value = value.reshape((2,) * self.bits + rest)
        left = list(reversed(range(self.bits)))
        for bit in order:
            axis = left.index(bit)
            place = self.chip_bit(bit)
            theirs = lax.dynamic_index_in_dim(value, 1 - place, axis, keepdims=False)
            ours = lax.dynamic_index_in_dim(value, place, axis, keepdims=False)
            got = self.over_bit(theirs, bit)
            value = (ours.astype(wide) + got.astype(wide)).astype(value.dtype)
            left.remove(bit)
        return value

    def sum_reps(self, value):
        reps, half = self.reps, self.reps // 2

        def add(one, other):
            return (one.astype(wide) + other.astype(wide)).astype(value.dtype)

        total = value
        for i in range(half - 1):
            got = lax.ppermute(total, "rep", [(i, i + 1), (reps - 1 - i, reps - 2 - i)])
            total = add(total, got)
        total = add(total, lax.ppermute(total, "rep", [(half - 1, half), (half, half - 1)]))
        for i in reversed(range(half - 1)):
            got = lax.ppermute(total, "rep", [(i + 1, i), (reps - 2 - i, reps - 1 - i)])
            outer = jnp.logical_or(self.rep == i, self.rep == reps - 1 - i)
            total = jnp.where(outer, got, total)
        return total

    def pair(self, value):
        return jnp.concatenate([value, self.over_core(value)], axis=0)

    def join(self, partial):
        rows = partial.shape[0] // 2
        return partial[:rows] + self.over_core(partial[rows:].astype(low)).astype(wide)


def halves(columns):
    return ((0, columns // 2), (columns // 2, columns))


def gather_weight(net, piece):
    orders = (list(range(net.bits)), list(reversed(range(net.bits))))
    parts = [
        net.gather_chips(piece[:, start:stop], order)
        for order, (start, stop) in zip(orders, halves(piece.shape[1]))
    ]
    return jnp.concatenate(parts, axis=2)


def scatter_weight(net, value):
    orders = (list(range(net.bits)), list(reversed(range(net.bits))))
    parts = [
        net.sum_reps(net.scatter_chips(value[:, :, start:stop], order))
        for order, (start, stop) in zip(orders, halves(value.shape[2]))
    ]
    return jnp.concatenate(parts, axis=1)


def by_core(weight, net, groups):
    rows, columns = weight.shape
    split = weight.reshape(rows, groups * net.high, 2, columns // (2 * groups * net.high))
    mine = lax.dynamic_index_in_dim(split, net.core, 2, keepdims=False)
    other = lax.dynamic_index_in_dim(split, 1 - net.core, 2, keepdims=False)
    return mine.reshape(rows, columns // 2), other.reshape(rows, columns // 2)


def swap_columns(weight, net, groups):
    mine, other = by_core(weight, net, groups)
    return net.in_order(mine, net.over_core(other), net.core).reshape(-1, mine.shape[1])


def swap_back(value, net, groups):
    rows = value.shape[0] // 2
    split = value.reshape(2, rows, value.shape[1])
    mine = lax.dynamic_index_in_dim(split, net.core, 0, keepdims=False)
    other = lax.dynamic_index_in_dim(split, 1 - net.core, 0, keepdims=False)
    got = net.over_core(other)
    block = value.shape[1] // (groups * net.high)
    both = [part.reshape(rows, groups * net.high, block) for part in (mine, got)]
    first = net.core == 0
    stacked = jnp.stack(
        [jnp.where(first, both[0], both[1]), jnp.where(first, both[1], both[0])], axis=2
    )
    return stacked.reshape(rows, 2 * value.shape[1])


def split_heads(rows, heads):
    return rows.reshape(2, rows.shape[0] // 2, heads, rows.shape[1] // heads)


def masked_scores(query, key_rows, same):
    scale = 1.0 / math.sqrt(query.shape[-1])
    scores = jnp.einsum("sqhd,skhd->shqk", query, key_rows, preferred_element_type=wide) * scale
    return jnp.where(same[:, None], scores, neg_large)


def forward_layer(net, hidden, weights, small, same):
    w_qkv, w_out, w_up, w_down = weights
    bias_qkv, bias_out, bias_up, bias_down, gain_first, shift_first, gain_second, shift_second = small
    heads = HEADS // 2
    third = w_qkv.shape[1] // 3
    both_hidden = net.pair(hidden.astype(low))
    qkv = (jnp.dot(both_hidden, w_qkv, preferred_element_type=wide) + bias_qkv).astype(low)
    query = split_heads(qkv[:, :third], heads)
    key_rows = split_heads(qkv[:, third : 2 * third], heads)
    value_rows = split_heads(qkv[:, 2 * third :], heads)
    masked = masked_scores(query, key_rows, same)
    top = jnp.max(masked, axis=3, keepdims=True)
    expo = jnp.exp(masked - top)
    total = jnp.sum(expo, axis=3, keepdims=True)
    probs = (expo / total).astype(low)
    log_total = top + jnp.log(total)
    head_top = jnp.max(top, axis=(0, 2, 3))
    attended = jnp.einsum("shqk,skhd->sqhd", probs, value_rows, preferred_element_type=wide)
    attended = attended.reshape(qkv.shape[0], third).astype(low)
    summed_one = (
        hidden + net.join(jnp.dot(attended, w_out, preferred_element_type=wide)) + bias_out
    )
    normed_one, rstd_one = normalize(summed_one)
    first = normed_one * gain_first + shift_first
    both_first = net.pair(first.astype(low))
    pre = jnp.dot(both_first, w_up, preferred_element_type=wide) + bias_up
    activation = jax.nn.gelu(pre, approximate=False).astype(low)
    summed_two = (
        first + net.join(jnp.dot(activation, w_down, preferred_element_type=wide)) + bias_down
    )
    normed_two, rstd_two = normalize(summed_two)
    result = normed_two * gain_second + shift_second
    saved = (
        both_hidden,
        qkv,
        log_total,
        attended,
        normed_one,
        rstd_one,
        both_first,
        pre,
        activation,
        normed_two,
        rstd_two,
    )
    return (result, head_top, saved)


def matmul_rows(left, right):
    return jnp.einsum("ti,to->io", left, right, preferred_element_type=wide).astype(low)


def matmul_back(left, right):
    return jnp.einsum("to,io->ti", left, right, preferred_element_type=wide)


def backward_layer(net, grad_out, weights, small, same, saved):
    w_qkv, w_out, w_up, w_down = weights
    bias_qkv, bias_out, bias_up, bias_down, gain_first, shift_first, gain_second, shift_second = small
    (
        both_hidden,
        qkv,
        log_total,
        attended,
        normed_one,
        rstd_one,
        both_first,
        pre,
        activation,
        normed_two,
        rstd_two,
    ) = saved
    heads = HEADS // 2
    third = w_qkv.shape[1] // 3
    scale = 1.0 / math.sqrt(third // heads)
    grad_gain_second = jnp.sum(grad_out * normed_two, axis=0)
    grad_shift_second = jnp.sum(grad_out, axis=0)
    grad_sum_two = norm_back(grad_out * gain_second, normed_two, rstd_two)
    branch_two = grad_sum_two.astype(low)
    grad_bias_down = column_sums(branch_two)
    both_two = net.pair(branch_two)
    grad_w_down = matmul_rows(activation, both_two)
    branch_pre = (matmul_back(both_two, w_down) * gelu_slope(pre)).astype(low)
    grad_bias_up = column_sums(branch_pre)
    grad_w_up = matmul_rows(both_first, branch_pre)
    grad_first = grad_sum_two + net.join(matmul_back(branch_pre, w_up))
    grad_gain_first = jnp.sum(grad_first * normed_one, axis=0)
    grad_shift_first = jnp.sum(grad_first, axis=0)
    grad_sum_one = norm_back(grad_first * gain_first, normed_one, rstd_one)
    branch_one = grad_sum_one.astype(low)
    grad_bias_out = column_sums(branch_one)
    both_one = net.pair(branch_one)
    grad_w_out = matmul_rows(attended, both_one)
    grad_attended = split_heads(matmul_back(both_one, w_out).astype(low), heads)
    query = split_heads(qkv[:, :third], heads)
    key_rows = split_heads(qkv[:, third : 2 * third], heads)
    value_rows = split_heads(qkv[:, 2 * third :], heads)
    masked = masked_scores(query, key_rows, same)
    probs = jnp.exp(masked - log_total)
    grad_value = jnp.einsum(
        "shqk,sqhd->skhd", probs.astype(low), grad_attended, preferred_element_type=wide
    )
    grad_probs = jnp.einsum("sqhd,skhd->shqk", grad_attended, value_rows, preferred_element_type=wide)
    row_inner = jnp.sum(probs * grad_probs, axis=3, keepdims=True)
    grad_scores = (probs * (grad_probs - row_inner)).astype(low)
    grad_query = (
        jnp.einsum("shqk,skhd->sqhd", grad_scores, key_rows, preferred_element_type=wide) * scale
    )
    grad_key = (
        jnp.einsum("shqk,sqhd->skhd", grad_scores, query, preferred_element_type=wide) * scale
    )
    grad_qkv = jnp.concatenate(
        [part.astype(low).reshape(qkv.shape[0], third) for part in (grad_query, grad_key, grad_value)],
        axis=1,
    )
    grad_bias_query = column_sums(grad_qkv[:, :third])
    grad_bias_value = column_sums(grad_qkv[:, 2 * third :])
    grad_w_qkv = matmul_rows(both_hidden, grad_qkv)
    grad_hidden = grad_sum_one + net.join(matmul_back(grad_qkv, w_qkv))
    large = []
    for value, paired in ((grad_w_qkv, True), (grad_w_out, False), (grad_w_up, True), (grad_w_down, False)):
        columns = value.shape[1]
        if paired:
            value = net.rows_by_pair(value.reshape(net.shards, -1, columns))
        large.append(scatter_weight(net, value.reshape(net.pairs, -1, columns)))
    owned = (
        swap_back(large[0], net, 3),
        large[1],
        swap_back(large[2], net, 1),
        large[3],
    )
    terms = (
        grad_bias_query,
        grad_bias_value,
        grad_bias_out,
        grad_bias_up,
        grad_bias_down,
        grad_gain_first,
        grad_shift_first,
        grad_gain_second,
        grad_shift_second,
    )
    return (grad_hidden, owned, terms)


def shards(
    inputs,
    cotangent,
    segments,
    w_qkv,
    w_out,
    w_up,
    w_down,
    bias_query,
    bias_value,
    bias_out,
    bias_up,
    bias_down,
    norm1_gain,
    norm1_bias,
    norm2_gain,
    norm2_bias,
    tau,
    *,
    shard_count,
    rep_count,
):
    layer_count = w_qkv.shape[0]
    width = w_qkv.shape[2] // 3
    rows_here = bias_query.shape[1]
    head_dim = width // HEADS
    net = Net(shard_count, rep_count, max(1, head_dim // rows_here))

    vectors = (
        bias_query,
        bias_value,
        bias_out,
        bias_up,
        bias_down,
        norm1_gain,
        norm1_bias,
        norm2_gain,
        norm2_bias,
    )
    lengths = [vector.shape[1] // rows_here for vector in vectors]
    packed = jnp.concatenate(
        [vector.reshape(layer_count, -1, rows_here) for vector in vectors], axis=1
    )
    packed = net.in_order(packed, net.over_core(packed), net.core)
    packed = net.rows_in_order(net.gather_chips(packed, list(range(net.bits))))

    def whole(layer_index, member):
        start = sum(lengths[:member])
        return packed[:, layer_index, start : start + lengths[member]].astype(wide)

    def of_core(layer_index, member):
        split = whole(layer_index, member).reshape(net.high, 2, -1)
        return lax.dynamic_index_in_dim(split, net.core, 1, keepdims=False).reshape(-1)

    def small_of(layer_index):
        bias_q = of_core(layer_index, 0)
        bias_qkv = jnp.concatenate([bias_q, jnp.zeros_like(bias_q), of_core(layer_index, 1)])
        return (
            bias_qkv,
            whole(layer_index, 2).reshape(-1),
            of_core(layer_index, 3),
        ) + tuple(whole(layer_index, member).reshape(-1) for member in (4, 5, 6, 7, 8))

    both_segments = jnp.concatenate([segments, net.over_core(segments)], axis=0)
    same = both_segments[:, :, None] == both_segments[:, None, :]

    hidden = inputs.astype(wide)
    saved_all, weights_all, small_all, tops = [], [], [], []
    for layer_index in range(layer_count):
        pieces = (
            swap_columns(w_qkv[layer_index], net, 3),
            w_out[layer_index],
            swap_columns(w_up[layer_index], net, 1),
            w_down[layer_index],
        )
        weights = []
        for piece, paired in zip(pieces, (True, False, True, False)):
            full = gather_weight(net, piece)
            if paired:
                full = net.rows_in_order(full.reshape(net.pairs, 2, -1, full.shape[2]))
            weights.append(full.reshape(-1, full.shape[2]))
        small = small_of(layer_index)
        hidden, head_top, saved = forward_layer(net, hidden, weights, small, same)
        saved_all.append(saved)
        weights_all.append(weights)
        small_all.append(small)
        tops.append(head_top)
    output = hidden.astype(low)

    local = jnp.stack(tops)
    local = net.in_order(local, net.over_core(local), net.core)
    local = local.reshape(2, layer_count, net.high, -1).transpose(1, 2, 0, 3).reshape(layer_count, HEADS)
    for bit in range(net.bits):
        local = jnp.maximum(local, net.over_bit(local, bit))
    step = 1
    while step < net.reps:
        local = jnp.maximum(
            local, lax.ppermute(local, "rep", [(i, i ^ step) for i in range(net.reps)])
        )
        step *= 2
    peak = local

    grad_flow = cotangent.astype(wide)
    owned_all = [None] * layer_count
    terms_all = [None] * layer_count
    for layer_index in reversed(range(layer_count)):
        grad_flow, owned, terms = backward_layer(
            net,
            grad_flow,
            weights_all[layer_index],
            small_all[layer_index],
            same,
            saved_all[layer_index],
        )
        owned_all[layer_index] = owned
        terms_all[layer_index] = terms
    large = tuple(
        jnp.stack([owned_all[layer_index][member].astype(wide) for layer_index in range(layer_count)])
        for member in range(4)
    )

    def placed(value, member):
        if member in (0, 1, 3):
            value = value.reshape(net.high, 1, net.step, lengths[member], rows_here)
            zero = jnp.zeros_like(value)
            first = net.core == 0
            return jnp.concatenate(
                [jnp.where(first, value, zero), jnp.where(first, zero, value)], axis=1
            )
        return value.reshape(net.high, 2, net.step, lengths[member], rows_here)

    terms = jnp.stack(
        [
            jnp.concatenate(
                [placed(value, member) for member, value in enumerate(terms_all[layer_index])], axis=3
            )
            for layer_index in range(layer_count)
        ],
        axis=3,
    )
    theirs = lax.dynamic_index_in_dim(terms, 1 - net.core, 1, keepdims=False)
    ours = lax.dynamic_index_in_dim(terms, net.core, 1, keepdims=False)
    terms = ours + net.over_core(theirs)
    terms = terms.reshape((net.pairs,) + terms.shape[2:])
    terms = net.sum_reps(net.scatter_chips(terms, list(range(net.bits))))
    vector_grads = []
    start = 0
    for length in lengths:
        vector_grads.append(terms[:, start : start + length].reshape(layer_count, -1))
        start += length

    factor = jnp.sqrt(tau / jnp.maximum(peak, tau))
    column_scale = jnp.repeat(factor, head_dim, axis=1)
    both_scale = jnp.concatenate([column_scale, column_scale], axis=1)
    clipped_qk = w_qkv[:, :, : 2 * width].astype(wide) * both_scale[:, None, :]
    start = lax.axis_index("shard") * rows_here
    scale_here = lax.dynamic_slice_in_dim(column_scale, start, rows_here, 1)
    clipped_bias_query = bias_query.astype(wide) * scale_here
    return (output, grad_flow) + large + tuple(vector_grads) + (clipped_qk, clipped_bias_query)


def solution(mesh):
    tokens = P(("rep", "shard"), None)
    matrix = P(None, "shard", None)
    vector = P(None, "shard")
    in_specs = (tokens, tokens, tokens) + (matrix,) * 4 + (vector,) * 9 + (P(),)
    out_specs = (tokens, tokens) + (matrix,) * 4 + (vector,) * 9 + (matrix, vector)

    def local(*arrays):
        return shards(*arrays, shard_count=mesh.shape["shard"], rep_count=mesh.shape["rep"])

    return jax.shard_map(local, mesh=mesh, in_specs=in_specs, out_specs=out_specs, check_vma=False)
```

time: 1450 us -> 874 us (0.60)
  waiting for transfers between devices: 934 us -> 264 us
  blocking collectives: 246 us -> 0 us
  starting transfers between devices: 1.27 us -> 194 us
  local copies, waits for them, and re-layouts: 30.3 us -> 158 us
  other arithmetic: 45.8 us -> 142 us
  matrix products: 171 us -> 100 us
    reduce_scatter x8 -> x0, waiting for transfers between devices: 661 us -> none  [the longest x2 234 us: reduce_group(): lax.psum_scatter(term_down, 'shard', scatter_dimension=0, tiled=True)]
    ppermute x0 -> x151, waiting for transfers between devices: none -> 264 us  [the longest x70 164 us: over_bit(): lax.ppermute(value, 'shard', [(i, i ^ step) for i in range(self.shards)])]
    ppermute x0 -> x151, starting transfers between devices: none -> 194 us  [the longest x17 79.4 us: sum_reps(): got = lax.ppermute(total, 'rep', [(i, i + 1), (reps - 1 - i, reps - 2 - i)])]
    all_gather x8 -> x0, waiting for transfers between devices: 156 us -> none  [the longest x2 54 us: fetch_forward(): lax.all_gather(w_up, 'shard', axis=0, tiled=True)]
    all_gather x18 -> x0, blocking collectives: 151 us -> none  [the longest x2 18 us: fetch_forward(): lax.all_gather(bias_query, 'shard', axis=0, tiled=True)]
    psum x1 -> x0, waiting for transfers between devices: 114 us -> none  [reduce_group(): lax.psum(term_qkv.astype(jnp.bfloat16), 'rep').astype(jnp.float32)]
    dot_general x36, matrix products: 171 us -> 100 us  [the longest x2 26.5 us: forward_layer(): pre = jnp.dot(both_first, w_up, preferred_element_type=wide) + bias_up]
    pmax x1 -> x0, blocking collectives: 44.9 us -> none  [shards(): peak = lax.pmax(jnp.stack(tops), ('rep', 'shard'))]
  transfers between devices with their start and end apart: 17 -> 151, of which waited for: 13 -> 53; matrix products, arithmetic and copies ran while one was open for 14% -> 41% of each run, Pallas kernels for 0% -> 0%
where the time goes in v1:
time: 874 us; the launch traced here: 864 us
  waiting for transfers between devices  264 us (30%)
  starting transfers between devices  194 us (22%)
  local copies, waits for them, and re-layouts  158 us (18%)
  other arithmetic  142 us (16%)
  matrix products  100 us (11%)
    ppermute x70, waiting for transfers between devices, over_bit(): lax.ppermute(value, 'shard', [(i, i ^ step) for i in range(self.shards)])  164 us
    ppermute x17, waiting for transfers between devices, sum_reps(): got = lax.ppermute(total, 'rep', [(i + 1, i), (reps - 2 - i, reps - 1 - i)])  80.3 us
    ppermute x17, starting transfers between devices, sum_reps(): got = lax.ppermute(total, 'rep', [(i, i + 1), (reps - 1 - i, reps - 2 - i)])  79.4 us
    ppermute x70, starting transfers between devices, over_bit(): lax.ppermute(value, 'shard', [(i, i ^ step) for i in range(self.shards)])  70.8 us
    another operation x58, other arithmetic, in_order(): jnp.stack([jnp.where(first, mine, other), jnp.where(first, other, mine)])  40.3 us
    unnamed x449, local copies, waits for them, and re-layouts  34.8 us
    reshape x16, local copies, waits for them, and re-layouts, split_heads(): return rows.reshape(2, rows.shape[0] // 2, heads, rows.shape[1] // heads)  30.7 us
    convert_element_type x32, other arithmetic, scatter_chips(): value = (ours.astype(wide) + got.astype(wide)).astype(value.dtype)  29.4 us
  transfers between devices with their start and end apart: 151, of which 53 were waited for; matrix products, arithmetic and copies ran while one was open for 41% of the time, Pallas kernels for 0%

profile of v1, /device:TPU:0, one launch (start us, length us, event | category | flops | bytes accessed | tf_op | source)
XLA Modules:
  0.0 863.7 jit_solution(16870860288308015282)
XLA Ops:
  9.3 2.8 collective-permute-start.32
  27.6 3.7 collective-permute-done.7
  32.6 2.6 collective-permute-done.8
  44.3 5.5 collective-permute-done.13
  53.5 2.7 collective-permute-done.33
  64.1 2.6 copy.228
  83.3 2.7 collective-permute-done.21
  108.3 5.7 collective-permute-done.17
  117.6 7.7 collective-permute-done.39
  130.8 16.9 %collective-permute-done.24 = bf16[2,512,512]{2,1,0:T(8,128)(2,1)S(1)} collective-permute-done((bf16[2,512,512]{2,1,0:T(8,128)(2,1)S(1)}, bf16[2,512,512]{2,1,0:T(8,128)(2,1)S(1)}, u32[]{:S(2)}, u32[]{:S(2)}) %collective-permute-start.24) | collective-permute-done | bytes 1048608 | tf_op jit(solution)/shard_map/ppermute | solution.py:57
  149.9 36.8 %collective-permute-done.5 = bf16[2,256,768]{2,1,0:T(8,128)(2,1)S(1)} collective-permute-done((bf16[2,256,768]{2,1,0:T(8,128)(2,1)S(1)}, bf16[2,256,768]{2,1,0:T(8,128)(2,1)S(1)}, u32[]{:S(2)}, u32[]{:S(2)}) %collective-permute-start.5) | collective-permute-done | bytes 786464 | tf_op jit(solution)/shard_map/ppermute | solution.py:57
  206.8 3.2 fusion.85
  213.9 3.2 select_bitcast_fusion.3
  220.0 16.8 %collective-permute-done.20 = bf16[2,256,1024]{2,1,0:T(8,128)(2,1)S(1)} collective-permute-done((bf16[2,256,1024]{2,1,0:T(8,128)(2,1)S(1)}, bf16[2,256,1024]{2,1,0:T(8,128)(2,1)S(1)}, u32[]{:S(2)}, u32[]{:S(2)}) %collective-permute-start.20) | collective-permute-done | bytes 1048608 | tf_op jit(solution)/shard_map/ppermute | solution.py:57
  237.4 6.7 collective-permute-done.18
  246.0 13.3 %fusion.2 = (bf16[512,2048]{1,0:T(8,128)(2,1)S(1)}, f32[512,2048]{1,0:T(8,128)}) fusion(f32[2048]{0:T(1024)S(1)} %bitcast.840, bf16[1024,1024]{1,0:T(8,128)(2,1)S(1)} %bitcast.726, bf16[1024,1024]{1,0:T(8,128)(2,1)S(1)} %bitcast.728, bf16[256,1024]{1,0:T(8,128)(2,1)S(1)} %collective-permute-done.15, bf16[256,1024]{1,0:T(8,128)(2,1)S(1)} %fusion.117), kind=kOutput, calls=%fused_computation.6 | convolution fusion | flops 2227175424 | bytes 11542528 | tf_op jit(solution)/shard_map/dot_general | solution.py:209
  261.9 2.7 select_bitcast_fusion.1
  275.5 2.5 copy.258
  282.9 2.5 reshape.1380
  285.4 2.5 copy.259
  304.1 13.2 %fusion.5 = (bf16[512,2048]{1,0:T(8,128)(2,1)S(1)}, f32[512,2048]{1,0:T(8,128)}) fusion(f32[2048]{0:T(1024)S(1)} %bitcast.842, bf16[1024,1024]{1,0:T(8,128)(2,1)S(1)} %bitcast.734, bf16[1024,1024]{1,0:T(8,128)(2,1)S(1)} %bitcast.736, bf16[256,1024]{1,0:T(8,128)(2,1)S(1)} %collective-permute-done.37, bf16[256,1024]{1,0:T(8,128)(2,1)S(1)} %fusion.119), kind=kOutput, calls=%fused_computation.9 | convolution fusion | flops 2227175424 | bytes 11542528 | tf_op jit(solution)/shard_map/dot_general | solution.py:209
  326.6 6.8 convert_reduce_fusion
  336.3 3.6 convolution_convert_fusion
  360.6 2.5 reshape.1383
  368.8 2.5 fusion.49
  371.3 3.9 convert_reduce_fusion.5
  386.4 3.8 collective-permute-done.109
  413.1 9.1 %collective-permute-done.89 = bf16[128,512]{1,0:T(8,128)(2,1)S(1)} collective-permute-done((bf16[128,512]{1,0:T(8,128)(2,1)S(1)}, bf16[128,512]{1,0:T(8,128)(2,1)S(1)}, u32[]{:S(2)}, u32[]{:S(2)}) %collective-permute-start.89) | collective-permute-done | bytes 131104 | tf_op jit(solution)/shard_map/ppermute | solution.py:57
  423.2 4.1 collective-permute-done.94
  431.6 3.5 collective-permute-start.90
  437.5 4.3 collective-permute-start.95
  449.7 8.9 %collective-permute-start.132 = (bf16[512,512]{1,0:T(8,128)(2,1)S(1)}, bf16[512,512]{1,0:T(8,128)(2,1)S(1)}, u32[]{:S(2)}, u32[]{:S(2)}) collective-permute-start(bf16[512,512]{1,0:T(8,128)(2,1)S(1)} %fusion.110), channel_id=1, source_target_pairs={{0,8},{24,16},{1,9},{25,17},{2,10},{26,18},{3,11},{27,19},{4,12},{... | collective-permute-start | bytes 1572872 | tf_op jit(solution)/shard_map/ppermute | solution.py:107
  463.5 5.6 collective-permute-done.92
  471.1 4.9 collective-permute-done.97
  486.2 4.1 convert_reduce_fusion.1
  506.5 9.5 %collective-permute-start.69 = (bf16[256,768]{1,0:T(8,128)(2,1)S(1)}, bf16[256,768]{1,0:T(8,128)(2,1)S(1)}, u32[]{:S(2)}, u32[]{:S(2)}) collective-permute-start(bf16[256,768]{1,0:T(8,128)(2,1)S(1)} %fusion.121), channel_id=1, source_target_pairs={{0,8},{24,16},{1,9},{25,17},{2,10},{26,18},{3,11},{27,19},{4,12},{... | collective-permute-start | bytes 1179656 | tf_op jit(solution)/shard_map/ppermute | solution.py:107
  517.0 10.3 %collective-permute-start.74 = (bf16[256,768]{1,0:T(8,128)(2,1)S(1)}, bf16[256,768]{1,0:T(8,128)(2,1)S(1)}, u32[]{:S(2)}, u32[]{:S(2)}) collective-permute-start(bf16[256,768]{1,0:T(8,128)(2,1)S(1)} %fusion.120), channel_id=1, source_target_pairs={{0,8},{24,16},{1,9},{25,17},{2,10},{26,18},{3,11},{27,19},{4,12},{... | collective-permute-start | bytes 1179656 | tf_op jit(solution)/shard_map/ppermute | solution.py:107
  528.5 4.0 collective-permute-done.74
  542.8 5.9 collective-permute-done.98
  550.0 4.9 collective-permute-done.103
  560.8 3.2 convert_reduce_fusion.9
  586.2 3.2 collective-permute-done.113
  594.0 5.4 collective-permute-done.118
  599.4 2.6 collective-permute-start.121
  607.7 3.2 fusion.61
  638.2 2.8 collective-permute-start.143
  643.2 2.8 convert_multiply_fusion
  648.6 5.9 collective-permute-done.145
  661.9 9.4 %collective-permute-done.78 = bf16[2,128,512]{2,1,0:T(8,128)(2,1)S(1)} collective-permute-done((bf16[2,128,512]{2,1,0:T(8,128)(2,1)S(1)}, bf16[2,128,512]{2,1,0:T(8,128)(2,1)S(1)}, u32[]{:S(2)}, u32[]{:S(2)}) %collective-permute-start.78) | collective-permute-done | bytes 262176 | tf_op jit(solution)/shard_map/ppermute | solution.py:57
  673.5 4.2 collective-permute-done.83
  685.1 2.9 collective-permute-done.84
  702.1 4.3 collective-permute-start.85
  709.7 5.1 collective-permute-start.122
  731.0 7.7 collective-permute-start.100
  741.5 4.2 collective-permute-done.82
  747.1 5.5 collective-permute-done.87
  766.2 9.7 %collective-permute-start.58 = (bf16[256,768]{1,0:T(8,128)(2,1)S(1)}, bf16[256,768]{1,0:T(8,128)(2,1)S(1)}, u32[]{:S(2)}, u32[]{:S(2)}) collective-permute-start(bf16[256,768]{1,0:T(8,128)(2,1)S(1)} %fusion.123), channel_id=1, source_target_pairs={{0,8},{24,16},{1,9},{25,17},{2,10},{26,18},{3,11},{27,19},{4,12},{... | collective-permute-start | bytes 1179656 | tf_op jit(solution)/shard_map/ppermute | solution.py:107
  776.0 2.8 collective-permute-start.63
  785.0 2.8 collective-permute-done.63
  793.0 31.6 %collective-permute-done.102 = bf16[256,1024]{1,0:T(8,128)(2,1)S(1)} collective-permute-done((bf16[256,1024]{1,0:T(8,128)(2,1)S(1)}, bf16[256,1024]{1,0:T(8,128)(2,1)S(1)}, u32[]{:S(2)}, u32[]{:S(2)}) %collective-permute-start.102) | collective-permute-done | bytes 524320 | tf_op jit(solution)/shard_map/ppermute | solution.py:111
  826.0 9.9 %collective-permute-done.107 = bf16[256,1024]{1,0:T(8,128)(2,1)S(1)} collective-permute-done((bf16[256,1024]{1,0:T(8,128)(2,1)S(1)}, bf16[256,1024]{1,0:T(8,128)(2,1)S(1)}, u32[]{:S(2)}, u32[]{:S(2)}) %collective-permute-start.107) | collective-permute-done | bytes 524320 | tf_op jit(solution)/shard_map/ppermute | solution.py:111
  839.6 2.6 maximum_convert_fusion.1
  844.0 3.2 collective-permute-done.65
  853.5 5.6 copy.323
  (1118 shorter events, 458.7 us)
Async XLA Ops:
  0.7 24.7 %collective-permute-start.9 = (s32[1,256]{1,0:T(1,128)}, s32[1,256]{1,0:T(1,128)}, u32[]{:S(2)}, u32[]{:S(2)}) collective-permute-start(s32[1,256]{1,0:T(1,128)} %param.19), channel_id=1, source_target_pairs={{0,1},{1,0},{2,3},{3,2},{4,5},{5,4},{6,7},{7,6},{8,9},{9,8},{10,11... | collective-permute-start | bytes 3080 | tf_op jit(solution)/shard_map/ppermute | solution.py:50
  9.3 31.9 %collective-permute-start.32 = (bf16[128,512]{1,0:T(8,128)(2,1)}, bf16[128,512]{1,0:T(8,128)(2,1)S(1)}, u32[]{:S(2)}, u32[]{:S(2)}) collective-permute-start(bf16[128,512]{1,0:T(8,128)(2,1)} %get-tuple-element.246), channel_id=1, source_target_pairs={{0,2},{1,3},{2,0},{3,1},{4,6},{5,7},{6,4},{7,5},{8,10},{9,11},{10,... | collective-permute-start | bytes 393224 | tf_op jit(solution)/shard_map/ppermute | solution.py:57
  12.1 29.4 %collective-permute-start.34 = (bf16[128,512]{1,0:T(8,128)(2,1)}, bf16[128,512]{1,0:T(8,128)(2,1)}, u32[]{:S(2)}, u32[]{:S(2)}) collective-permute-start(bf16[128,512]{1,0:T(8,128)(2,1)} %get-tuple-element.247), channel_id=1, source_target_pairs={{0,4},{1,5},{2,6},{3,7},{4,0},{5,1},{6,2},{7,3},{8,12},{9,13},{10,... | collective-permute-start | bytes 393224 | tf_op jit(solution)/shard_map/ppermute | solution.py:57
  13.6 80.9 %collective-permute-start = (bf16[256,1024]{1,0:T(8,128)(2,1)}, bf16[256,1024]{1,0:T(8,128)(2,1)}, u32[]{:S(2)}, u32[]{:S(2)}) collective-permute-start(bf16[256,1024]{1,0:T(8,128)(2,1)} %param.17), channel_id=1, source_target_pairs={{0,1},{1,0},{2,3},{3,2},{4,5},{5,4},{6,7},{7,6},{8,9},{9,8},{10,11... | collective-permute-start | bytes 1572872 | tf_op jit(solution)/shard_map/ppermute | solution.py:50
  38.4 21.4 %collective-permute-start.1 = (bf16[128,1536]{0,1:T(8,128)(2,1)}, bf16[128,1536]{0,1:T(8,128)(2,1)S(1)}, u32[]{:S(2)}, u32[]{:S(2)}) collective-permute-start(bf16[128,1536]{0,1:T(8,128)(2,1)} %bitcast.783), channel_id=1, source_target_pairs={{0,1},{1,0},{2,3},{3,2},{4,5},{5,4},{6,7},{7,6},{8,9},{9,8},{10,11... | collective-permute-start | bytes 1179656 | tf_op jit(solution)/shard_map/ppermute | solution.py:50
  98.6 26.6 %collective-permute-start.39 = (bf16[256,1024]{1,0:T(8,128)(2,1)S(1)}, bf16[256,1024]{1,0:T(8,128)(2,1)S(1)}, u32[]{:S(2)}, u32[]{:S(2)}) collective-permute-start(bf16[256,1024]{1,0:T(8,128)(2,1)S(1)} %get-tuple-element.196), channel_id=1, source_target_pairs={{0,2},{1,3},{2,0},{3,1},{4,6},{5,7},{6,4},{7,5},{8,10},{9,11},{10,... | collective-permute-start | bytes 1572872 | tf_op jit(solution)/shard_map/ppermute | solution.py:57
  102.9 23.0 %collective-permute-start.41 = (bf16[256,1024]{1,0:T(8,128)(2,1)S(1)}, bf16[256,1024]{1,0:T(8,128)(2,1)S(1)}, u32[]{:S(2)}, u32[]{:S(2)}) collective-permute-start(bf16[256,1024]{1,0:T(8,128)(2,1)S(1)} %get-tuple-element.197), channel_id=1, source_target_pairs={{0,4},{1,5},{2,6},{3,7},{4,0},{5,1},{6,2},{7,3},{8,12},{9,13},{10,... | collective-permute-start | bytes 1572872 | tf_op jit(solution)/shard_map/ppermute | solution.py:57
  103.5 44.2 %collective-permute-start.24 = (bf16[2,512,512]{2,1,0:T(8,128)(2,1)S(1)}, bf16[2,512,512]{2,1,0:T(8,128)(2,1)S(1)}, u32[]{:S(2)}, u32[]{:S(2)}) collective-permute-start(bf16[2,512,512]{2,1,0:T(8,128)(2,1)S(1)} %copy-done.138), channel_id=1, source_target_pairs={{0,2},{1,3},{2,0},{3,1},{4,6},{5,7},{6,4},{7,5},{8,10},{9,11},{10,... | collective-permute-start | bytes 3145736 | tf_op jit(solution)/shard_map/ppermute | solution.py:57
  114.0 97.6 %collective-permute-start.22 = (bf16[2,512,512]{2,1,0:T(8,128)(2,1)}, bf16[2,512,512]{2,1,0:T(8,128)(2,1)}, u32[]{:S(2)}, u32[]{:S(2)}) collective-permute-start(bf16[2,512,512]{2,1,0:T(8,128)(2,1)} %pad_maximum_fusion.30), channel_id=1, source_target_pairs={{0,4},{1,5},{2,6},{3,7},{4,0},{5,1},{6,2},{7,3},{8,12},{9,13},{10,... | collective-permute-start | bytes 3145736 | tf_op jit(solution)/shard_map/ppermute | solution.py:57
  114.6 147.2 %collective-permute-start.46 = (bf16[2,512,512]{2,1,0:T(8,128)(2,1)}, bf16[2,512,512]{2,1,0:T(8,128)(2,1)}, u32[]{:S(2)}, u32[]{:S(2)}) collective-permute-start(bf16[2,512,512]{2,1,0:T(8,128)(2,1)} %pad_maximum_fusion.39), channel_id=1, source_target_pairs={{0,2},{1,3},{2,0},{3,1},{4,6},{5,7},{6,4},{7,5},{8,10},{9,11},{10,... | collective-permute-start | bytes 3145736 | tf_op jit(solution)/shard_map/ppermute | solution.py:57
  125.2 88.6 %collective-permute-start.44 = (bf16[2,512,512]{2,1,0:T(8,128)(2,1)}, bf16[2,512,512]{2,1,0:T(8,128)(2,1)}, u32[]{:S(2)}, u32[]{:S(2)}) collective-permute-start(bf16[2,512,512]{2,1,0:T(8,128)(2,1)} %pad_maximum_fusion.38), channel_id=1, source_target_pairs={{0,4},{1,5},{2,6},{3,7},{4,0},{5,1},{6,2},{7,3},{8,12},{9,13},{10,... | collective-permute-start | bytes 3145736 | tf_op jit(solution)/shard_map/ppermute | solution.py:57
  125.9 60.8 %collective-permute-start.5 = (bf16[2,256,768]{2,1,0:T(8,128)(2,1)S(1)}, bf16[2,256,768]{2,1,0:T(8,128)(2,1)S(1)}, u32[]{:S(2)}, u32[]{:S(2)}) collective-permute-start(bf16[2,256,768]{2,1,0:T(8,128)(2,1)S(1)} %pad_maximum_fusion.50), channel_id=1, source_target_pairs={{0,2},{1,3},{2,0},{3,1},{4,6},{5,7},{6,4},{7,5},{8,10},{9,11},{10,... | collective-permute-start | bytes 2359304 | tf_op jit(solution)/shard_map/ppermute | solution.py:57
  147.7 39.6 %collective-permute-start.3 = (bf16[2,256,768]{2,1,0:T(8,128)(2,1)S(1)}, bf16[2,256,768]{2,1,0:T(8,128)(2,1)S(1)}, u32[]{:S(2)}, u32[]{:S(2)}) collective-permute-start(bf16[2,256,768]{2,1,0:T(8,128)(2,1)S(1)} %pad_maximum_fusion.49), channel_id=1, source_target_pairs={{0,4},{1,5},{2,6},{3,7},{4,0},{5,1},{6,2},{7,3},{8,12},{9,13},{10,... | collective-permute-start | bytes 2359304 | tf_op jit(solution)/shard_map/ppermute | solution.py:57
  186.6 78.0 %collective-permute-start.31 = (bf16[2,256,768]{2,1,0:T(8,128)(2,1)}, bf16[2,256,768]{2,1,0:T(8,128)(2,1)}, u32[]{:S(2)}, u32[]{:S(2)}) collective-permute-start(bf16[2,256,768]{2,1,0:T(8,128)(2,1)} %pad_maximum_fusion.53), channel_id=1, source_target_pairs={{0,2},{1,3},{2,0},{3,1},{4,6},{5,7},{6,4},{7,5},{8,10},{9,11},{10,... | collective-permute-start | bytes 2359304 | tf_op jit(solution)/shard_map/ppermute | solution.py:57
  187.3 80.5 %collective-permute-start.29 = (bf16[2,256,768]{2,1,0:T(8,128)(2,1)}, bf16[2,256,768]{2,1,0:T(8,128)(2,1)}, u32[]{:S(2)}, u32[]{:S(2)}) collective-permute-start(bf16[2,256,768]{2,1,0:T(8,128)(2,1)} %pad_maximum_fusion.52), channel_id=1, source_target_pairs={{0,4},{1,5},{2,6},{3,7},{4,0},{5,1},{6,2},{7,3},{8,12},{9,13},{10,... | collective-permute-start | bytes 2359304 | tf_op jit(solution)/shard_map/ppermute | solution.py:57
  212.1 24.7 %collective-permute-start.20 = (bf16[2,256,1024]{2,1,0:T(8,128)(2,1)S(1)}, bf16[2,256,1024]{2,1,0:T(8,128)(2,1)S(1)}, u32[]{:S(2)}, u32[]{:S(2)}) collective-permute-start(bf16[2,256,1024]{2,1,0:T(8,128)(2,1)S(1)} %copy-done.137), channel_id=1, source_target_pairs={{0,2},{1,3},{2,0},{3,1},{4,6},{5,7},{6,4},{7,5},{8,10},{9,11},{10,... | collective-permute-start | bytes 3145736 | tf_op jit(solution)/shard_map/ppermute | solution.py:57
  218.5 25.5 %collective-permute-start.18 = (bf16[2,256,1024]{2,1,0:T(8,128)(2,1)S(1)}, bf16[2,256,1024]{2,1,0:T(8,128)(2,1)S(1)}, u32[]{:S(2)}, u32[]{:S(2)}) collective-permute-start(bf16[2,256,1024]{2,1,0:T(8,128)(2,1)S(1)} %copy-done.136), channel_id=1, source_target_pairs={{0,4},{1,5},{2,6},{3,7},{4,0},{5,1},{6,2},{7,3},{8,12},{9,13},{10,... | collective-permute-start | bytes 3145736 | tf_op jit(solution)/shard_map/ppermute | solution.py:57
  244.1 53.3 %collective-permute-start.42 = (bf16[2,256,1024]{2,1,0:T(8,128)(2,1)}, bf16[2,256,1024]{2,1,0:T(8,128)(2,1)}, u32[]{:S(2)}, u32[]{:S(2)}) collective-permute-start(bf16[2,256,1024]{2,1,0:T(8,128)(2,1)} %pad_maximum_fusion.37), channel_id=1, source_target_pairs={{0,2},{1,3},{2,0},{3,1},{4,6},{5,7},{6,4},{7,5},{8,10},{9,11},{10,... | collective-permute-start | bytes 3145736 | tf_op jit(solution)/shard_map/ppermute | solution.py:57
  244.7 56.5 %collective-permute-start.40 = (bf16[2,256,1024]{2,1,0:T(8,128)(2,1)}, bf16[2,256,1024]{2,1,0:T(8,128)(2,1)}, u32[]{:S(2)}, u32[]{:S(2)}) collective-permute-start(bf16[2,256,1024]{2,1,0:T(8,128)(2,1)} %pad_maximum_fusion.36), channel_id=1, source_target_pairs={{0,4},{1,5},{2,6},{3,7},{4,0},{5,1},{6,2},{7,3},{8,12},{9,13},{10,... | collective-permute-start | bytes 3145736 | tf_op jit(solution)/shard_map/ppermute | solution.py:57
  341.4 26.3 %collective-permute-start.130 = (bf16[2,512,512]{2,1,0:T(8,128)(2,1)}, bf16[2,512,512]{2,1,0:T(8,128)(2,1)}, u32[]{:S(2)}, u32[]{:S(2)}) collective-permute-start(bf16[2,512,512]{2,1,0:T(8,128)(2,1)} %dynamic-slice_bitcast_fusion.1), channel_id=1, source_target_pairs={{0,2},{1,3},{2,0},{3,1},{4,6},{5,7},{6,4},{7,5},{8,10},{9,11},{10,... | collective-permute-start | bytes 3145736 | tf_op jit(solution)/shard_map/ppermute | solution.py:57
  343.8 36.6 %collective-permute-start.135 = (bf16[2,512,512]{2,1,0:T(8,128)(2,1)}, bf16[2,512,512]{2,1,0:T(8,128)(2,1)}, u32[]{:S(2)}, u32[]{:S(2)}) collective-permute-start(bf16[2,512,512]{2,1,0:T(8,128)(2,1)} %dynamic-slice_bitcast_fusion), channel_id=1, source_target_pairs={{0,4},{1,5},{2,6},{3,7},{4,0},{5,1},{6,2},{7,3},{8,12},{9,13},{10,... | collective-permute-start | bytes 3145736 | tf_op jit(solution)/shard_map/ppermute | solution.py:57
  352.7 37.5 %collective-permute-start.109 = (bf16[2,256,1024]{2,1,0:T(8,128)(2,1)}, bf16[2,256,1024]{2,1,0:T(8,128)(2,1)}, u32[]{:S(2)}, u32[]{:S(2)}) collective-permute-start(bf16[2,256,1024]{2,1,0:T(8,128)(2,1)} %dynamic-slice_bitcast_fusion.5), channel_id=1, source_target_pairs={{0,2},{1,3},{2,0},{3,1},{4,6},{5,7},{6,4},{7,5},{8,10},{9,11},{10,... | collective-permute-start | bytes 3145736 | tf_op jit(solution)/shard_map/ppermute | solution.py:57
  354.4 42.9 %collective-permute-start.114 = (bf16[2,256,1024]{2,1,0:T(8,128)(2,1)}, bf16[2,256,1024]{2,1,0:T(8,128)(2,1)}, u32[]{:S(2)}, u32[]{:S(2)}) collective-permute-start(bf16[2,256,1024]{2,1,0:T(8,128)(2,1)} %dynamic-slice_bitcast_fusion.4), channel_id=1, source_target_pairs={{0,4},{1,5},{2,6},{3,7},{4,0},{5,1},{6,2},{7,3},{8,12},{9,13},{10,... | collective-permute-start | bytes 3145736 | tf_op jit(solution)/shard_map/ppermute | solution.py:57
  357.7 52.0 %collective-permute-start.88 = (bf16[2,128,512]{2,1,0:T(8,128)(2,1)S(1)}, bf16[2,128,512]{2,1,0:T(8,128)(2,1)}, u32[]{:S(2)}, u32[]{:S(2)}) collective-permute-start(bf16[2,128,512]{2,1,0:T(8,128)(2,1)S(1)} %dynamic-slice_bitcast_fusion.29), channel_id=1, source_target_pairs={{0,2},{1,3},{2,0},{3,1},{4,6},{5,7},{6,4},{7,5},{8,10},{9,11},{10,... | collective-permute-start | bytes 786440 | tf_op jit(solution)/shard_map/ppermute | solution.py:57
  367.7 43.7 %collective-permute-start.93 = (bf16[2,128,512]{2,1,0:T(8,128)(2,1)}, bf16[2,128,512]{2,1,0:T(8,128)(2,1)}, u32[]{:S(2)}, u32[]{:S(2)}) collective-permute-start(bf16[2,128,512]{2,1,0:T(8,128)(2,1)} %dynamic-slice_bitcast_fusion.28), channel_id=1, source_target_pairs={{0,4},{1,5},{2,6},{3,7},{4,0},{5,1},{6,2},{7,3},{8,12},{9,13},{10,... | collective-permute-start | bytes 786440 | tf_op jit(solution)/shard_map/ppermute | solution.py:57
  380.4 51.2 %collective-permute-start.131 = (bf16[512,512]{1,0:T(8,128)(2,1)}, bf16[512,512]{1,0:T(8,128)(2,1)}, u32[]{:S(2)}, u32[]{:S(2)}) collective-permute-start(bf16[512,512]{1,0:T(8,128)(2,1)} %dynamic-slice_bitcast_fusion.13), channel_id=1, source_target_pairs={{0,4},{1,5},{2,6},{3,7},{4,0},{5,1},{6,2},{7,3},{8,12},{9,13},{10,... | collective-permute-start | bytes 1572872 | tf_op jit(solution)/shard_map/ppermute | solution.py:57
  390.2 55.6 %collective-permute-start.136 = (bf16[512,512]{1,0:T(8,128)(2,1)}, bf16[512,512]{1,0:T(8,128)(2,1)}, u32[]{:S(2)}, u32[]{:S(2)}) collective-permute-start(bf16[512,512]{1,0:T(8,128)(2,1)} %dynamic-slice_bitcast_fusion.12), channel_id=1, source_target_pairs={{0,2},{1,3},{2,0},{3,1},{4,6},{5,7},{6,4},{7,5},{8,10},{9,11},{10,... | collective-permute-start | bytes 1572872 | tf_op jit(solution)/shard_map/ppermute | solution.py:57
  397.3 50.5 %collective-permute-start.110 = (bf16[256,1024]{1,0:T(8,128)(2,1)}, bf16[256,1024]{1,0:T(8,128)(2,1)}, u32[]{:S(2)}, u32[]{:S(2)}) collective-permute-start(bf16[256,1024]{1,0:T(8,128)(2,1)} %dynamic-slice_bitcast_fusion.18), channel_id=1, source_target_pairs={{0,4},{1,5},{2,6},{3,7},{4,0},{5,1},{6,2},{7,3},{8,12},{9,13},{10,... | collective-permute-start | bytes 1572872 | tf_op jit(solution)/shard_map/ppermute | solution.py:57
  427.2 22.4 %collective-permute-start.115 = (bf16[256,1024]{1,0:T(8,128)(2,1)S(1)}, bf16[256,1024]{1,0:T(8,128)(2,1)S(1)}, u32[]{:S(2)}, u32[]{:S(2)}) collective-permute-start(bf16[256,1024]{1,0:T(8,128)(2,1)S(1)} %copy-done.149), channel_id=1, source_target_pairs={{0,2},{1,3},{2,0},{3,1},{4,6},{5,7},{6,4},{7,5},{8,10},{9,11},{10,... | collective-permute-start | bytes 1572872 | tf_op jit(solution)/shard_map/ppermute | solution.py:57
  428.2 33.7 %collective-permute-start.67 = (bf16[2,256,768]{2,1,0:T(8,128)(2,1)S(1)}, bf16[2,256,768]{2,1,0:T(8,128)(2,1)S(1)}, u32[]{:S(2)}, u32[]{:S(2)}) collective-permute-start(bf16[2,256,768]{2,1,0:T(8,128)(2,1)S(1)} %dynamic-slice_bitcast_fusion.9), channel_id=1, source_target_pairs={{0,2},{1,3},{2,0},{3,1},{4,6},{5,7},{6,4},{7,5},{8,10},{9,11},{10,... | collective-permute-start | bytes 2359304 | tf_op jit(solution)/shard_map/ppermute | solution.py:57
  444.4 32.3 %collective-permute-start.72 = (bf16[2,256,768]{2,1,0:T(8,128)(2,1)S(1)}, bf16[2,256,768]{2,1,0:T(8,128)(2,1)S(1)}, u32[]{:S(2)}, u32[]{:S(2)}) collective-permute-start(bf16[2,256,768]{2,1,0:T(8,128)(2,1)S(1)} %dynamic-slice_bitcast_fusion.8), channel_id=1, source_target_pairs={{0,4},{1,5},{2,6},{3,7},{4,0},{5,1},{6,2},{7,3},{8,12},{9,13},{10,... | collective-permute-start | bytes 2359304 | tf_op jit(solution)/shard_map/ppermute | solution.py:57
  449.7 31.9 %collective-permute-start.132 = (bf16[512,512]{1,0:T(8,128)(2,1)S(1)}, bf16[512,512]{1,0:T(8,128)(2,1)S(1)}, u32[]{:S(2)}, u32[]{:S(2)}) collective-permute-start(bf16[512,512]{1,0:T(8,128)(2,1)S(1)} %fusion.110), channel_id=1, source_target_pairs={{0,8},{24,16},{1,9},{25,17},{2,10},{26,18},{3,11},{27,19},{4,12},{... | collective-permute-start | bytes 1572872 | tf_op jit(solution)/shard_map/ppermute | solution.py:107
  458.8 24.4 %collective-permute-start.137 = (bf16[512,512]{1,0:T(8,128)(2,1)S(1)}, bf16[512,512]{1,0:T(8,128)(2,1)S(1)}, u32[]{:S(2)}, u32[]{:S(2)}) collective-permute-start(bf16[512,512]{1,0:T(8,128)(2,1)S(1)} %fusion.109), channel_id=1, source_target_pairs={{0,8},{24,16},{1,9},{25,17},{2,10},{26,18},{3,11},{27,19},{4,12},{... | collective-permute-start | bytes 1572872 | tf_op jit(solution)/shard_map/ppermute | solution.py:107
  460.2 35.0 %collective-permute-start.111 = (bf16[256,1024]{1,0:T(8,128)(2,1)S(1)}, bf16[256,1024]{1,0:T(8,128)(2,1)S(1)}, u32[]{:S(2)}, u32[]{:S(2)}) collective-permute-start(bf16[256,1024]{1,0:T(8,128)(2,1)S(1)} %fusion.114), channel_id=1, source_target_pairs={{0,8},{24,16},{1,9},{25,17},{2,10},{26,18},{3,11},{27,19},{4,12},{... | collective-permute-start | bytes 1572872 | tf_op jit(solution)/shard_map/ppermute | solution.py:107
  476.7 21.6 %collective-permute-start.116 = (bf16[256,1024]{1,0:T(8,128)(2,1)S(1)}, bf16[256,1024]{1,0:T(8,128)(2,1)S(1)}, u32[]{:S(2)}, u32[]{:S(2)}) collective-permute-start(bf16[256,1024]{1,0:T(8,128)(2,1)S(1)} %fusion.113), channel_id=1, source_target_pairs={{0,8},{24,16},{1,9},{25,17},{2,10},{26,18},{3,11},{27,19},{4,12},{... | collective-permute-start | bytes 1572872 | tf_op jit(solution)/shard_map/ppermute | solution.py:107
  483.2 21.7 %collective-permute-start.133 = (bf16[512,512]{1,0:T(8,128)(2,1)S(1)}, bf16[512,512]{1,0:T(8,128)(2,1)S(1)}, u32[]{:S(2)}, u32[]{:S(2)}) collective-permute-start(bf16[512,512]{1,0:T(8,128)(2,1)S(1)} %add_convert_fusion.3), channel_id=1, source_target_pairs={{8,16},{16,8},{9,17},{17,9},{10,18},{18,10},{11,19},{19,11},{12,20... | collective-permute-start | bytes 1572872 | tf_op jit(solution)/shard_map/ppermute | solution.py:109
  499.8 33.5 %collective-permute-start.117 = (bf16[256,1024]{1,0:T(8,128)(2,1)S(1)}, bf16[256,1024]{1,0:T(8,128)(2,1)S(1)}, u32[]{:S(2)}, u32[]{:S(2)}) collective-permute-start(bf16[256,1024]{1,0:T(8,128)(2,1)S(1)} %add_convert_fusion.9), channel_id=1, source_target_pairs={{8,16},{16,8},{9,17},{17,9},{10,18},{18,10},{11,19},{19,11},{12,20... | collective-permute-start | bytes 1572872 | tf_op jit(solution)/shard_map/ppermute | solution.py:109
  500.6 36.9 %collective-permute-start.120 = (bf16[2,512,512]{2,1,0:T(8,128)(2,1)S(1)}, bf16[2,512,512]{2,1,0:T(8,128)(2,1)S(1)}, u32[]{:S(2)}, u32[]{:S(2)}) collective-permute-start(bf16[2,512,512]{2,1,0:T(8,128)(2,1)S(1)} %dynamic-slice_bitcast_fusion.3), channel_id=1, source_target_pairs={{0,2},{1,3},{2,0},{3,1},{4,6},{5,7},{6,4},{7,5},{8,10},{9,11},{10,... | collective-permute-start | bytes 3145736 | tf_op jit(solution)/shard_map/ppermute | solution.py:57
  504.9 35.1 %collective-permute-start.125 = (bf16[2,512,512]{2,1,0:T(8,128)(2,1)S(1)}, bf16[2,512,512]{2,1,0:T(8,128)(2,1)S(1)}, u32[]{:S(2)}, u32[]{:S(2)}) collective-permute-start(bf16[2,512,512]{2,1,0:T(8,128)(2,1)S(1)} %dynamic-slice_bitcast_fusion.2), channel_id=1, source_target_pairs={{0,4},{1,5},{2,6},{3,7},{4,0},{5,1},{6,2},{7,3},{8,12},{9,13},{10,... | collective-permute-start | bytes 3145736 | tf_op jit(solution)/shard_map/ppermute | solution.py:57
  527.5 21.2 %collective-permute-start.98 = (bf16[2,256,1024]{2,1,0:T(8,128)(2,1)S(1)}, bf16[2,256,1024]{2,1,0:T(8,128)(2,1)S(1)}, u32[]{:S(2)}, u32[]{:S(2)}) collective-permute-start(bf16[2,256,1024]{2,1,0:T(8,128)(2,1)S(1)} %dynamic-slice_bitcast_fusion.7), channel_id=1, source_target_pairs={{0,2},{1,3},{2,0},{3,1},{4,6},{5,7},{6,4},{7,5},{8,10},{9,11},{10,... | collective-permute-start | bytes 3145736 | tf_op jit(solution)/shard_map/ppermute | solution.py:57
  535.3 69.3 %collective-permute-start.134 = (bf16[512,512]{1,0:T(8,128)(2,1)}, bf16[512,512]{1,0:T(8,128)(2,1)}, u32[]{:S(2)}, u32[]{:S(2)}) collective-permute-start(bf16[512,512]{1,0:T(8,128)(2,1)} %add_convert_fusion.2), channel_id=1, source_target_pairs={{8,0},{16,24},{9,1},{17,25},{10,2},{18,26},{11,3},{19,27},{12,4},{... | collective-permute-start | bytes 1572872 | tf_op jit(solution)/shard_map/ppermute | solution.py:111
  537.5 73.3 %collective-permute-start.139 = (bf16[512,512]{1,0:T(8,128)(2,1)}, bf16[512,512]{1,0:T(8,128)(2,1)}, u32[]{:S(2)}, u32[]{:S(2)}) collective-permute-start(bf16[512,512]{1,0:T(8,128)(2,1)} %add_convert_fusion), channel_id=1, source_target_pairs={{8,0},{16,24},{9,1},{17,25},{10,2},{18,26},{11,3},{19,27},{12,4},{... | collective-permute-start | bytes 1572872 | tf_op jit(solution)/shard_map/ppermute | solution.py:111
  540.0 49.4 %collective-permute-start.113 = (bf16[256,1024]{1,0:T(8,128)(2,1)S(1)}, bf16[256,1024]{1,0:T(8,128)(2,1)}, u32[]{:S(2)}, u32[]{:S(2)}) collective-permute-start(bf16[256,1024]{1,0:T(8,128)(2,1)S(1)} %add_convert_fusion.10), channel_id=1, source_target_pairs={{8,0},{16,24},{9,1},{17,25},{10,2},{18,26},{11,3},{19,27},{12,4},{... | collective-permute-start | bytes 1572872 | tf_op jit(solution)/shard_map/ppermute | solution.py:111
  554.9 44.5 %collective-permute-start.118 = (bf16[256,1024]{1,0:T(8,128)(2,1)S(1)}, bf16[256,1024]{1,0:T(8,128)(2,1)}, u32[]{:S(2)}, u32[]{:S(2)}) collective-permute-start(bf16[256,1024]{1,0:T(8,128)(2,1)S(1)} %add_convert_fusion.8), channel_id=1, source_target_pairs={{8,0},{16,24},{9,1},{17,25},{10,2},{18,26},{11,3},{19,27},{12,4},{... | collective-permute-start | bytes 1572872 | tf_op jit(solution)/shard_map/ppermute | solution.py:111
  557.6 100.1 %collective-permute-start.71 = (bf16[256,768]{1,0:T(8,128)(2,1)S(1)}, bf16[256,768]{1,0:T(8,128)(2,1)}, u32[]{:S(2)}, u32[]{:S(2)}) collective-permute-start(bf16[256,768]{1,0:T(8,128)(2,1)S(1)} %add_convert_fusion.19), channel_id=1, source_target_pairs={{8,0},{16,24},{9,1},{17,25},{10,2},{18,26},{11,3},{19,27},{12,4},{... | collective-permute-start | bytes 1179656 | tf_op jit(solution)/shard_map/ppermute | solution.py:111
  589.4 70.6 %collective-permute-start.76 = (bf16[256,768]{1,0:T(8,128)(2,1)}, bf16[256,768]{1,0:T(8,128)(2,1)}, u32[]{:S(2)}, u32[]{:S(2)}) collective-permute-start(bf16[256,768]{1,0:T(8,128)(2,1)} %add_convert_fusion.17), channel_id=1, source_target_pairs={{8,0},{16,24},{9,1},{17,25},{10,2},{18,26},{11,3},{19,27},{12,4},{... | collective-permute-start | bytes 1179656 | tf_op jit(solution)/shard_map/ppermute | solution.py:111
  599.4 89.5 %collective-permute-start.121 = (bf16[512,512]{1,0:T(8,128)(2,1)}, bf16[512,512]{1,0:T(8,128)(2,1)}, u32[]{:S(2)}, u32[]{:S(2)}) collective-permute-start(bf16[512,512]{1,0:T(8,128)(2,1)} %dynamic-slice_bitcast_fusion.15), channel_id=1, source_target_pairs={{0,4},{1,5},{2,6},{3,7},{4,0},{5,1},{6,2},{7,3},{8,12},{9,13},{10,... | collective-permute-start | bytes 1572872 | tf_op jit(solution)/shard_map/ppermute | solution.py:57
  628.5 63.1 %collective-permute-start.126 = (bf16[512,512]{1,0:T(8,128)(2,1)}, bf16[512,512]{1,0:T(8,128)(2,1)}, u32[]{:S(2)}, u32[]{:S(2)}) collective-permute-start(bf16[512,512]{1,0:T(8,128)(2,1)} %dynamic-slice_bitcast_fusion.14), channel_id=1, source_target_pairs={{0,2},{1,3},{2,0},{3,1},{4,6},{5,7},{6,4},{7,5},{8,10},{9,11},{10,... | collective-permute-start | bytes 1572872 | tf_op jit(solution)/shard_map/ppermute | solution.py:57
  654.5 40.4 %collective-permute-start.99 = (bf16[256,1024]{1,0:T(8,128)(2,1)}, bf16[256,1024]{1,0:T(8,128)(2,1)}, u32[]{:S(2)}, u32[]{:S(2)}) collective-permute-start(bf16[256,1024]{1,0:T(8,128)(2,1)} %dynamic-slice_bitcast_fusion.21), channel_id=1, source_target_pairs={{0,4},{1,5},{2,6},{3,7},{4,0},{5,1},{6,2},{7,3},{8,12},{9,13},{10,... | collective-permute-start | bytes 1572872 | tf_op jit(solution)/shard_map/ppermute | solution.py:57
  657.7 39.6 %collective-permute-start.104 = (bf16[256,1024]{1,0:T(8,128)(2,1)}, bf16[256,1024]{1,0:T(8,128)(2,1)}, u32[]{:S(2)}, u32[]{:S(2)}) collective-permute-start(bf16[256,1024]{1,0:T(8,128)(2,1)} %dynamic-slice_bitcast_fusion.20), channel_id=1, source_target_pairs={{0,2},{1,3},{2,0},{3,1},{4,6},{5,7},{6,4},{7,5},{8,10},{9,11},{10,... | collective-permute-start | bytes 1572872 | tf_op jit(solution)/shard_map/ppermute | solution.py:57
  688.0 21.7 %collective-permute-start.119 = (bf16[128,2048]{1,0:T(8,128)(2,1)}, bf16[128,2048]{1,0:T(8,128)(2,1)}, u32[]{:S(2)}, u32[]{:S(2)}) collective-permute-start(bf16[128,2048]{1,0:T(8,128)(2,1)} %get-tuple-element.173), channel_id=1, source_target_pairs={{0,1},{1,0},{2,3},{3,2},{4,5},{5,4},{6,7},{7,6},{8,9},{9,8},{10,11... | collective-permute-start | bytes 1572872 | tf_op jit(solution)/shard_map/ppermute | solution.py:50
  688.9 30.5 %collective-permute-start.55 = (bf16[256,1024]{1,0:T(8,128)(2,1)}, bf16[256,1024]{1,0:T(8,128)(2,1)}, u32[]{:S(2)}, u32[]{:S(2)}) collective-permute-start(bf16[256,1024]{1,0:T(8,128)(2,1)} %slice.559), channel_id=1, source_target_pairs={{0,1},{1,0},{2,3},{3,2},{4,5},{5,4},{6,7},{7,6},{8,9},{9,8},{10,11... | collective-permute-start | bytes 1572872 | tf_op jit(solution)/shard_map/ppermute | solution.py:50
  691.7 47.1 %collective-permute-start.56 = (bf16[2,256,768]{2,1,0:T(8,128)(2,1)}, bf16[2,256,768]{2,1,0:T(8,128)(2,1)}, u32[]{:S(2)}, u32[]{:S(2)}) collective-permute-start(bf16[2,256,768]{2,1,0:T(8,128)(2,1)} %dynamic-slice_bitcast_fusion.11), channel_id=1, source_target_pairs={{0,2},{1,3},{2,0},{3,1},{4,6},{5,7},{6,4},{7,5},{8,10},{9,11},{10,... | collective-permute-start | bytes 2359304 | tf_op jit(solution)/shard_map/ppermute | solution.py:57
  694.9 59.3 %collective-permute-start.61 = (bf16[2,256,768]{2,1,0:T(8,128)(2,1)}, bf16[2,256,768]{2,1,0:T(8,128)(2,1)}, u32[]{:S(2)}, u32[]{:S(2)}) collective-permute-start(bf16[2,256,768]{2,1,0:T(8,128)(2,1)} %dynamic-slice_bitcast_fusion.10), channel_id=1, source_target_pairs={{0,4},{1,5},{2,6},{3,7},{4,0},{5,1},{6,2},{7,3},{8,12},{9,13},{10,... | collective-permute-start | bytes 2359304 | tf_op jit(solution)/shard_map/ppermute | solution.py:57
  709.7 48.7 %collective-permute-start.122 = (bf16[512,512]{1,0:T(8,128)(2,1)}, bf16[512,512]{1,0:T(8,128)(2,1)}, u32[]{:S(2)}, u32[]{:S(2)}) collective-permute-start(bf16[512,512]{1,0:T(8,128)(2,1)} %fusion.112), channel_id=1, source_target_pairs={{0,8},{24,16},{1,9},{25,17},{2,10},{26,18},{3,11},{27,19},{4,12},{... | collective-permute-start | bytes 1572872 | tf_op jit(solution)/shard_map/ppermute | solution.py:107
  719.5 41.3 %collective-permute-start.127 = (bf16[512,512]{1,0:T(8,128)(2,1)}, bf16[512,512]{1,0:T(8,128)(2,1)}, u32[]{:S(2)}, u32[]{:S(2)}) collective-permute-start(bf16[512,512]{1,0:T(8,128)(2,1)} %fusion.111), channel_id=1, source_target_pairs={{0,8},{24,16},{1,9},{25,17},{2,10},{26,18},{3,11},{27,19},{4,12},{... | collective-permute-start | bytes 1572872 | tf_op jit(solution)/shard_map/ppermute | solution.py:107
  731.0 32.0 %collective-permute-start.100 = (bf16[256,1024]{1,0:T(8,128)(2,1)S(1)}, bf16[256,1024]{1,0:T(8,128)(2,1)S(1)}, u32[]{:S(2)}, u32[]{:S(2)}) collective-permute-start(bf16[256,1024]{1,0:T(8,128)(2,1)S(1)} %copy-done.93), channel_id=1, source_target_pairs={{0,8},{24,16},{1,9},{25,17},{2,10},{26,18},{3,11},{27,19},{4,12},{... | collective-permute-start | bytes 1572872 | tf_op jit(solution)/shard_map/ppermute | solution.py:107
  764.9 23.7 %collective-permute-start.106 = (bf16[256,1024]{1,0:T(8,128)(2,1)S(1)}, bf16[256,1024]{1,0:T(8,128)(2,1)S(1)}, u32[]{:S(2)}, u32[]{:S(2)}) collective-permute-start(bf16[256,1024]{1,0:T(8,128)(2,1)S(1)} %add_convert_fusion.13), channel_id=1, source_target_pairs={{8,16},{16,8},{9,17},{17,9},{10,18},{18,10},{11,19},{19,11},{12,20... | collective-permute-start | bytes 1572872 | tf_op jit(solution)/shard_map/ppermute | solution.py:109
  778.9 58.4 %collective-permute-start.124 = (bf16[512,512]{1,0:T(8,128)(2,1)S(1)}, bf16[512,512]{1,0:T(8,128)(2,1)}, u32[]{:S(2)}, u32[]{:S(2)}) collective-permute-start(bf16[512,512]{1,0:T(8,128)(2,1)S(1)} %add_convert_fusion.6), channel_id=1, source_target_pairs={{8,0},{16,24},{9,1},{17,25},{10,2},{18,26},{11,3},{19,27},{12,4},{... | collective-permute-start | bytes 1572872 | tf_op jit(solution)/shard_map/ppermute | solution.py:111
  780.4 58.1 %collective-permute-start.129 = (bf16[512,512]{1,0:T(8,128)(2,1)S(1)}, bf16[512,512]{1,0:T(8,128)(2,1)}, u32[]{:S(2)}, u32[]{:S(2)}) collective-permute-start(bf16[512,512]{1,0:T(8,128)(2,1)S(1)} %add_convert_fusion.4), channel_id=1, source_target_pairs={{8,0},{16,24},{9,1},{17,25},{10,2},{18,26},{11,3},{19,27},{12,4},{... | collective-permute-start | bytes 1572872 | tf_op jit(solution)/shard_map/ppermute | solution.py:111
  783.6 41.1 %collective-permute-start.102 = (bf16[256,1024]{1,0:T(8,128)(2,1)S(1)}, bf16[256,1024]{1,0:T(8,128)(2,1)S(1)}, u32[]{:S(2)}, u32[]{:S(2)}) collective-permute-start(bf16[256,1024]{1,0:T(8,128)(2,1)S(1)} %add_convert_fusion.14), channel_id=1, source_target_pairs={{8,0},{16,24},{9,1},{17,25},{10,2},{18,26},{11,3},{19,27},{12,4},{... | collective-permute-start | bytes 1572872 | tf_op jit(solution)/shard_map/ppermute | solution.py:111
  789.5 46.4 %collective-permute-start.107 = (bf16[256,1024]{1,0:T(8,128)(2,1)S(1)}, bf16[256,1024]{1,0:T(8,128)(2,1)S(1)}, u32[]{:S(2)}, u32[]{:S(2)}) collective-permute-start(bf16[256,1024]{1,0:T(8,128)(2,1)S(1)} %add_convert_fusion.12), channel_id=1, source_target_pairs={{8,0},{16,24},{9,1},{17,25},{10,2},{18,26},{11,3},{19,27},{12,4},{... | collective-permute-start | bytes 1572872 | tf_op jit(solution)/shard_map/ppermute | solution.py:111
  790.9 52.1 %collective-permute-start.60 = (bf16[256,768]{1,0:T(8,128)(2,1)S(1)}, bf16[256,768]{1,0:T(8,128)(2,1)}, u32[]{:S(2)}, u32[]{:S(2)}) collective-permute-start(bf16[256,768]{1,0:T(8,128)(2,1)S(1)} %add_convert_fusion.23), channel_id=1, source_target_pairs={{8,0},{16,24},{9,1},{17,25},{10,2},{18,26},{11,3},{19,27},{12,4},{... | collective-permute-start | bytes 1179656 | tf_op jit(solution)/shard_map/ppermute | solution.py:111
  824.7 22.5 %collective-permute-start.65 = (bf16[256,768]{1,0:T(8,128)(2,1)}, bf16[256,768]{1,0:T(8,128)(2,1)}, u32[]{:S(2)}, u32[]{:S(2)}) collective-permute-start(bf16[256,768]{1,0:T(8,128)(2,1)} %add_convert_fusion.21), channel_id=1, source_target_pairs={{8,0},{16,24},{9,1},{17,25},{10,2},{18,26},{11,3},{19,27},{12,4},{... | collective-permute-start | bytes 1179656 | tf_op jit(solution)/shard_map/ppermute | solution.py:111
  (297 other events, 2489.0 us)

commit v2 on v1

--- a/solution.py
+++ b/solution.py
@@ -1,11 +1,15 @@
+import functools
 import math
 
 import jax
 import jax.numpy as jnp
 from jax import lax
+from jax.experimental import pallas as pl
+from jax.experimental.pallas import tpu as pltpu
 from jax.sharding import PartitionSpec as P
 
 HEADS = 16
+MESH = pl.DeviceIdType.MESH
 
 
 epsilon = 1e-05
@@ -23,11 +27,6 @@
 def norm_back(grad_norm, normed, rstd):
     inner = jnp.mean(grad_norm * normed, axis=-1, keepdims=True)
     return rstd * (grad_norm - jnp.mean(grad_norm, axis=-1, keepdims=True) - normed * inner)
-
-
-def gelu_slope(pre):
-    cdf = 0.5 * (1.0 + lax.erf(pre * (1.0 / math.sqrt(2.0))))
-    return cdf + pre * jnp.exp(-0.5 * pre * pre) * (1.0 / math.sqrt(2.0 * math.pi))
 
 
 def column_sums(values):
@@ -125,15 +124,6 @@
     return ((0, columns // 2), (columns // 2, columns))
 
 
-def gather_weight(net, piece):
-    orders = (list(range(net.bits)), list(reversed(range(net.bits))))
-    parts = [
-        net.gather_chips(piece[:, start:stop], order)
-        for order, (start, stop) in zip(orders, halves(piece.shape[1]))
-    ]
-    return jnp.concatenate(parts, axis=2)
-
-
 def scatter_weight(net, value):
     orders = (list(range(net.bits)), list(reversed(range(net.bits))))
     parts = [
@@ -143,17 +133,10 @@
     return jnp.concatenate(parts, axis=1)
 
 
-def by_core(weight, net, groups):
-    rows, columns = weight.shape
-    split = weight.reshape(rows, groups * net.high, 2, columns // (2 * groups * net.high))
-    mine = lax.dynamic_index_in_dim(split, net.core, 2, keepdims=False)
-    other = lax.dynamic_index_in_dim(split, 1 - net.core, 2, keepdims=False)
-    return mine.reshape(rows, columns // 2), other.reshape(rows, columns // 2)
-
-
-def swap_columns(weight, net, groups):
-    mine, other = by_core(weight, net, groups)
-    return net.in_order(mine, net.over_core(other), net.core).reshape(-1, mine.shape[1])
+def by_half(weight, net, groups):
+    layers, rows, columns = weight.shape
+    split = weight.reshape(layers, rows, groups * net.high, 2, columns // (2 * groups * net.high))
+    return split.transpose(0, 3, 1, 2, 4).reshape(layers, 2, rows, columns // 2)
 
 
 def swap_back(value, net, groups):
@@ -175,58 +158,589 @@
     return rows.reshape(2, rows.shape[0] // 2, heads, rows.shape[1] // heads)
 
 
-def masked_scores(query, key_rows, same):
-    scale = 1.0 / math.sqrt(query.shape[-1])
-    scores = jnp.einsum("sqhd,skhd->shqk", query, key_rows, preferred_element_type=wide) * scale
-    return jnp.where(same[:, None], scores, neg_large)
-
-
-def forward_layer(net, hidden, weights, small, same):
-    w_qkv, w_out, w_up, w_down = weights
-    bias_qkv, bias_out, bias_up, bias_down, gain_first, shift_first, gain_second, shift_second = small
-    heads = HEADS // 2
-    third = w_qkv.shape[1] // 3
-    both_hidden = net.pair(hidden.astype(low))
-    qkv = (jnp.dot(both_hidden, w_qkv, preferred_element_type=wide) + bias_qkv).astype(low)
-    query = split_heads(qkv[:, :third], heads)
-    key_rows = split_heads(qkv[:, third : 2 * third], heads)
-    value_rows = split_heads(qkv[:, 2 * third :], heads)
-    masked = masked_scores(query, key_rows, same)
-    top = jnp.max(masked, axis=3, keepdims=True)
-    expo = jnp.exp(masked - top)
-    total = jnp.sum(expo, axis=3, keepdims=True)
-    probs = (expo / total).astype(low)
-    log_total = top + jnp.log(total)
-    head_top = jnp.max(top, axis=(0, 2, 3))
-    attended = jnp.einsum("shqk,skhd->sqhd", probs, value_rows, preferred_element_type=wide)
-    attended = attended.reshape(qkv.shape[0], third).astype(low)
-    summed_one = (
-        hidden + net.join(jnp.dot(attended, w_out, preferred_element_type=wide)) + bias_out
-    )
-    normed_one, rstd_one = normalize(summed_one)
-    first = normed_one * gain_first + shift_first
-    both_first = net.pair(first.astype(low))
-    pre = jnp.dot(both_first, w_up, preferred_element_type=wide) + bias_up
-    activation = jax.nn.gelu(pre, approximate=False).astype(low)
-    summed_two = (
-        first + net.join(jnp.dot(activation, w_down, preferred_element_type=wide)) + bias_down
-    )
-    normed_two, rstd_two = normalize(summed_two)
-    result = normed_two * gain_second + shift_second
-    saved = (
-        both_hidden,
-        qkv,
-        log_total,
-        attended,
-        normed_one,
-        rstd_one,
-        both_first,
-        pre,
-        activation,
-        normed_two,
-        rstd_two,
-    )
-    return (result, head_top, saved)
+class Place:
+    def __init__(self, dims):
+        self.dims = dims
+        step = dims.step
+        self.rep = lax.axis_index("rep")
+        self.me = lax.axis_index("shard")
+        self.half = (self.me // step) % 2
+        self.pair = (self.me // (2 * step)) * step + self.me % step
+        self.plane = self.rep % 2
+
+    def flip(self, value, bit):
+        size = 1 << bit
+        return value + size * (1 - 2 * ((value // size) % 2))
+
+    def mate(self):
+        return (self.rep, self.me + self.dims.step * (1 - 2 * self.half))
+
+    def over_bit(self, bit):
+        stride = (1 << bit) if (1 << bit) < self.dims.step else (2 << bit)
+        return (self.rep, self.me + stride * (1 - 2 * ((self.me // stride) % 2)))
+
+    def over_plane(self):
+        return (self.rep + 1 - 2 * self.plane, self.me)
+
+    def first_shard(self, pair):
+        step = self.dims.step
+        return (pair // step) * (2 * step) + pair % step
+
+
+class Dims:
+    def __init__(self, shards, reps, step, layers, tokens, width, hidden):
+        self.shards, self.reps, self.step = shards, reps, step
+        self.pairs = shards // 2
+        self.bits = self.pairs.bit_length() - 1
+        self.layers, self.tokens, self.width, self.hidden = layers, tokens, width, hidden
+        self.head_dim = width // HEADS
+        self.third = width // 2
+        self.rows = width // shards
+        self.kinds = (
+            (self.rows, width, 3 * width // 2, True),
+            (self.rows, width // 2, width, False),
+            (self.rows, width, hidden // 2, True),
+            (hidden // shards, hidden // 2, width, False),
+        )
+
+
+def remote(src, dst, send, recv, where):
+    return pltpu.make_async_remote_copy(
+        src_ref=src, dst_ref=dst, send_sem=send, recv_sem=recv, device_id=where, device_id_type=MESH
+    )
+
+
+class Gather:
+    def __init__(self, place, layer, kind, source, whole, sems, in_plane):
+        self.place, self.dims = place, place.dims
+        self.layer, self.kind = layer, kind
+        self.source, self.whole = source, whole
+        self.rows, self.held, self.columns, self.paired = self.dims.kinds[kind]
+        self.local, self.send, self.recv = sems
+        self.at = layer * 4 + kind
+        self.in_plane = in_plane
+        self.stage = 0
+        self.stages = self.dims.bits + (2 if in_plane < self.columns else 1)
+
+    def blocks(self, pair):
+        if not self.paired:
+            return [pair * self.rows], self.rows
+        first = self.place.first_shard(pair) * self.rows
+        if self.dims.step == 1:
+            return [first], 2 * self.rows
+        return [first, first + self.dims.step * self.rows], self.rows
+
+    def window(self, part):
+        size = self.in_plane // 2
+        if (size % 128) and part < 2:
+            low_size = size // 128 * 128
+            size = low_size if part == 0 else self.in_plane - low_size
+            offset = 0 if part == 0 else low_size
+        else:
+            offset = part * size
+        start = self.place.plane * (self.columns - self.in_plane) + offset
+        return pl.ds(pl.multiple_of(start, 128), size), size
+
+    def order(self, part):
+        bits = list(range(self.dims.bits))
+        return bits if part == 0 else bits[::-1]
+
+    def subset(self, done):
+        pairs = [self.place.pair]
+        for bit in done:
+            pairs = pairs + [self.place.flip(pair, bit) for pair in pairs]
+        return pairs
+
+    def begin(self):
+        place = self.place
+        if self.paired:
+            mine = place.me * self.rows
+            rows = pl.ds(pl.multiple_of(mine, 16), self.rows)
+            pltpu.make_async_copy(
+                self.source.at[self.layer, place.half], self.whole.at[self.layer, rows], self.local.at[self.at]
+            ).start()
+            remote(
+                self.source.at[self.layer, 1 - place.half],
+                self.whole.at[self.layer, rows],
+                self.send.at[self.at, 0],
+                self.recv.at[self.at, 0],
+                place.mate(),
+            ).start()
+        else:
+            rows = pl.ds(pl.multiple_of(place.pair * self.rows, 16), self.rows)
+            pltpu.make_async_copy(
+                self.source.at[self.layer], self.whole.at[self.layer, rows], self.local.at[self.at]
+            ).start()
+
+    def some(self, rows, columns):
+        return self.whole.at[self.layer, pl.ds(0, rows), columns]
+
+    def phase(self, turn):
+        place = self.place
+        for part in range(2):
+            order = self.order(part)
+            columns, _ = self.window(part)
+            for pair in self.subset(order[:turn]):
+                starts, count = self.blocks(pair)
+                for start in starts:
+                    block = self.whole.at[self.layer, pl.ds(pl.multiple_of(start, 16), count), columns]
+                    remote(
+                        block,
+                        block,
+                        self.send.at[self.at, 1 + 2 * turn + part],
+                        self.recv.at[self.at, 1 + 2 * turn + part],
+                        place.over_bit(order[turn]),
+                    ).start()
+
+    def phase_bytes(self, turn, part):
+        columns = pl.ds(0, self.window(part)[1])
+        per_pair = self.rows * (2 if self.paired else 1)
+        block = self.some(per_pair << turn, columns)
+        at = 1 + 2 * turn + part
+        return remote(block, block, self.send.at[self.at, at], self.recv.at[self.at, at], self.place.mate())
+
+    def across(self):
+        place = self.place
+        size = self.columns - self.in_plane
+        columns = pl.ds(pl.multiple_of(place.plane * self.in_plane, 128), size)
+        at = 1 + 2 * self.dims.bits
+        for pair in self.subset(range(self.dims.bits))[1:]:
+            starts, count = self.blocks(pair)
+            for start in starts:
+                block = self.whole.at[self.layer, pl.ds(pl.multiple_of(start, 16), count), columns]
+                remote(block, block, self.send.at[self.at, at], self.recv.at[self.at, at], place.over_plane()).start()
+
+    def across_bytes(self):
+        per_pair = self.rows * (2 if self.paired else 1)
+        block = self.some(per_pair * (self.dims.pairs - 1), pl.ds(0, self.columns - self.in_plane))
+        at = 1 + 2 * self.dims.bits
+        return remote(block, block, self.send.at[self.at, at], self.recv.at[self.at, at], self.place.over_plane())
+
+    def own_bytes(self):
+        if not self.paired:
+            return None
+        block = self.some(self.rows, pl.ds(0, self.columns))
+        return remote(block, block, self.send.at[self.at, 0], self.recv.at[self.at, 0], self.place.mate())
+
+    def advance(self):
+        if self.stage == 0:
+            own = self.some(self.rows, pl.ds(0, self.columns))
+            pltpu.make_async_copy(own, own, self.local.at[self.at]).wait()
+            if self.paired:
+                self.own_bytes().wait_recv()
+        elif self.stage <= self.dims.bits:
+            for part in range(2):
+                self.phase_bytes(self.stage - 1, part).wait_recv()
+        else:
+            self.across_bytes().wait_recv()
+        if self.stage < self.dims.bits:
+            self.phase(self.stage)
+        elif self.stage + 1 < self.stages:
+            self.across()
+        self.stage += 1
+
+    def reach(self, stage):
+        while self.stage < min(stage, self.stages):
+            self.advance()
+
+    def finish_sends(self):
+        if self.paired:
+            self.own_bytes().wait_send()
+        for turn in range(self.dims.bits):
+            for part in range(2):
+                self.phase_bytes(turn, part).wait_send()
+        if self.in_plane < self.columns:
+            self.across_bytes().wait_send()
+
+
+def in_plane_columns(dims, layer, kind):
+    columns = dims.kinds[kind][2]
+    if dims.reps % 2:
+        return columns
+    blocks = columns // 128
+    return {12: 8, 8: 6, 16: 10}.get(blocks, blocks - blocks // 3) * 128
+
+
+def gelu_and_slope(pre):
+    cdf = 0.5 * (1.0 + lax.erf(pre * (1.0 / math.sqrt(2.0))))
+    slope = cdf + pre * jnp.exp(-0.5 * pre * pre) * (1.0 / math.sqrt(2.0 * math.pi))
+    return pre * cdf, slope
+
+
+def dot_last(left, right):
+    return lax.dot_general(left, right, (((1,), (1,)), ((), ())), preferred_element_type=wide)
+
+
+def dot_first(left, right):
+    return lax.dot_general(left, right, (((0,), (0,)), ((), ())), preferred_element_type=wide)
+
+
+def tiles(count, body):
+    def step(j, carry):
+        body(j)
+        return carry
+
+    lax.fori_loop(0, count, step, 0)
+
+
+def forward_kernel(
+    dims,
+    x_ref,
+    seg_row,
+    seg_col,
+    small,
+    src_qkv,
+    src_out,
+    src_up,
+    src_down,
+    output,
+    tops,
+    out_qkv_w,
+    out_out_w,
+    out_up_w,
+    out_down_w,
+    out_hidden,
+    out_qkv,
+    out_attended,
+    out_probs,
+    out_norm1,
+    out_first,
+    out_act,
+    out_slope,
+    out_norm2,
+    out_rstd,
+    w_qkv,
+    w_out,
+    w_up,
+    w_down,
+    both_hidden,
+    qkv,
+    attended,
+    probs,
+    norm1,
+    both_first,
+    act,
+    slope,
+    norm2,
+    rstd,
+    hidden,
+    first,
+    total,
+    away,
+    back,
+    bias,
+    seg_rows,
+    seg_cols,
+    gather_local,
+    gather_send,
+    gather_recv,
+    mate_send,
+    mate_recv,
+    save_sem,
+):
+    place = Place(dims)
+    tokens, width = dims.tokens, dims.width
+    heads_row = 128 // dims.head_dim
+    scale = 1.0 / math.sqrt(dims.head_dim)
+
+    barrier = pltpu.get_barrier_semaphore()
+    others = [place.mate()] + [place.over_bit(bit) for bit in range(dims.bits)]
+    if dims.reps % 2 == 0:
+        others.append(place.over_plane())
+    for other in others:
+        pl.semaphore_signal(barrier, 1, device_id=other, device_id_type=MESH)
+    pl.semaphore_wait(barrier, len(others))
+
+    sources = (src_qkv, src_out, src_up, src_down)
+    wholes = (w_qkv, w_out, w_up, w_down)
+    gathers = [
+        Gather(
+            place,
+            layer,
+            kind,
+            sources[kind],
+            wholes[kind],
+            (gather_local, gather_send, gather_recv),
+            in_plane_columns(dims, layer, kind),
+        )
+        for layer in range(dims.layers)
+        for kind in range(4)
+    ]
+
+    exchanges = []
+
+    def to_mate(src, dst):
+        at = len(exchanges)
+        copy = remote(src, dst, mate_send.at[at], mate_recv.at[at], place.mate())
+        copy.start()
+        exchanges.append(copy)
+        return copy
+
+    rows_copy = to_mate(seg_row, seg_rows)
+    cols_copy = to_mate(seg_col, seg_cols)
+    both_hidden[0, pl.ds(0, tokens)] = x_ref[...]
+    hidden_copy = to_mate(both_hidden.at[0, pl.ds(0, tokens)], both_hidden.at[0, pl.ds(tokens, tokens)])
+    for gather in gathers:
+        gather.begin()
+    for gather in gathers[:3]:
+        gather.reach(1)
+
+    def prepare(at):
+        for ahead in reversed(range(1, dims.bits + 2)):
+            if at + ahead < len(gathers):
+                gathers[at + ahead].reach(max(1, gathers[at + ahead].stages - ahead))
+        gathers[at].reach(gathers[at].stages)
+
+    saves = []
+
+    def save(src, dst):
+        copy = pltpu.make_async_copy(src, dst, save_sem.at[len(saves)])
+        copy.start()
+        saves.append(copy)
+
+    hidden[...] = x_ref[...].astype(wide)
+    tops[...] = jnp.full(tops.shape, neg_large, wide)
+    rows_copy.wait_recv()
+    cols_copy.wait_recv()
+    for s, (row_ref, col_ref) in enumerate(((seg_row, seg_col), (seg_rows, seg_cols))):
+        same = col_ref[:, 0:1] == row_ref[0:1, :]
+        bias[s] = jnp.where(same, 0.0, neg_large)
+
+    chunk = 32 if tokens % 32 == 0 else tokens
+
+    def layer_norm(residual, partial, other, bias_row, gain_row, shift_row, normed, rstd_out, results):
+        def body(j):
+            rows = pl.ds(pl.multiple_of(j * chunk, chunk), chunk)
+            value = residual[rows] + partial[rows] + other[rows].astype(wide) + bias_row
+            centred = value - jnp.mean(value, axis=-1, keepdims=True)
+            scale_row = lax.rsqrt(jnp.mean(centred * centred, axis=-1, keepdims=True) + epsilon)
+            normal = centred * scale_row
+            normed[rows] = normal
+            rstd_out[rows] = jnp.broadcast_to(scale_row, (chunk, 128))
+            results(rows, normal * gain_row + shift_row)
+
+        tiles(tokens // chunk, body)
+
+    def project(left, right, at, tile):
+        columns = dims.width
+
+        def far(j):
+            cols = pl.ds(pl.multiple_of(j * tile, tile), tile)
+            away[at % 2, :, cols] = jnp.dot(
+                left[pl.ds(tokens, tokens)], right[:, cols], preferred_element_type=wide
+            ).astype(low)
+
+        def near(j):
+            cols = pl.ds(pl.multiple_of(j * tile, tile), tile)
+            total[:, cols] = jnp.dot(left[pl.ds(0, tokens)], right[:, cols], preferred_element_type=wide)
+
+        tiles(columns // tile, far)
+        copy = to_mate(away.at[at % 2], back.at[at])
+        tiles(columns // tile, near)
+        return copy
+
+    tile = min(512, width)
+    waits = []
+    for layer in range(dims.layers):
+        prepare(4 * layer)
+        hidden_copy.wait_recv()
+
+        def qkv_tile(j, layer=layer):
+            cols = pl.ds(pl.multiple_of(j * tile, tile), tile)
+            value = jnp.dot(both_hidden[layer], w_qkv[layer, :, cols], preferred_element_type=wide)
+            qkv[layer, :, cols] = (value + small[layer, 0:1, cols]).astype(low)
+
+        tiles(dims.kinds[0][2] // tile, qkv_tile)
+        lane_blocks = dims.third // 128
+
+        def attend(j, layer=layer):
+            s, block = j // lane_blocks, j % lane_blocks
+            rows = pl.ds(pl.multiple_of(s * tokens, tokens), tokens)
+
+            def lanes(which):
+                start = pl.multiple_of(which * dims.third + block * 128, 128)
+                return qkv[layer, rows, pl.ds(start, 128)]
+
+            query, key_rows, value_rows = lanes(0), lanes(1), lanes(2)
+            mask = bias[s]
+            outs = []
+            for e in range(heads_row):
+                part = slice(e * dims.head_dim, (e + 1) * dims.head_dim)
+                scores = dot_last(query[:, part], key_rows[:, part]) * scale + mask
+                top = jnp.max(scores, axis=1, keepdims=True)
+                expo = jnp.exp(scores - top)
+                prob = (expo * (1.0 / jnp.sum(expo, axis=1, keepdims=True))).astype(low)
+                head = block * heads_row + e
+                probs[layer, s * (lane_blocks * heads_row) + head] = prob
+                outs.append(jnp.dot(prob, value_rows[:, part], preferred_element_type=wide))
+                peak = jnp.broadcast_to(jnp.max(top, axis=0, keepdims=True), (1, 128))
+                tops[layer, pl.ds(head, 1)] = jnp.maximum(tops[layer, pl.ds(head, 1)], peak)
+            attended[layer, rows, pl.ds(pl.multiple_of(block * 128, 128), 128)] = jnp.concatenate(
+                outs, axis=1
+            ).astype(low)
+
+        tiles(2 * lane_blocks, attend)
+
+        prepare(4 * layer + 1)
+        if layer > 0:
+            waits[2 * layer - 2].wait_send()
+        copy = project(attended.at[layer], w_out.at[layer], 2 * layer, tile)
+        waits.append(copy)
+        copy.wait_recv()
+
+        def first_rows(rows, value, layer=layer):
+            first[rows] = value
+            both_first[layer, rows] = value.astype(low)
+
+        layer_norm(
+            hidden,
+            total,
+            back.at[2 * layer],
+            small[layer, 1:2, :width],
+            small[layer, 4:5, :width],
+            small[layer, 5:6, :width],
+            norm1.at[layer],
+            rstd.at[layer, 0],
+            first_rows,
+        )
+        first_copy = to_mate(
+            both_first.at[layer, pl.ds(0, tokens)], both_first.at[layer, pl.ds(tokens, tokens)]
+        )
+
+        prepare(4 * layer + 2)
+        first_copy.wait_recv()
+        narrow = 256
+
+        def up_tile(j, layer=layer):
+            cols = pl.ds(pl.multiple_of(j * narrow, narrow), narrow)
+            pre = jnp.dot(both_first[layer], w_up[layer, :, cols], preferred_element_type=wide)
+            value, steep = gelu_and_slope(pre + small[layer, 2:3, cols])
+            act[layer, :, cols] = value.astype(low)
+            slope[layer, :, cols] = steep.astype(low)
+
+        tiles(dims.kinds[2][2] // narrow, up_tile)
+
+        prepare(4 * layer + 3)
+        if layer > 0:
+            waits[2 * layer - 1].wait_send()
+        copy = project(act.at[layer], w_down.at[layer], 2 * layer + 1, tile)
+        waits.append(copy)
+        copy.wait_recv()
+        last = layer == dims.layers - 1
+
+        def second_rows(rows, value, layer=layer, last=last):
+            if last:
+                output[rows] = value.astype(low)
+            else:
+                hidden[rows] = value
+                both_hidden[layer + 1, rows] = value.astype(low)
+
+        layer_norm(
+            first,
+            total,
+            back.at[2 * layer + 1],
+            small[layer, 3:4, :width],
+            small[layer, 6:7, :width],
+            small[layer, 7:8, :width],
+            norm2.at[layer],
+            rstd.at[layer, 1],
+            second_rows,
+        )
+        if not last:
+            hidden_copy = to_mate(
+                both_hidden.at[layer + 1, pl.ds(0, tokens)],
+                both_hidden.at[layer + 1, pl.ds(tokens, tokens)],
+            )
+        for src, dst in (
+            (both_hidden, out_hidden),
+            (qkv, out_qkv),
+            (attended, out_attended),
+            (probs, out_probs),
+            (norm1, out_norm1),
+            (both_first, out_first),
+            (act, out_act),
+            (slope, out_slope),
+            (norm2, out_norm2),
+            (rstd, out_rstd),
+            (w_qkv, out_qkv_w),
+            (w_out, out_out_w),
+            (w_up, out_up_w),
+            (w_down, out_down_w),
+        ):
+            save(src.at[layer], dst.at[layer])
+
+    for copy in exchanges:
+        if not any(copy is other for other in waits[: 2 * dims.layers - 2]):
+            copy.wait_send()
+    for gather in gathers:
+        gather.finish_sends()
+    for copy in saves:
+        copy.wait()
+
+
+def run_forward(dims, x, segments, small, weights):
+    layers, tokens, width = dims.layers, dims.tokens, dims.width
+    both = 2 * tokens
+    held = [
+        jax.ShapeDtypeStruct((layers, rows, columns), low) for _, rows, columns, _ in dims.kinds
+    ]
+    states = [
+        ((layers, both, width), low),
+        ((layers, both, 3 * dims.third), low),
+        ((layers, both, dims.third), low),
+        ((layers, HEADS, tokens, tokens), low),
+        ((layers, tokens, width), wide),
+        ((layers, both, width), low),
+        ((layers, both, dims.hidden // 2), low),
+        ((layers, both, dims.hidden // 2), low),
+        ((layers, tokens, width), wide),
+        ((layers, 2, tokens, 128), wide),
+    ]
+    saved = held + [jax.ShapeDtypeStruct(shape, dtype) for shape, dtype in states]
+    seg = segments.astype(wide)
+    seg_row = jnp.broadcast_to(seg, (8, tokens))
+    seg_col = jnp.broadcast_to(seg.reshape(tokens, 1), (tokens, 128))
+    vmem = pl.BlockSpec(memory_space=pltpu.VMEM)
+    anywhere = pl.BlockSpec(memory_space=pl.ANY)
+    outs = [
+        jax.ShapeDtypeStruct((tokens, width), low),
+        jax.ShapeDtypeStruct((layers, HEADS // 2, 128), wide),
+    ] + saved
+    dma = pltpu.SemaphoreType.DMA
+    slots = 2 + 2 * dims.bits
+    exchange_count = 3 + 4 * layers
+    scratch = (
+        [pltpu.VMEM(item.shape, item.dtype) for item in saved]
+        + [
+            pltpu.VMEM((tokens, width), wide),
+            pltpu.VMEM((tokens, width), wide),
+            pltpu.VMEM((tokens, width), wide),
+            pltpu.VMEM((2, tokens, width), low),
+            pltpu.VMEM((2 * layers, tokens, width), low),
+            pltpu.VMEM((2, tokens, tokens), wide),
+            pltpu.VMEM((8, tokens), wide),
+            pltpu.VMEM((tokens, 128), wide),
+        ]
+        + [
+            dma((4 * layers,)),
+            dma((4 * layers, slots)),
+            dma((4 * layers, slots)),
+            dma((exchange_count,)),
+            dma((exchange_count,)),
+            dma((len(saved) * layers,)),
+        ]
+    )
+    return pl.pallas_call(
+        functools.partial(forward_kernel, dims),
+        out_shape=outs,
+        in_specs=[vmem] * 4 + [anywhere] * 4,
+        out_specs=[vmem] * 2 + [anywhere] * len(saved),
+        scratch_shapes=scratch,
+        compiler_params=pltpu.CompilerParams(
+            collective_id=0, has_side_effects=True, vmem_limit_bytes=63 * 2**20
+        ),
+        name="forward",
+    )(x, seg_row, seg_col, small, *weights)
 
 
 def matmul_rows(left, right):
@@ -237,22 +751,11 @@
     return jnp.einsum("to,io->ti", left, right, preferred_element_type=wide)
 
 
-def backward_layer(net, grad_out, weights, small, same, saved):
+def backward_layer(net, grad_out, weights, small, saved):
     w_qkv, w_out, w_up, w_down = weights
-    bias_qkv, bias_out, bias_up, bias_down, gain_first, shift_first, gain_second, shift_second = small
-    (
-        both_hidden,
-        qkv,
-        log_total,
-        attended,
-        normed_one,
-        rstd_one,
-        both_first,
-        pre,
-        activation,
-        normed_two,
-        rstd_two,
-    ) = saved
+    gain_first, gain_second = small[4, : grad_out.shape[1]], small[6, : grad_out.shape[1]]
+    both_hidden, qkv, attended, probs, normed_one, both_first, activation, slope, normed_two, rstd = saved
+    rstd_one, rstd_two = rstd[0, :, :1], rstd[1, :, :1]
     heads = HEADS // 2
     third = w_qkv.shape[1] // 3
     scale = 1.0 / math.sqrt(third // heads)
@@ -263,7 +766,7 @@
     grad_bias_down = column_sums(branch_two)
     both_two = net.pair(branch_two)
     grad_w_down = matmul_rows(activation, both_two)
-    branch_pre = (matmul_back(both_two, w_down) * gelu_slope(pre)).astype(low)
+    branch_pre = (matmul_back(both_two, w_down) * slope.astype(wide)).astype(low)
     grad_bias_up = column_sums(branch_pre)
     grad_w_up = matmul_rows(both_first, branch_pre)
     grad_first = grad_sum_two + net.join(matmul_back(branch_pre, w_up))
@@ -278,8 +781,7 @@
     query = split_heads(qkv[:, :third], heads)
     key_rows = split_heads(qkv[:, third : 2 * third], heads)
     value_rows = split_heads(qkv[:, 2 * third :], heads)
-    masked = masked_scores(query, key_rows, same)
-    probs = jnp.exp(masked - log_total)
+    probs = probs.reshape((2, heads) + probs.shape[1:]).astype(wide)
     grad_value = jnp.einsum(
         "shqk,sqhd->skhd", probs.astype(low), grad_attended, preferred_element_type=wide
     )
@@ -389,33 +891,26 @@
             of_core(layer_index, 3),
         ) + tuple(whole(layer_index, member).reshape(-1) for member in (4, 5, 6, 7, 8))
 
-    both_segments = jnp.concatenate([segments, net.over_core(segments)], axis=0)
-    same = both_segments[:, :, None] == both_segments[:, None, :]
-
-    hidden = inputs.astype(wide)
-    saved_all, weights_all, small_all, tops = [], [], [], []
-    for layer_index in range(layer_count):
-        pieces = (
-            swap_columns(w_qkv[layer_index], net, 3),
-            w_out[layer_index],
-            swap_columns(w_up[layer_index], net, 1),
-            w_down[layer_index],
-        )
-        weights = []
-        for piece, paired in zip(pieces, (True, False, True, False)):
-            full = gather_weight(net, piece)
-            if paired:
-                full = net.rows_in_order(full.reshape(net.pairs, 2, -1, full.shape[2]))
-            weights.append(full.reshape(-1, full.shape[2]))
-        small = small_of(layer_index)
-        hidden, head_top, saved = forward_layer(net, hidden, weights, small, same)
-        saved_all.append(saved)
-        weights_all.append(weights)
-        small_all.append(small)
-        tops.append(head_top)
-    output = hidden.astype(low)
-
-    local = jnp.stack(tops)
+    tokens = inputs.shape[0]
+    dims = Dims(shard_count, rep_count, net.step, layer_count, tokens, width, w_up.shape[2])
+
+    def wide_row(row):
+        return jnp.pad(row, (0, dims.hidden // 2 - row.shape[0]))
+
+    small = jnp.stack(
+        [jnp.stack([wide_row(row) for row in small_of(layer)]) for layer in range(layer_count)]
+    )
+    results = run_forward(
+        dims,
+        inputs,
+        segments,
+        small,
+        (by_half(w_qkv, net, 3), w_out, by_half(w_up, net, 1), w_down),
+    )
+    output, tops = results[0], results[1]
+    weights_all, saved_all = results[2:6], results[6:]
+
+    local = tops[:, :, 0]
     local = net.in_order(local, net.over_core(local), net.core)
     local = local.reshape(2, layer_count, net.high, -1).transpose(1, 2, 0, 3).reshape(layer_count, HEADS)
     for bit in range(net.bits):
@@ -435,10 +930,9 @@
         grad_flow, owned, terms = backward_layer(
             net,
             grad_flow,
-            weights_all[layer_index],
-            small_all[layer_index],
-            same,
-            saved_all[layer_index],
+            [weight[layer_index] for weight in weights_all],
+            small[layer_index],
+            [state[layer_index] for state in saved_all],
         )
         owned_all[layer_index] = owned
         terms_all[layer_index] = terms

time: 874 us -> 888 us (1.016)
  Pallas kernels: 0 us -> 223 us
  other arithmetic: 142 us -> 78.4 us
  matrix products: 100 us -> 55.7 us
  waiting for transfers between devices: 264 us -> 220 us
  starting transfers between devices: 194 us -> 152 us
  local copies, waits for them, and re-layouts: 158 us -> 142 us
    pallas_call x0 -> x1, Pallas kernels: none -> 223 us  [run_forward(): pl.pallas_call(functools.partial(forward_kernel, dims), out_shape=outs, i...]
    ppermute x70 -> x38, waiting for transfers between devices: 164 us -> 61.7 us  [over_bit(): lax.ppermute(value, 'shard', [(i, i ^ step) for i in range(self.shards)])]
    ppermute x17, waiting for transfers between devices: 80.3 us -> 135 us  [sum_reps(): got = lax.ppermute(total, 'rep', [(i + 1, i), (reps - 2 - i, reps - 1 - i)])]
    dot_general x12 -> x0, matrix products: 44.4 us -> none  [the longest x2 26.5 us: forward_layer(): pre = jnp.dot(both_first, w_up, preferred_element_type=wide) + bias_up]
    another operation x58 -> x6, other arithmetic: 40.3 us -> 0.24 us  [in_order(): jnp.stack([jnp.where(first, mine, other), jnp.where(first, other, mine)])]
    ppermute x70 -> x38, starting transfers between devices: 70.8 us -> 42.2 us  [over_bit(): lax.ppermute(value, 'shard', [(i, i ^ step) for i in range(self.shards)])]
    ppermute x17, starting transfers between devices: 79.4 us -> 69.1 us  [sum_reps(): got = lax.ppermute(total, 'rep', [(i, i + 1), (reps - 1 - i, reps - 2 - i)])]
    reshape x16 -> x10, local copies, waits for them, and re-layouts: 30.7 us -> 21 us  [split_heads(): return rows.reshape(2, rows.shape[0] // 2, heads, rows.shape[1] // heads)]
  transfers between devices with their start and end apart: 151 -> 106, of which waited for: 53 -> 32; matrix products, arithmetic and copies ran while one was open for 41% -> 28% of each run, Pallas kernels for 0% -> 0%
where the time goes in v2:
time: 888 us; the launch traced here: 876 us
  Pallas kernels  223 us (25%)
  waiting for transfers between devices  220 us (25%)
  starting transfers between devices  152 us (17%)
  local copies, waits for them, and re-layouts  142 us (16%)
  other arithmetic  78.4 us (9%)
  matrix products  55.7 us (6%)
    pallas_call x1, Pallas kernels, run_forward(): pl.pallas_call(functools.partial(forward_kernel, dims), out_shape=outs, i...  223 us
    ppermute x17, waiting for transfers between devices, sum_reps(): got = lax.ppermute(total, 'rep', [(i + 1, i), (reps - 2 - i, reps - 1 - i)])  135 us
    ppermute x17, starting transfers between devices, sum_reps(): got = lax.ppermute(total, 'rep', [(i, i + 1), (reps - 1 - i, reps - 2 - i)])  69.1 us
    ppermute x38, waiting for transfers between devices, over_bit(): lax.ppermute(value, 'shard', [(i, i ^ step) for i in range(self.shards)])  61.7 us
    ppermute x38, starting transfers between devices, over_bit(): lax.ppermute(value, 'shard', [(i, i ^ step) for i in range(self.shards)])  42.2 us
    convert_element_type x32, other arithmetic, scatter_chips(): value = (ours.astype(wide) + got.astype(wide)).astype(value.dtype)  29.2 us
    unnamed x276, local copies, waits for them, and re-layouts  28.1 us
    dot_general x8, matrix products, matmul_back(): return jnp.einsum('to,io->ti', left, right, preferred_element_type=wide)  28.1 us
  transfers between devices with their start and end apart: 106, of which 32 were waited for; matrix products, arithmetic and copies ran while one was open for 28% of the time, Pallas kernels for 0%

profile of v2, /device:TPU:0, one launch (start us, length us, event | category | flops | bytes accessed | tf_op | source)
XLA Modules:
  0.0 876.0 jit_solution(11558536907965482890)
XLA Ops:
  8.0 2.9 collective-permute-start.1
  15.4 4.5 reshape.1057
  19.9 2.4 copy.356
  22.3 2.8 reshape.1058.src_up
  31.7 222.9 %forward.1 = (bf16[256,1024]{1,0:T(8,128)(2,1)}, f32[2,8,128]{2,1,0:T(8,128)}, bf16[2,1024,1536]{2,1,0:T(8,128)(2,1)}, bf16[2,512,1024]{2,1,0:T(8,128)(2,1)}, bf...) custom-call(bf16[256,1024]{1,0:T(8,128)(2,1)} %x_ref.1, ...), custom_call_target="tpu_custom_call" | custom-call | tf_op jit(solution)/shard_map/forward/pallas_call | solution.py:733
  260.1 4.7 fusion.159
  264.8 3.9 copy.213
  268.7 3.2 slice_bitcast_fusion
  272.9 2.6 reshape.1181
  281.0 3.9 copy.228
  286.4 2.4 reshape.1184
  296.0 2.6 collective-permute-start.105
  301.3 3.0 convert_multiply_fusion.6
  304.2 5.7 convert_reduce_fusion
  310.0 2.4 fusion.10
  312.5 3.6 convolution_convert_fusion
  320.7 2.4 convolution_convert_fusion.2
  324.4 10.7 %fusion.158 = (bf16[4,256,1024]{2,1,0:T(8,128)(2,1)S(1)}, bf16[4,256,1024]{2,1,0:T(8,128)(2,1)S(1)}) fusion(bf16[4,256,2048]{2,1,0:T(8,128)(2,1)S(1)} %bitcast.650), kind=kLoop, calls=%fused_computation.485 | loop fusion | bytes 8388608 | tf_op jit(solution)/shard_map/slice | solution.py:130
  341.6 2.4 reshape.1186
  344.0 2.5 copy.216
  346.5 2.5 convert_reduce_fusion.5
  355.3 3.2 fusion.20
  375.7 8.9 %collective-permute-done.43 = bf16[2,128,512]{2,1,0:T(8,128)(2,1)S(1)} collective-permute-done((bf16[2,128,512]{2,1,0:T(8,128)(2,1)S(1)}, bf16[2,128,512]{2,1,0:T(8,128)(2,1)S(1)}, u32[]{:S(2)}, u32[]{:S(2)}) %collective-permute-start.43) | collective-permute-done | bytes 262176 | tf_op jit(solution)/shard_map/ppermute | solution.py:56
  385.6 10.2 %collective-permute-done.48 = bf16[2,128,512]{2,1,0:T(8,128)(2,1)S(1)} collective-permute-done((bf16[2,128,512]{2,1,0:T(8,128)(2,1)S(1)}, bf16[2,128,512]{2,1,0:T(8,128)(2,1)S(1)}, u32[]{:S(2)}, u32[]{:S(2)}) %collective-permute-start.48) | collective-permute-done | bytes 262176 | tf_op jit(solution)/shard_map/ppermute | solution.py:56
  396.9 3.9 collective-permute-done.44
  401.8 4.3 collective-permute-done.49
  409.5 3.0 collective-permute-start.45
  415.7 5.2 collective-permute-done.70
  421.2 2.8 collective-permute-start.87
  425.5 15.4 %collective-permute-start.92 = (bf16[512,512]{1,0:T(8,128)(2,1)S(1)}, bf16[512,512]{1,0:T(8,128)(2,1)S(1)}, u32[]{:S(2)}, u32[]{:S(2)}) collective-permute-start(bf16[512,512]{1,0:T(8,128)(2,1)S(1)} %fusion.65), channel_id=1, source_target_pairs={{0,8},{24,16},{1,9},{25,17},{2,10},{26,18},{3,11},{27,19},{4,12},{... | collective-permute-start | bytes 1572872 | tf_op jit(solution)/shard_map/ppermute | solution.py:106
  444.4 5.3 collective-permute-done.47
  451.6 4.9 collective-permute-done.52
  459.6 6.6 convert_reduce_fusion.1
  466.3 4.0 fusion.6
  470.3 4.0 convolution_convert_fusion.1
  479.7 2.4 convolution_convert_fusion.3
  492.0 6.0 collective-permute-done.24
  498.7 4.8 collective-permute-done.29
  519.3 2.5 reshape.1187
  521.8 2.5 copy.231
  546.4 59.9 %collective-permute-done.68 = bf16[256,1024]{1,0:T(8,128)(2,1)S(1)} collective-permute-done((bf16[256,1024]{1,0:T(8,128)(2,1)S(1)}, bf16[256,1024]{1,0:T(8,128)(2,1)S(1)}, u32[]{:S(2)}, u32[]{:S(2)}) %collective-permute-start.68) | collective-permute-done | bytes 524320 | tf_op jit(solution)/shard_map/ppermute | solution.py:110
  608.4 9.9 %collective-permute-done.73 = bf16[256,1024]{1,0:T(8,128)(2,1)S(1)} collective-permute-done((bf16[256,1024]{1,0:T(8,128)(2,1)S(1)}, bf16[256,1024]{1,0:T(8,128)(2,1)S(1)}, u32[]{:S(2)}, u32[]{:S(2)}) %collective-permute-start.73) | collective-permute-done | bytes 524320 | tf_op jit(solution)/shard_map/ppermute | solution.py:110
  632.1 3.2 fusion.18
  641.0 9.0 %collective-permute-done.96 = f32[2,2,12,128]{3,1,2,0:T(2,128)S(1)} collective-permute-done((f32[2,2,12,128]{3,1,2,0:T(2,128)S(1)}, f32[2,2,12,128]{3,1,2,0:T(2,128)S(1)}, u32[]{:S(2)}, u32[]{:S(2)}) %collective-permute-start.96) | collective-permute-done | bytes 24608 | tf_op jit(solution)/shard_map/ppermute | solution.py:56
  653.9 6.0 collective-permute-start.98
  668.9 3.3 collective-permute-done.100
  678.4 6.6 collective-permute-done.33
  688.4 4.6 collective-permute-done.38
  700.9 3.0 collective-permute-done.39
  720.0 4.1 collective-permute-start.35
  728.1 4.4 collective-permute-start.77
  732.5 2.7 collective-permute-start.82
  742.0 9.1 %collective-permute-start.55 = (bf16[256,1024]{1,0:T(8,128)(2,1)S(1)}, bf16[256,1024]{1,0:T(8,128)(2,1)S(1)}, u32[]{:S(2)}, u32[]{:S(2)}) collective-permute-start(bf16[256,1024]{1,0:T(8,128)(2,1)S(1)} %copy-done.45), channel_id=1, source_target_pairs={{0,8},{24,16},{1,9},{25,17},{2,10},{26,18},{3,11},{27,19},{4,12},{... | collective-permute-start | bytes 1572872 | tf_op jit(solution)/shard_map/ppermute | solution.py:106
  756.7 4.1 collective-permute-done.37
  762.1 5.5 collective-permute-done.42
  778.1 9.4 %collective-permute-start.13 = (bf16[256,768]{1,0:T(8,128)(2,1)S(1)}, bf16[256,768]{1,0:T(8,128)(2,1)S(1)}, u32[]{:S(2)}, u32[]{:S(2)}) collective-permute-start(bf16[256,768]{1,0:T(8,128)(2,1)S(1)} %fusion.108), channel_id=1, source_target_pairs={{0,8},{24,16},{1,9},{25,17},{2,10},{26,18},{3,11},{27,19},{4,12},{... | collective-permute-start | bytes 1179656 | tf_op jit(solution)/shard_map/ppermute | solution.py:106
  787.7 2.8 collective-permute-start.18
  793.6 3.5 collective-permute-done.13
  798.5 3.4 collective-permute-done.18
  807.1 29.2 %collective-permute-done.57 = bf16[256,1024]{1,0:T(8,128)(2,1)S(1)} collective-permute-done((bf16[256,1024]{1,0:T(8,128)(2,1)S(1)}, bf16[256,1024]{1,0:T(8,128)(2,1)S(1)}, u32[]{:S(2)}, u32[]{:S(2)}) %collective-permute-start.57) | collective-permute-done | bytes 524320 | tf_op jit(solution)/shard_map/ppermute | solution.py:110
  837.6 9.9 %collective-permute-done.62 = bf16[256,1024]{1,0:T(8,128)(2,1)S(1)} collective-permute-done((bf16[256,1024]{1,0:T(8,128)(2,1)S(1)}, bf16[256,1024]{1,0:T(8,128)(2,1)S(1)}, u32[]{:S(2)}, u32[]{:S(2)}) %collective-permute-start.62) | collective-permute-done | bytes 524320 | tf_op jit(solution)/shard_map/ppermute | solution.py:110
  851.1 2.6 maximum_convert_fusion.1
  854.7 3.0 collective-permute-done.20
  864.2 5.6 copy.274
  (753 shorter events, 272.7 us)
Async XLA Ops:
  12.6 16.1 %collective-permute-start.2 = (bf16[2,2,2,12,128]{4,2,3,1,0:T(2,128)(2,1)S(1)}, bf16[2,2,2,12,128]{4,2,3,1,0:T(2,128)(2,1)S(1)}, u32[]{:S(2)}, u32[]{:S(2)}) collective-permute-start(bf16[2,2,2,12,128]{4,2,3,1,0:T(2,128)(2,1)S(1)} %pad_maximum_fusion.22), channel_id=1, source_target_pairs={{0,4},{1,5},{2,6},{3,7},{4,0},{5,1},{6,2},{7,3},{8,12},{9,13},{10,... | collective-permute-start | bytes 73736 | tf_op jit(solution)/shard_map/ppermute | solution.py:56
  255.6 29.3 %collective-permute-start.101 = (f32[2,8]{1,0:T(2,128)S(1)}, f32[2,8]{1,0:T(2,128)S(1)}, u32[]{:S(2)}, u32[]{:S(2)}) collective-permute-start(f32[2,8]{1,0:T(2,128)S(1)} %slice_reduce_fusion.4), channel_id=1, source_target_pairs={{0,1},{1,0},{2,3},{3,2},{4,5},{5,4},{6,7},{7,6},{8,9},{9,8},{10,11... | collective-permute-start | bytes 200 | tf_op jit(solution)/shard_map/ppermute | solution.py:49
  260.1 44.1 %collective-permute-start.3 = (bf16[256,1024]{1,0:T(8,128)(2,1)}, bf16[256,1024]{1,0:T(8,128)(2,1)}, u32[]{:S(2)}, u32[]{:S(2)}) collective-permute-start(bf16[256,1024]{1,0:T(8,128)(2,1)} %get-tuple-element.104), channel_id=1, source_target_pairs={{0,1},{1,0},{2,3},{3,2},{4,5},{5,4},{6,7},{7,6},{8,9},{9,8},{10,11... | collective-permute-start | bytes 1572872 | tf_op jit(solution)/shard_map/ppermute | solution.py:49
  317.6 42.6 %collective-permute-start.85 = (bf16[2,512,512]{2,1,0:T(8,128)(2,1)}, bf16[2,512,512]{2,1,0:T(8,128)(2,1)}, u32[]{:S(2)}, u32[]{:S(2)}) collective-permute-start(bf16[2,512,512]{2,1,0:T(8,128)(2,1)} %dynamic-slice_bitcast_fusion.1), channel_id=1, source_target_pairs={{0,2},{1,3},{2,0},{3,1},{4,6},{5,7},{6,4},{7,5},{8,10},{9,11},{10,... | collective-permute-start | bytes 3145736 | tf_op jit(solution)/shard_map/ppermute | solution.py:56
  319.8 43.6 %collective-permute-start.90 = (bf16[2,512,512]{2,1,0:T(8,128)(2,1)}, bf16[2,512,512]{2,1,0:T(8,128)(2,1)}, u32[]{:S(2)}, u32[]{:S(2)}) collective-permute-start(bf16[2,512,512]{2,1,0:T(8,128)(2,1)} %dynamic-slice_bitcast_fusion), channel_id=1, source_target_pairs={{0,4},{1,5},{2,6},{3,7},{4,0},{5,1},{6,2},{7,3},{8,12},{9,13},{10,... | collective-permute-start | bytes 3145736 | tf_op jit(solution)/shard_map/ppermute | solution.py:56
  324.3 14.9 %collective-permute-start.5 = (bf16[256,1024]{1,0:T(8,128)(2,1)S(1)}, bf16[256,1024]{1,0:T(8,128)(2,1)S(1)}, u32[]{:S(2)}, u32[]{:S(2)}) collective-permute-start(bf16[256,1024]{1,0:T(8,128)(2,1)S(1)} %get-tuple-element.106), channel_id=1, source_target_pairs={{0,1},{1,0},{2,3},{3,2},{4,5},{5,4},{6,7},{7,6},{8,9},{9,8},{10,11... | collective-permute-start | bytes 1572872 | tf_op jit(solution)/shard_map/ppermute | solution.py:49
  336.1 29.8 %collective-permute-start.64 = (bf16[2,256,1024]{2,1,0:T(8,128)(2,1)}, bf16[2,256,1024]{2,1,0:T(8,128)(2,1)}, u32[]{:S(2)}, u32[]{:S(2)}) collective-permute-start(bf16[2,256,1024]{2,1,0:T(8,128)(2,1)} %dynamic-slice_bitcast_fusion.5), channel_id=1, source_target_pairs={{0,2},{1,3},{2,0},{3,1},{4,6},{5,7},{6,4},{7,5},{8,10},{9,11},{10,... | collective-permute-start | bytes 3145736 | tf_op jit(solution)/shard_map/ppermute | solution.py:56
  338.3 30.5 %collective-permute-start.69 = (bf16[2,256,1024]{2,1,0:T(8,128)(2,1)}, bf16[2,256,1024]{2,1,0:T(8,128)(2,1)}, u32[]{:S(2)}, u32[]{:S(2)}) collective-permute-start(bf16[2,256,1024]{2,1,0:T(8,128)(2,1)} %dynamic-slice_bitcast_fusion.4), channel_id=1, source_target_pairs={{0,4},{1,5},{2,6},{3,7},{4,0},{5,1},{6,2},{7,3},{8,12},{9,13},{10,... | collective-permute-start | bytes 3145736 | tf_op jit(solution)/shard_map/ppermute | solution.py:56
  360.1 52.7 %collective-permute-start.6 = (bf16[256,1024]{1,0:T(8,128)(2,1)S(1)}, bf16[256,1024]{1,0:T(8,128)(2,1)S(1)}, u32[]{:S(2)}, u32[]{:S(2)}) collective-permute-start(bf16[256,1024]{1,0:T(8,128)(2,1)S(1)} %slice.588), channel_id=1, source_target_pairs={{0,1},{1,0},{2,3},{3,2},{4,5},{5,4},{6,7},{7,6},{8,9},{9,8},{10,11... | collective-permute-start | bytes 1572872 | tf_op jit(solution)/shard_map/ppermute | solution.py:49
  362.2 44.8 %collective-permute-start.86 = (bf16[512,512]{1,0:T(8,128)(2,1)S(1)}, bf16[512,512]{1,0:T(8,128)(2,1)S(1)}, u32[]{:S(2)}, u32[]{:S(2)}) collective-permute-start(bf16[512,512]{1,0:T(8,128)(2,1)S(1)} %dynamic-slice_bitcast_fusion.13), channel_id=1, source_target_pairs={{0,4},{1,5},{2,6},{3,7},{4,0},{5,1},{6,2},{7,3},{8,12},{9,13},{10,... | collective-permute-start | bytes 1572872 | tf_op jit(solution)/shard_map/ppermute | solution.py:56
  365.0 43.4 %collective-permute-start.91 = (bf16[512,512]{1,0:T(8,128)(2,1)S(1)}, bf16[512,512]{1,0:T(8,128)(2,1)S(1)}, u32[]{:S(2)}, u32[]{:S(2)}) collective-permute-start(bf16[512,512]{1,0:T(8,128)(2,1)S(1)} %dynamic-slice_bitcast_fusion.12), channel_id=1, source_target_pairs={{0,2},{1,3},{2,0},{3,1},{4,6},{5,7},{6,4},{7,5},{8,10},{9,11},{10,... | collective-permute-start | bytes 1572872 | tf_op jit(solution)/shard_map/ppermute | solution.py:56
  367.7 41.8 %collective-permute-start.65 = (bf16[256,1024]{1,0:T(8,128)(2,1)S(1)}, bf16[256,1024]{1,0:T(8,128)(2,1)S(1)}, u32[]{:S(2)}, u32[]{:S(2)}) collective-permute-start(bf16[256,1024]{1,0:T(8,128)(2,1)S(1)} %dynamic-slice_bitcast_fusion.18), channel_id=1, source_target_pairs={{0,4},{1,5},{2,6},{3,7},{4,0},{5,1},{6,2},{7,3},{8,12},{9,13},{10,... | collective-permute-start | bytes 1572872 | tf_op jit(solution)/shard_map/ppermute | solution.py:56
  371.5 13.1 %collective-permute-start.43 = (bf16[2,128,512]{2,1,0:T(8,128)(2,1)S(1)}, bf16[2,128,512]{2,1,0:T(8,128)(2,1)S(1)}, u32[]{:S(2)}, u32[]{:S(2)}) collective-permute-start(bf16[2,128,512]{2,1,0:T(8,128)(2,1)S(1)} %dynamic-slice_bitcast_fusion.29), channel_id=1, source_target_pairs={{0,2},{1,3},{2,0},{3,1},{4,6},{5,7},{6,4},{7,5},{8,10},{9,11},{10,... | collective-permute-start | bytes 786440 | tf_op jit(solution)/shard_map/ppermute | solution.py:56
  384.6 11.3 %collective-permute-start.48 = (bf16[2,128,512]{2,1,0:T(8,128)(2,1)S(1)}, bf16[2,128,512]{2,1,0:T(8,128)(2,1)S(1)}, u32[]{:S(2)}, u32[]{:S(2)}) collective-permute-start(bf16[2,128,512]{2,1,0:T(8,128)(2,1)S(1)} %dynamic-slice_bitcast_fusion.28), channel_id=1, source_target_pairs={{0,4},{1,5},{2,6},{3,7},{4,0},{5,1},{6,2},{7,3},{8,12},{9,13},{10,... | collective-permute-start | bytes 786440 | tf_op jit(solution)/shard_map/ppermute | solution.py:56
  406.1 14.9 %collective-permute-start.70 = (bf16[256,1024]{1,0:T(8,128)(2,1)S(1)}, bf16[256,1024]{1,0:T(8,128)(2,1)S(1)}, u32[]{:S(2)}, u32[]{:S(2)}) collective-permute-start(bf16[256,1024]{1,0:T(8,128)(2,1)S(1)} %dynamic-slice_bitcast_fusion.17), channel_id=1, source_target_pairs={{0,2},{1,3},{2,0},{3,1},{4,6},{5,7},{6,4},{7,5},{8,10},{9,11},{10,... | collective-permute-start | bytes 1572872 | tf_op jit(solution)/shard_map/ppermute | solution.py:56
  407.1 33.9 %collective-permute-start.22 = (bf16[2,256,768]{2,1,0:T(8,128)(2,1)S(1)}, bf16[2,256,768]{2,1,0:T(8,128)(2,1)S(1)}, u32[]{:S(2)}, u32[]{:S(2)}) collective-permute-start(bf16[2,256,768]{2,1,0:T(8,128)(2,1)S(1)} %dynamic-slice_bitcast_fusion.9), channel_id=1, source_target_pairs={{0,2},{1,3},{2,0},{3,1},{4,6},{5,7},{6,4},{7,5},{8,10},{9,11},{10,... | collective-permute-start | bytes 2359304 | tf_op jit(solution)/shard_map/ppermute | solution.py:56
  408.4 34.1 %collective-permute-start.27 = (bf16[2,256,768]{2,1,0:T(8,128)(2,1)S(1)}, bf16[2,256,768]{2,1,0:T(8,128)(2,1)S(1)}, u32[]{:S(2)}, u32[]{:S(2)}) collective-permute-start(bf16[2,256,768]{2,1,0:T(8,128)(2,1)S(1)} %dynamic-slice_bitcast_fusion.8), channel_id=1, source_target_pairs={{0,4},{1,5},{2,6},{3,7},{4,0},{5,1},{6,2},{7,3},{8,12},{9,13},{10,... | collective-permute-start | bytes 2359304 | tf_op jit(solution)/shard_map/ppermute | solution.py:56
  409.5 11.6 %collective-permute-start.45 = (bf16[128,512]{1,0:T(8,128)(2,1)S(1)}, bf16[128,512]{1,0:T(8,128)(2,1)S(1)}, u32[]{:S(2)}, u32[]{:S(2)}) collective-permute-start(bf16[128,512]{1,0:T(8,128)(2,1)S(1)} %fusion.118), channel_id=1, source_target_pairs={{0,8},{24,16},{1,9},{25,17},{2,10},{26,18},{3,11},{27,19},{4,12},{... | collective-permute-start | bytes 393224 | tf_op jit(solution)/shard_map/ppermute | solution.py:106
  412.8 11.3 %collective-permute-start.50 = (bf16[128,512]{1,0:T(8,128)(2,1)S(1)}, bf16[128,512]{1,0:T(8,128)(2,1)S(1)}, u32[]{:S(2)}, u32[]{:S(2)}) collective-permute-start(bf16[128,512]{1,0:T(8,128)(2,1)S(1)} %fusion.117), channel_id=1, source_target_pairs={{0,8},{24,16},{1,9},{25,17},{2,10},{26,18},{3,11},{27,19},{4,12},{... | collective-permute-start | bytes 393224 | tf_op jit(solution)/shard_map/ppermute | solution.py:106
  420.9 37.8 %collective-permute-start.7 = (bf16[256,1024]{1,0:T(8,128)(2,1)S(1)}, bf16[256,1024]{1,0:T(8,128)(2,1)S(1)}, u32[]{:S(2)}, u32[]{:S(2)}) collective-permute-start(bf16[256,1024]{1,0:T(8,128)(2,1)S(1)} %get-tuple-element.108), channel_id=1, source_target_pairs={{0,1},{1,0},{2,3},{3,2},{4,5},{5,4},{6,7},{7,6},{8,9},{9,8},{10,11... | collective-permute-start | bytes 1572872 | tf_op jit(solution)/shard_map/ppermute | solution.py:49
  421.2 53.1 %collective-permute-start.87 = (bf16[512,512]{1,0:T(8,128)(2,1)S(1)}, bf16[512,512]{1,0:T(8,128)(2,1)S(1)}, u32[]{:S(2)}, u32[]{:S(2)}) collective-permute-start(bf16[512,512]{1,0:T(8,128)(2,1)S(1)} %fusion.66), channel_id=1, source_target_pairs={{0,8},{24,16},{1,9},{25,17},{2,10},{26,18},{3,11},{27,19},{4,12},{... | collective-permute-start | bytes 1572872 | tf_op jit(solution)/shard_map/ppermute | solution.py:106
  425.5 50.5 %collective-permute-start.92 = (bf16[512,512]{1,0:T(8,128)(2,1)S(1)}, bf16[512,512]{1,0:T(8,128)(2,1)S(1)}, u32[]{:S(2)}, u32[]{:S(2)}) collective-permute-start(bf16[512,512]{1,0:T(8,128)(2,1)S(1)} %fusion.65), channel_id=1, source_target_pairs={{0,8},{24,16},{1,9},{25,17},{2,10},{26,18},{3,11},{27,19},{4,12},{... | collective-permute-start | bytes 1572872 | tf_op jit(solution)/shard_map/ppermute | solution.py:106
  441.0 41.1 %collective-permute-start.66 = (bf16[256,1024]{1,0:T(8,128)(2,1)S(1)}, bf16[256,1024]{1,0:T(8,128)(2,1)S(1)}, u32[]{:S(2)}, u32[]{:S(2)}) collective-permute-start(bf16[256,1024]{1,0:T(8,128)(2,1)S(1)} %fusion.70), channel_id=1, source_target_pairs={{0,8},{24,16},{1,9},{25,17},{2,10},{26,18},{3,11},{27,19},{4,12},{... | collective-permute-start | bytes 1572872 | tf_op jit(solution)/shard_map/ppermute | solution.py:106
  456.5 28.5 %collective-permute-start.71 = (bf16[256,1024]{1,0:T(8,128)(2,1)S(1)}, bf16[256,1024]{1,0:T(8,128)(2,1)S(1)}, u32[]{:S(2)}, u32[]{:S(2)}) collective-permute-start(bf16[256,1024]{1,0:T(8,128)(2,1)S(1)} %fusion.69), channel_id=1, source_target_pairs={{0,8},{24,16},{1,9},{25,17},{2,10},{26,18},{3,11},{27,19},{4,12},{... | collective-permute-start | bytes 1572872 | tf_op jit(solution)/shard_map/ppermute | solution.py:106
  458.7 28.3 %collective-permute-start.23 = (bf16[256,768]{1,0:T(8,128)(2,1)S(1)}, bf16[256,768]{1,0:T(8,128)(2,1)S(1)}, u32[]{:S(2)}, u32[]{:S(2)}) collective-permute-start(bf16[256,768]{1,0:T(8,128)(2,1)S(1)} %dynamic-slice_bitcast_fusion.24), channel_id=1, source_target_pairs={{0,4},{1,5},{2,6},{3,7},{4,0},{5,1},{6,2},{7,3},{8,12},{9,13},{10,... | collective-permute-start | bytes 1179656 | tf_op jit(solution)/shard_map/ppermute | solution.py:56
  474.3 14.1 %collective-permute-start.28 = (bf16[256,768]{1,0:T(8,128)(2,1)S(1)}, bf16[256,768]{1,0:T(8,128)(2,1)S(1)}, u32[]{:S(2)}, u32[]{:S(2)}) collective-permute-start(bf16[256,768]{1,0:T(8,128)(2,1)S(1)} %dynamic-slice_bitcast_fusion.23), channel_id=1, source_target_pairs={{0,2},{1,3},{2,0},{3,1},{4,6},{5,7},{6,4},{7,5},{8,10},{9,11},{10,... | collective-permute-start | bytes 1179656 | tf_op jit(solution)/shard_map/ppermute | solution.py:56
  476.0 28.3 %collective-permute-start.8 = (bf16[256,1024]{1,0:T(8,128)(2,1)S(1)}, bf16[256,1024]{1,0:T(8,128)(2,1)S(1)}, u32[]{:S(2)}, u32[]{:S(2)}) collective-permute-start(bf16[256,1024]{1,0:T(8,128)(2,1)S(1)} %slice.587), channel_id=1, source_target_pairs={{0,1},{1,0},{2,3},{3,2},{4,5},{5,4},{6,7},{7,6},{8,9},{9,8},{10,11... | collective-permute-start | bytes 1572872 | tf_op jit(solution)/shard_map/ppermute | solution.py:49
  482.1 54.7 %collective-permute-start.75 = (bf16[2,512,512]{2,1,0:T(8,128)(2,1)}, bf16[2,512,512]{2,1,0:T(8,128)(2,1)}, u32[]{:S(2)}, u32[]{:S(2)}) collective-permute-start(bf16[2,512,512]{2,1,0:T(8,128)(2,1)} %dynamic-slice_bitcast_fusion.3), channel_id=1, source_target_pairs={{0,2},{1,3},{2,0},{3,1},{4,6},{5,7},{6,4},{7,5},{8,10},{9,11},{10,... | collective-permute-start | bytes 3145736 | tf_op jit(solution)/shard_map/ppermute | solution.py:56
  485.0 56.2 %collective-permute-start.80 = (bf16[2,512,512]{2,1,0:T(8,128)(2,1)}, bf16[2,512,512]{2,1,0:T(8,128)(2,1)}, u32[]{:S(2)}, u32[]{:S(2)}) collective-permute-start(bf16[2,512,512]{2,1,0:T(8,128)(2,1)} %dynamic-slice_bitcast_fusion.2), channel_id=1, source_target_pairs={{0,4},{1,5},{2,6},{3,7},{4,0},{5,1},{6,2},{7,3},{8,12},{9,13},{10,... | collective-permute-start | bytes 3145736 | tf_op jit(solution)/shard_map/ppermute | solution.py:56
  488.5 15.0 %collective-permute-start.29 = (bf16[256,768]{1,0:T(8,128)(2,1)S(1)}, bf16[256,768]{1,0:T(8,128)(2,1)S(1)}, u32[]{:S(2)}, u32[]{:S(2)}) collective-permute-start(bf16[256,768]{1,0:T(8,128)(2,1)S(1)} %fusion.105), channel_id=1, source_target_pairs={{0,8},{24,16},{1,9},{25,17},{2,10},{26,18},{3,11},{27,19},{4,12},{... | collective-permute-start | bytes 1179656 | tf_op jit(solution)/shard_map/ppermute | solution.py:106
  513.4 114.7 %collective-permute-start.53 = (bf16[2,256,1024]{2,1,0:T(8,128)(2,1)}, bf16[2,256,1024]{2,1,0:T(8,128)(2,1)}, u32[]{:S(2)}, u32[]{:S(2)}) collective-permute-start(bf16[2,256,1024]{2,1,0:T(8,128)(2,1)} %dynamic-slice_bitcast_fusion.7), channel_id=1, source_target_pairs={{0,2},{1,3},{2,0},{3,1},{4,6},{5,7},{6,4},{7,5},{8,10},{9,11},{10,... | collective-permute-start | bytes 3145736 | tf_op jit(solution)/shard_map/ppermute | solution.py:56
  514.6 120.7 %collective-permute-start.58 = (bf16[2,256,1024]{2,1,0:T(8,128)(2,1)}, bf16[2,256,1024]{2,1,0:T(8,128)(2,1)}, u32[]{:S(2)}, u32[]{:S(2)}) collective-permute-start(bf16[2,256,1024]{2,1,0:T(8,128)(2,1)} %dynamic-slice_bitcast_fusion.6), channel_id=1, source_target_pairs={{0,4},{1,5},{2,6},{3,7},{4,0},{5,1},{6,2},{7,3},{8,12},{9,13},{10,... | collective-permute-start | bytes 3145736 | tf_op jit(solution)/shard_map/ppermute | solution.py:56
  516.5 105.8 %collective-permute-start.89 = (bf16[512,512]{1,0:T(8,128)(2,1)}, bf16[512,512]{1,0:T(8,128)(2,1)}, u32[]{:S(2)}, u32[]{:S(2)}) collective-permute-start(bf16[512,512]{1,0:T(8,128)(2,1)} %add_convert_fusion.2), channel_id=1, source_target_pairs={{8,0},{16,24},{9,1},{17,25},{10,2},{18,26},{11,3},{19,27},{12,4},{... | collective-permute-start | bytes 1572872 | tf_op jit(solution)/shard_map/ppermute | solution.py:110
  536.8 88.4 %collective-permute-start.94 = (bf16[512,512]{1,0:T(8,128)(2,1)}, bf16[512,512]{1,0:T(8,128)(2,1)S(1)}, u32[]{:S(2)}, u32[]{:S(2)}) collective-permute-start(bf16[512,512]{1,0:T(8,128)(2,1)} %add_convert_fusion), channel_id=1, source_target_pairs={{8,0},{16,24},{9,1},{17,25},{10,2},{18,26},{11,3},{19,27},{12,4},{... | collective-permute-start | bytes 1572872 | tf_op jit(solution)/shard_map/ppermute | solution.py:110
  541.4 64.9 %collective-permute-start.68 = (bf16[256,1024]{1,0:T(8,128)(2,1)S(1)}, bf16[256,1024]{1,0:T(8,128)(2,1)S(1)}, u32[]{:S(2)}, u32[]{:S(2)}) collective-permute-start(bf16[256,1024]{1,0:T(8,128)(2,1)S(1)} %copy-done.47), channel_id=1, source_target_pairs={{8,0},{16,24},{9,1},{17,25},{10,2},{18,26},{11,3},{19,27},{12,4},{... | collective-permute-start | bytes 1572872 | tf_op jit(solution)/shard_map/ppermute | solution.py:110
  606.3 12.1 %collective-permute-start.73 = (bf16[256,1024]{1,0:T(8,128)(2,1)S(1)}, bf16[256,1024]{1,0:T(8,128)(2,1)S(1)}, u32[]{:S(2)}, u32[]{:S(2)}) collective-permute-start(bf16[256,1024]{1,0:T(8,128)(2,1)S(1)} %copy-done.46), channel_id=1, source_target_pairs={{8,0},{16,24},{9,1},{17,25},{10,2},{18,26},{11,3},{19,27},{12,4},{... | collective-permute-start | bytes 1572872 | tf_op jit(solution)/shard_map/ppermute | solution.py:110
  618.4 56.8 %collective-permute-start.26 = (bf16[256,768]{1,0:T(8,128)(2,1)S(1)}, bf16[256,768]{1,0:T(8,128)(2,1)}, u32[]{:S(2)}, u32[]{:S(2)}) collective-permute-start(bf16[256,768]{1,0:T(8,128)(2,1)S(1)} %add_convert_fusion.18), channel_id=1, source_target_pairs={{8,0},{16,24},{9,1},{17,25},{10,2},{18,26},{11,3},{19,27},{12,4},{... | collective-permute-start | bytes 1179656 | tf_op jit(solution)/shard_map/ppermute | solution.py:110
  622.3 53.9 %collective-permute-start.31 = (bf16[256,768]{1,0:T(8,128)(2,1)}, bf16[256,768]{1,0:T(8,128)(2,1)}, u32[]{:S(2)}, u32[]{:S(2)}) collective-permute-start(bf16[256,768]{1,0:T(8,128)(2,1)} %add_convert_fusion.16), channel_id=1, source_target_pairs={{8,0},{16,24},{9,1},{17,25},{10,2},{18,26},{11,3},{19,27},{12,4},{... | collective-permute-start | bytes 1179656 | tf_op jit(solution)/shard_map/ppermute | solution.py:110
  625.3 13.8 %collective-permute-start.95 = (f32[4,1,2,12,128]{4,2,3,0,1:T(2,128)S(1)}, f32[4,1,2,12,128]{4,2,3,0,1:T(2,128)S(1)}, u32[]{:S(2)}, u32[]{:S(2)}) collective-permute-start(f32[4,1,2,12,128]{4,2,3,0,1:T(2,128)S(1)} %bitcast.722), channel_id=1, source_target_pairs={{0,1},{1,0},{2,3},{3,2},{4,5},{5,4},{6,7},{7,6},{8,9},{9,8},{10,11... | collective-permute-start | bytes 147464 | tf_op jit(solution)/shard_map/ppermute | solution.py:49
  628.1 82.9 %collective-permute-start.76 = (bf16[512,512]{1,0:T(8,128)(2,1)}, bf16[512,512]{1,0:T(8,128)(2,1)}, u32[]{:S(2)}, u32[]{:S(2)}) collective-permute-start(bf16[512,512]{1,0:T(8,128)(2,1)} %dynamic-slice_bitcast_fusion.15), channel_id=1, source_target_pairs={{0,4},{1,5},{2,6},{3,7},{4,0},{5,1},{6,2},{7,3},{8,12},{9,13},{10,... | collective-permute-start | bytes 1572872 | tf_op jit(solution)/shard_map/ppermute | solution.py:56
  635.3 79.2 %collective-permute-start.81 = (bf16[512,512]{1,0:T(8,128)(2,1)}, bf16[512,512]{1,0:T(8,128)(2,1)}, u32[]{:S(2)}, u32[]{:S(2)}) collective-permute-start(bf16[512,512]{1,0:T(8,128)(2,1)} %dynamic-slice_bitcast_fusion.14), channel_id=1, source_target_pairs={{0,2},{1,3},{2,0},{3,1},{4,6},{5,7},{6,4},{7,5},{8,10},{9,11},{10,... | collective-permute-start | bytes 1572872 | tf_op jit(solution)/shard_map/ppermute | solution.py:56
  639.1 10.9 %collective-permute-start.96 = (f32[2,2,12,128]{3,1,2,0:T(2,128)S(1)}, f32[2,2,12,128]{3,1,2,0:T(2,128)S(1)}, u32[]{:S(2)}, u32[]{:S(2)}) collective-permute-start(f32[2,2,12,128]{3,1,2,0:T(2,128)S(1)} %dynamic-slice_bitcast_fusion.36), channel_id=1, source_target_pairs={{0,2},{1,3},{2,0},{3,1},{4,6},{5,7},{6,4},{7,5},{8,10},{9,11},{10,... | collective-permute-start | bytes 73736 | tf_op jit(solution)/shard_map/ppermute | solution.py:56
  672.2 45.5 %collective-permute-start.54 = (bf16[256,1024]{1,0:T(8,128)(2,1)}, bf16[256,1024]{1,0:T(8,128)(2,1)}, u32[]{:S(2)}, u32[]{:S(2)}) collective-permute-start(bf16[256,1024]{1,0:T(8,128)(2,1)} %dynamic-slice_bitcast_fusion.21), channel_id=1, source_target_pairs={{0,4},{1,5},{2,6},{3,7},{4,0},{5,1},{6,2},{7,3},{8,12},{9,13},{10,... | collective-permute-start | bytes 1572872 | tf_op jit(solution)/shard_map/ppermute | solution.py:56
  675.2 31.3 %collective-permute-start.74 = (bf16[128,2048]{1,0:T(8,128)(2,1)}, bf16[128,2048]{1,0:T(8,128)(2,1)}, u32[]{:S(2)}, u32[]{:S(2)}) collective-permute-start(bf16[128,2048]{1,0:T(8,128)(2,1)} %get-tuple-element.143), channel_id=1, source_target_pairs={{0,1},{1,0},{2,3},{3,2},{4,5},{5,4},{6,7},{7,6},{8,9},{9,8},{10,11... | collective-permute-start | bytes 1572872 | tf_op jit(solution)/shard_map/ppermute | solution.py:49
  703.9 21.6 %collective-permute-start.59 = (bf16[256,1024]{1,0:T(8,128)(2,1)}, bf16[256,1024]{1,0:T(8,128)(2,1)}, u32[]{:S(2)}, u32[]{:S(2)}) collective-permute-start(bf16[256,1024]{1,0:T(8,128)(2,1)} %dynamic-slice_bitcast_fusion.20), channel_id=1, source_target_pairs={{0,2},{1,3},{2,0},{3,1},{4,6},{5,7},{6,4},{7,5},{8,10},{9,11},{10,... | collective-permute-start | bytes 1572872 | tf_op jit(solution)/shard_map/ppermute | solution.py:56
  706.5 44.6 %collective-permute-start.11 = (bf16[2,256,768]{2,1,0:T(8,128)(2,1)}, bf16[2,256,768]{2,1,0:T(8,128)(2,1)}, u32[]{:S(2)}, u32[]{:S(2)}) collective-permute-start(bf16[2,256,768]{2,1,0:T(8,128)(2,1)} %dynamic-slice_bitcast_fusion.11), channel_id=1, source_target_pairs={{0,2},{1,3},{2,0},{3,1},{4,6},{5,7},{6,4},{7,5},{8,10},{9,11},{10,... | collective-permute-start | bytes 2359304 | tf_op jit(solution)/shard_map/ppermute | solution.py:56
  714.5 39.3 %collective-permute-start.16 = (bf16[2,256,768]{2,1,0:T(8,128)(2,1)}, bf16[2,256,768]{2,1,0:T(8,128)(2,1)}, u32[]{:S(2)}, u32[]{:S(2)}) collective-permute-start(bf16[2,256,768]{2,1,0:T(8,128)(2,1)} %dynamic-slice_bitcast_fusion.10), channel_id=1, source_target_pairs={{0,4},{1,5},{2,6},{3,7},{4,0},{5,1},{6,2},{7,3},{8,12},{9,13},{10,... | collective-permute-start | bytes 2359304 | tf_op jit(solution)/shard_map/ppermute | solution.py:56
  717.7 18.3 %collective-permute-start.32 = (bf16[128,1536]{1,0:T(8,128)(2,1)S(1)}, bf16[128,1536]{1,0:T(8,128)(2,1)S(1)}, u32[]{:S(2)}, u32[]{:S(2)}) collective-permute-start(bf16[128,1536]{1,0:T(8,128)(2,1)S(1)} %copy-done.68), channel_id=1, source_target_pairs={{0,1},{1,0},{2,3},{3,2},{4,5},{5,4},{6,7},{7,6},{8,9},{9,8},{10,11... | collective-permute-start | bytes 1179656 | tf_op jit(solution)/shard_map/ppermute | solution.py:49
  728.1 41.7 %collective-permute-start.77 = (bf16[512,512]{1,0:T(8,128)(2,1)}, bf16[512,512]{1,0:T(8,128)(2,1)}, u32[]{:S(2)}, u32[]{:S(2)}) collective-permute-start(bf16[512,512]{1,0:T(8,128)(2,1)} %fusion.68), channel_id=1, source_target_pairs={{0,8},{24,16},{1,9},{25,17},{2,10},{26,18},{3,11},{27,19},{4,12},{... | collective-permute-start | bytes 1572872 | tf_op jit(solution)/shard_map/ppermute | solution.py:106
  732.5 39.6 %collective-permute-start.82 = (bf16[512,512]{1,0:T(8,128)(2,1)}, bf16[512,512]{1,0:T(8,128)(2,1)}, u32[]{:S(2)}, u32[]{:S(2)}) collective-permute-start(bf16[512,512]{1,0:T(8,128)(2,1)} %fusion.67), channel_id=1, source_target_pairs={{0,8},{24,16},{1,9},{25,17},{2,10},{26,18},{3,11},{27,19},{4,12},{... | collective-permute-start | bytes 1572872 | tf_op jit(solution)/shard_map/ppermute | solution.py:106
  742.0 32.5 %collective-permute-start.55 = (bf16[256,1024]{1,0:T(8,128)(2,1)S(1)}, bf16[256,1024]{1,0:T(8,128)(2,1)S(1)}, u32[]{:S(2)}, u32[]{:S(2)}) collective-permute-start(bf16[256,1024]{1,0:T(8,128)(2,1)S(1)} %copy-done.45), channel_id=1, source_target_pairs={{0,8},{24,16},{1,9},{25,17},{2,10},{26,18},{3,11},{27,19},{4,12},{... | collective-permute-start | bytes 1572872 | tf_op jit(solution)/shard_map/ppermute | solution.py:106
  751.1 25.3 %collective-permute-start.60 = (bf16[256,1024]{1,0:T(8,128)(2,1)S(1)}, bf16[256,1024]{1,0:T(8,128)(2,1)S(1)}, u32[]{:S(2)}, u32[]{:S(2)}) collective-permute-start(bf16[256,1024]{1,0:T(8,128)(2,1)S(1)} %fusion.71), channel_id=1, source_target_pairs={{0,8},{24,16},{1,9},{25,17},{2,10},{26,18},{3,11},{27,19},{4,12},{... | collective-permute-start | bytes 1572872 | tf_op jit(solution)/shard_map/ppermute | solution.py:106
  772.2 15.5 %collective-permute-start.78 = (bf16[512,512]{1,0:T(8,128)(2,1)S(1)}, bf16[512,512]{1,0:T(8,128)(2,1)S(1)}, u32[]{:S(2)}, u32[]{:S(2)}) collective-permute-start(bf16[512,512]{1,0:T(8,128)(2,1)S(1)} %add_convert_fusion.7), channel_id=1, source_target_pairs={{8,16},{16,8},{9,17},{17,9},{10,18},{18,10},{11,19},{19,11},{12,20... | collective-permute-start | bytes 1572872 | tf_op jit(solution)/shard_map/ppermute | solution.py:108
  774.5 16.1 %collective-permute-start.83 = (bf16[512,512]{1,0:T(8,128)(2,1)S(1)}, bf16[512,512]{1,0:T(8,128)(2,1)S(1)}, u32[]{:S(2)}, u32[]{:S(2)}) collective-permute-start(bf16[512,512]{1,0:T(8,128)(2,1)S(1)} %add_convert_fusion.5), channel_id=1, source_target_pairs={{8,16},{16,8},{9,17},{17,9},{10,18},{18,10},{11,19},{19,11},{12,20... | collective-permute-start | bytes 1572872 | tf_op jit(solution)/shard_map/ppermute | solution.py:108
  776.4 15.7 %collective-permute-start.56 = (bf16[256,1024]{1,0:T(8,128)(2,1)S(1)}, bf16[256,1024]{1,0:T(8,128)(2,1)S(1)}, u32[]{:S(2)}, u32[]{:S(2)}) collective-permute-start(bf16[256,1024]{1,0:T(8,128)(2,1)S(1)} %add_convert_fusion.15), channel_id=1, source_target_pairs={{8,16},{16,8},{9,17},{17,9},{10,18},{18,10},{11,19},{19,11},{12,20... | collective-permute-start | bytes 1572872 | tf_op jit(solution)/shard_map/ppermute | solution.py:108
  777.3 25.4 %collective-permute-start.61 = (bf16[256,1024]{1,0:T(8,128)(2,1)S(1)}, bf16[256,1024]{1,0:T(8,128)(2,1)S(1)}, u32[]{:S(2)}, u32[]{:S(2)}) collective-permute-start(bf16[256,1024]{1,0:T(8,128)(2,1)S(1)} %add_convert_fusion.13), channel_id=1, source_target_pairs={{8,16},{16,8},{9,17},{17,9},{10,18},{18,10},{11,19},{19,11},{12,20... | collective-permute-start | bytes 1572872 | tf_op jit(solution)/shard_map/ppermute | solution.py:108
  778.1 19.0 %collective-permute-start.13 = (bf16[256,768]{1,0:T(8,128)(2,1)S(1)}, bf16[256,768]{1,0:T(8,128)(2,1)S(1)}, u32[]{:S(2)}, u32[]{:S(2)}) collective-permute-start(bf16[256,768]{1,0:T(8,128)(2,1)S(1)} %fusion.108), channel_id=1, source_target_pairs={{0,8},{24,16},{1,9},{25,17},{2,10},{26,18},{3,11},{27,19},{4,12},{... | collective-permute-start | bytes 1179656 | tf_op jit(solution)/shard_map/ppermute | solution.py:106
  787.7 14.2 %collective-permute-start.18 = (bf16[256,768]{1,0:T(8,128)(2,1)S(1)}, bf16[256,768]{1,0:T(8,128)(2,1)S(1)}, u32[]{:S(2)}, u32[]{:S(2)}) collective-permute-start(bf16[256,768]{1,0:T(8,128)(2,1)S(1)} %fusion.107), channel_id=1, source_target_pairs={{0,8},{24,16},{1,9},{25,17},{2,10},{26,18},{3,11},{27,19},{4,12},{... | collective-permute-start | bytes 1179656 | tf_op jit(solution)/shard_map/ppermute | solution.py:106
  790.6 58.2 %collective-permute-start.79 = (bf16[512,512]{1,0:T(8,128)(2,1)S(1)}, bf16[512,512]{1,0:T(8,128)(2,1)}, u32[]{:S(2)}, u32[]{:S(2)}) collective-permute-start(bf16[512,512]{1,0:T(8,128)(2,1)S(1)} %add_convert_fusion.6), channel_id=1, source_target_pairs={{8,0},{16,24},{9,1},{17,25},{10,2},{18,26},{11,3},{19,27},{12,4},{... | collective-permute-start | bytes 1572872 | tf_op jit(solution)/shard_map/ppermute | solution.py:110
  792.0 57.9 %collective-permute-start.84 = (bf16[512,512]{1,0:T(8,128)(2,1)S(1)}, bf16[512,512]{1,0:T(8,128)(2,1)}, u32[]{:S(2)}, u32[]{:S(2)}) collective-permute-start(bf16[512,512]{1,0:T(8,128)(2,1)S(1)} %add_convert_fusion.4), channel_id=1, source_target_pairs={{8,0},{16,24},{9,1},{17,25},{10,2},{18,26},{11,3},{19,27},{12,4},{... | collective-permute-start | bytes 1572872 | tf_op jit(solution)/shard_map/ppermute | solution.py:110
  797.1 39.2 %collective-permute-start.57 = (bf16[256,1024]{1,0:T(8,128)(2,1)S(1)}, bf16[256,1024]{1,0:T(8,128)(2,1)S(1)}, u32[]{:S(2)}, u32[]{:S(2)}) collective-permute-start(bf16[256,1024]{1,0:T(8,128)(2,1)S(1)} %add_convert_fusion.14), channel_id=1, source_target_pairs={{8,0},{16,24},{9,1},{17,25},{10,2},{18,26},{11,3},{19,27},{12,4},{... | collective-permute-start | bytes 1572872 | tf_op jit(solution)/shard_map/ppermute | solution.py:110
  803.6 43.9 %collective-permute-start.62 = (bf16[256,1024]{1,0:T(8,128)(2,1)S(1)}, bf16[256,1024]{1,0:T(8,128)(2,1)S(1)}, u32[]{:S(2)}, u32[]{:S(2)}) collective-permute-start(bf16[256,1024]{1,0:T(8,128)(2,1)S(1)} %add_convert_fusion.12), channel_id=1, source_target_pairs={{8,0},{16,24},{9,1},{17,25},{10,2},{18,26},{11,3},{19,27},{12,4},{... | collective-permute-start | bytes 1572872 | tf_op jit(solution)/shard_map/ppermute | solution.py:110
  805.0 48.7 %collective-permute-start.15 = (bf16[256,768]{1,0:T(8,128)(2,1)S(1)}, bf16[256,768]{1,0:T(8,128)(2,1)}, u32[]{:S(2)}, u32[]{:S(2)}) collective-permute-start(bf16[256,768]{1,0:T(8,128)(2,1)S(1)} %add_convert_fusion.22), channel_id=1, source_target_pairs={{8,0},{16,24},{9,1},{17,25},{10,2},{18,26},{11,3},{19,27},{12,4},{... | collective-permute-start | bytes 1179656 | tf_op jit(solution)/shard_map/ppermute | solution.py:110
  836.3 21.4 %collective-permute-start.20 = (bf16[256,768]{1,0:T(8,128)(2,1)}, bf16[256,768]{1,0:T(8,128)(2,1)}, u32[]{:S(2)}, u32[]{:S(2)}) collective-permute-start(bf16[256,768]{1,0:T(8,128)(2,1)} %add_convert_fusion.20), channel_id=1, source_target_pairs={{8,0},{16,24},{9,1},{17,25},{10,2},{18,26},{11,3},{19,27},{12,4},{... | collective-permute-start | bytes 1179656 | tf_op jit(solution)/shard_map/ppermute | solution.py:110
  (158 other events, 1674.9 us)

commit v3 on v2

--- a/solution.py
+++ b/solution.py
@@ -16,21 +16,6 @@
 neg_large = -1e30
 low = jnp.bfloat16
 wide = jnp.float32
-
-
-def normalize(values):
-    centred = values - jnp.mean(values, axis=-1, keepdims=True)
-    rstd = lax.rsqrt(jnp.mean(centred * centred, axis=-1, keepdims=True) + epsilon)
-    return (centred * rstd, rstd)
-
-
-def norm_back(grad_norm, normed, rstd):
-    inner = jnp.mean(grad_norm * normed, axis=-1, keepdims=True)
-    return rstd * (grad_norm - jnp.mean(grad_norm, axis=-1, keepdims=True) - normed * inner)
-
-
-def column_sums(values):
-    return jnp.sum(values.astype(wide), axis=0)
 
 
 class Net:
@@ -112,26 +97,6 @@
             total = jnp.where(outer, got, total)
         return total
 
-    def pair(self, value):
-        return jnp.concatenate([value, self.over_core(value)], axis=0)
-
-    def join(self, partial):
-        rows = partial.shape[0] // 2
-        return partial[:rows] + self.over_core(partial[rows:].astype(low)).astype(wide)
-
-
-def halves(columns):
-    return ((0, columns // 2), (columns // 2, columns))
-
-
-def scatter_weight(net, value):
-    orders = (list(range(net.bits)), list(reversed(range(net.bits))))
-    parts = [
-        net.sum_reps(net.scatter_chips(value[:, :, start:stop], order))
-        for order, (start, stop) in zip(orders, halves(value.shape[2]))
-    ]
-    return jnp.concatenate(parts, axis=1)
-
 
 def by_half(weight, net, groups):
     layers, rows, columns = weight.shape
@@ -139,23 +104,15 @@
     return split.transpose(0, 3, 1, 2, 4).reshape(layers, 2, rows, columns // 2)
 
 
-def swap_back(value, net, groups):
-    rows = value.shape[0] // 2
-    split = value.reshape(2, rows, value.shape[1])
-    mine = lax.dynamic_index_in_dim(split, net.core, 0, keepdims=False)
-    other = lax.dynamic_index_in_dim(split, 1 - net.core, 0, keepdims=False)
-    got = net.over_core(other)
-    block = value.shape[1] // (groups * net.high)
-    both = [part.reshape(rows, groups * net.high, block) for part in (mine, got)]
+def whole_columns(mine, other, net, groups):
+    layers, rows, columns = mine.shape
+    block = columns // (groups * net.high)
+    both = [part.reshape(layers, rows, groups * net.high, block) for part in (mine, other)]
     first = net.core == 0
     stacked = jnp.stack(
-        [jnp.where(first, both[0], both[1]), jnp.where(first, both[1], both[0])], axis=2
+        [jnp.where(first, both[0], both[1]), jnp.where(first, both[1], both[0])], axis=3
     )
-    return stacked.reshape(rows, 2 * value.shape[1])
-
-
-def split_heads(rows, heads):
-    return rows.reshape(2, rows.shape[0] // 2, heads, rows.shape[1] // heads)
+    return stacked.reshape(layers, rows, 2 * columns).astype(wide)
 
 
 class Place:
@@ -353,6 +310,249 @@
             self.across_bytes().wait_send()
 
 
+class Reduce:
+    def __init__(self, place, layer, kind, part, terms, arrived, lines, done, swapped, sems, bufs):
+        self.place, self.dims = place, place.dims
+        self.layer, self.kind, self.part = layer, kind, part
+        self.terms, self.arrived, self.lines, self.done, self.swapped = terms, arrived, lines, done, swapped
+        self.send, self.recv = sems
+        self.mine, self.other, self.load_sem, self.store_sem = bufs
+        self.rows, self.held, self.columns, self.paired = self.dims.kinds[kind]
+        self.size = self.columns // 2
+        self.columns_here = pl.ds(part * self.size, self.size)
+        self.at = (layer * 4 + kind) * 2 + part
+        bits = list(range(self.dims.bits))
+        self.order = bits if part == 0 else bits[::-1]
+        self.moves = self.dims.reps - 1
+        self.stage = 0
+        self.stages = 1 + self.dims.bits + self.moves + (1 if self.paired else 0)
+        self.split = self.paired and self.dims.step > 1
+        self.piece = self.rows * (2 if self.paired and not self.split else 1)
+        self.pieces = 2 if self.split else 1
+
+    def row_of(self, pair, which):
+        if not self.paired:
+            return pair * self.rows
+        return (self.place.first_shard(pair) + which * self.dims.step) * self.rows
+
+    def sems(self, slot):
+        return self.send.at[self.at, slot], self.recv.at[self.at, slot]
+
+    def kept(self, index, turn, away):
+        pair = self.place.pair
+        for i, bit in enumerate(self.order[turn + 1 :]):
+            size = 1 << bit
+            wanted = (index // (1 << i)) % 2
+            pair = pair + size * (wanted - (self.place.pair // size) % 2)
+        if away:
+            pair = self.place.flip(pair, self.order[turn])
+        return pair
+
+    def count(self, turn):
+        return (self.dims.pairs >> (turn + 1)) * self.pieces
+
+    def loop(self, count, body):
+        if count <= 4:
+            for i in range(count):
+                body(i)
+        else:
+            tiles(count, body)
+
+    def block(self, ref, index, turn, away):
+        pair = self.kept(index // self.pieces, turn, away)
+        start = self.row_of(pair, index % self.pieces)
+        return ref.at[self.layer, pl.ds(pl.multiple_of(start, 16), self.piece), self.columns_here]
+
+    def start_turn(self, turn):
+        def one(index):
+            remote(
+                self.block(self.terms, index, turn, True),
+                self.block(self.arrived[turn], index, turn, True),
+                *self.sems(turn),
+                self.place.over_bit(self.order[turn]),
+            ).start()
+
+        self.loop(self.count(turn), one)
+
+    def turn_bytes(self, turn):
+        ref = self.terms.at[self.layer, pl.ds(0, self.count(turn) * self.piece), self.columns_here]
+        return remote(ref, ref, *self.sems(turn), self.place.over_bit(self.order[turn]))
+
+    def add(self, count, own, other, result):
+        step = min(self.piece, self.mine.shape[1])
+        per = self.piece // step
+        total = count * per
+
+        def part_of(make, index):
+            ref = make(index // per)
+            return ref.at[pl.ds(pl.multiple_of((index % per) * step, 16), step)]
+
+        def slots(index):
+            slot = index % 2
+            rows, cols = pl.ds(0, step), pl.ds(0, self.size)
+            return self.mine.at[slot, rows, cols], self.other.at[slot, rows, cols], slot
+
+        def load(index):
+            one, two, slot = slots(index)
+            return (
+                pltpu.make_async_copy(part_of(own, index), one, self.load_sem.at[slot, 0]),
+                pltpu.make_async_copy(part_of(other, index), two, self.load_sem.at[slot, 1]),
+            )
+
+        def store(index):
+            one, _, slot = slots(index)
+            return pltpu.make_async_copy(one, part_of(result, index), self.store_sem.at[slot])
+
+        def body(index, first, last):
+            @when(jnp.logical_not(last) if not isinstance(last, bool) else not last)
+            def _():
+                @when(jnp.logical_not(first) if not isinstance(first, bool) else not first)
+                def _():
+                    store(index - 1).wait()
+
+                for copy in load(index + 1):
+                    copy.start()
+
+            for copy in load(index):
+                copy.wait()
+            one, two, _ = slots(index)
+            one[...] = (one[...].astype(wide) + two[...].astype(wide)).astype(low)
+            store(index).start()
+
+        for copy in load(0):
+            copy.start()
+        if total <= 4:
+            for index in range(total):
+                body(index, index == 0, index == total - 1)
+        else:
+            tiles(total, lambda index: body(index, index == 0, index == total - 1))
+        if total > 1:
+            store(total - 2).wait()
+        store(total - 1).wait()
+
+    def finish_turn(self, turn):
+        self.turn_bytes(turn).wait_recv()
+        self.add(
+            self.count(turn),
+            lambda index: self.block(self.terms, index, turn, False),
+            lambda index: self.block(self.arrived[turn], index, turn, False),
+            lambda index: self.block(self.terms, index, turn, False),
+        )
+
+    def own(self, which):
+        start = self.row_of(self.place.pair, which)
+        return self.terms.at[self.layer, pl.ds(pl.multiple_of(start, 16), self.piece), self.columns_here]
+
+    def line(self, move, which):
+        return self.lines.at[self.layer, move, pl.ds(which * self.piece, self.piece), self.columns_here]
+
+    def final(self, which):
+        return self.done.at[self.layer, pl.ds(which * self.piece, self.piece), self.columns_here]
+
+    def roles(self, move):
+        reps, half = self.dims.reps, self.dims.reps // 2
+        if move < half - 1:
+            return (move, reps - 1 - move), (move + 1, reps - 2 - move)
+        if move == half - 1:
+            return (half - 1, half), (half, half - 1)
+        back = reps - 2 - move
+        return (back + 1, reps - 2 - back), (back, reps - 1 - back)
+
+    def move_copies(self, move, target):
+        half = self.dims.reps // 2
+        slot = self.dims.bits + move
+        for which in range(self.pieces):
+            src = self.own(which) if move < half else self.final(which)
+            dst = self.line(move, which) if move < half else self.final(which)
+            yield remote(src, dst, *self.sems(slot), (target, self.place.me))
+
+    def move_bytes(self, move):
+        slot = self.dims.bits + move
+        ref = self.done.at[self.layer, pl.ds(0, self.pieces * self.piece), self.columns_here]
+        return remote(ref, ref, *self.sems(slot), self.place.mate())
+
+    def start_move(self, move):
+        senders, receivers = self.roles(move)
+        for sender, receiver in zip(senders, receivers):
+
+            @pl.when(self.place.rep == sender)
+            def _(receiver=receiver):
+                for copy in self.move_copies(move, receiver):
+                    copy.start()
+
+    def finish_move(self, move):
+        half = self.dims.reps // 2
+        _, receivers = self.roles(move)
+
+        @pl.when(jnp.logical_or(self.place.rep == receivers[0], self.place.rep == receivers[1]))
+        def _():
+            self.move_bytes(move).wait_recv()
+            if move < half:
+                self.add(
+                    self.pieces,
+                    self.own,
+                    lambda which: self.line(move, which),
+                    self.own if move < half - 1 else self.final,
+                )
+
+    def swap_copy(self):
+        rows = self.done.at[
+            self.layer,
+            pl.ds(pl.multiple_of((1 - self.place.half) * self.rows, 16), self.rows),
+            self.columns_here,
+        ]
+        return remote(
+            rows,
+            self.swapped.at[self.layer, pl.ds(0, self.rows), self.columns_here],
+            *self.sems(self.dims.bits + self.moves),
+            self.place.mate(),
+        )
+
+    def advance(self):
+        bits = self.dims.bits
+        if self.stage == 0:
+            self.start_turn(0)
+        elif self.stage < bits:
+            self.finish_turn(self.stage - 1)
+            self.start_turn(self.stage)
+        elif self.stage == bits:
+            self.finish_turn(bits - 1)
+            self.start_move(0)
+        elif self.stage < bits + self.moves:
+            self.finish_move(self.stage - bits - 1)
+            self.start_move(self.stage - bits)
+        elif self.stage == bits + self.moves:
+            self.finish_move(self.moves - 1)
+            if self.paired:
+                self.swap_copy().start()
+        else:
+            self.swap_copy().wait_recv()
+        self.stage += 1
+
+    def reach(self, stage):
+        while self.stage < min(stage, self.stages):
+            self.advance()
+
+    def finish_sends(self):
+        for turn in range(self.dims.bits):
+            self.turn_bytes(turn).wait_send()
+        for move in range(self.moves):
+            senders, _ = self.roles(move)
+
+            @pl.when(jnp.logical_or(self.place.rep == senders[0], self.place.rep == senders[1]))
+            def _(move=move):
+                self.move_bytes(move).wait_send()
+
+        if self.paired:
+            self.swap_copy().wait_send()
+
+
+def when(condition):
+    if isinstance(condition, bool):
+        return (lambda body: body()) if condition else (lambda body: None)
+    return pl.when(condition)
+
+
 def in_plane_columns(dims, layer, kind):
     columns = dims.kinds[kind][2]
     if dims.reps % 2:
@@ -383,61 +583,25 @@
     lax.fori_loop(0, count, step, 0)
 
 
-def forward_kernel(
-    dims,
-    x_ref,
-    seg_row,
-    seg_col,
-    small,
-    src_qkv,
-    src_out,
-    src_up,
-    src_down,
-    output,
-    tops,
-    out_qkv_w,
-    out_out_w,
-    out_up_w,
-    out_down_w,
-    out_hidden,
-    out_qkv,
-    out_attended,
-    out_probs,
-    out_norm1,
-    out_first,
-    out_act,
-    out_slope,
-    out_norm2,
-    out_rstd,
-    w_qkv,
-    w_out,
-    w_up,
-    w_down,
-    both_hidden,
-    qkv,
-    attended,
-    probs,
-    norm1,
-    both_first,
-    act,
-    slope,
-    norm2,
-    rstd,
-    hidden,
-    first,
-    total,
-    away,
-    back,
-    bias,
-    seg_rows,
-    seg_cols,
-    gather_local,
-    gather_send,
-    gather_recv,
-    mate_send,
-    mate_recv,
-    save_sem,
-):
+def layers_kernel(dims, *refs):
+    refs = iter(refs)
+
+    def take(count):
+        return [next(refs) for _ in range(count)]
+
+    x_ref, cotangent, seg_row, seg_col, small = take(5)
+    src_qkv, src_out, src_up, src_down = take(4)
+    output, tops, vectors, input_grad = take(4)
+    terms = take(4)
+    arrived = [take(4) for _ in range(dims.bits)]
+    lines, done = take(4), take(4)
+    swapped = take(2)
+    w_qkv, w_out, w_up, w_down = take(4)
+    both_hidden, qkv, attended, probs, norm1, both_first, act, slope, norm2, rstd = take(10)
+    hidden, first, total, away, back, bias, both_grad, ring, add_mine, add_other = take(10)
+    seg_rows, seg_cols = take(2)
+    gather_local, gather_send, gather_recv, mate_send, mate_recv = take(5)
+    reduce_send, reduce_recv, load_sem, store_sem, ring_sem, io_sem = take(6)
     place = Place(dims)
     tokens, width = dims.tokens, dims.width
     heads_row = 128 // dims.head_dim
@@ -445,8 +609,9 @@
 
     barrier = pltpu.get_barrier_semaphore()
     others = [place.mate()] + [place.over_bit(bit) for bit in range(dims.bits)]
-    if dims.reps % 2 == 0:
-        others.append(place.over_plane())
+    reps = dims.reps
+    groups = sorted({1 % reps, (reps - 1) % reps} - {0})
+    others += [((place.rep + step) % reps, place.me) for step in groups]
     for other in others:
         pl.semaphore_signal(barrier, 1, device_id=other, device_id_type=MESH)
     pl.semaphore_wait(barrier, len(others))
@@ -478,7 +643,11 @@
 
     rows_copy = to_mate(seg_row, seg_rows)
     cols_copy = to_mate(seg_col, seg_cols)
-    both_hidden[0, pl.ds(0, tokens)] = x_ref[...]
+    x_copy = pltpu.make_async_copy(x_ref, both_hidden.at[0, pl.ds(0, tokens)], io_sem.at[0])
+    cotangent_copy = pltpu.make_async_copy(cotangent, both_grad.at[pl.ds(0, tokens)], io_sem.at[1])
+    x_copy.start()
+    cotangent_copy.start()
+    x_copy.wait()
     hidden_copy = to_mate(both_hidden.at[0, pl.ds(0, tokens)], both_hidden.at[0, pl.ds(tokens, tokens)])
     for gather in gathers:
         gather.begin()
@@ -491,14 +660,8 @@
                 gathers[at + ahead].reach(max(1, gathers[at + ahead].stages - ahead))
         gathers[at].reach(gathers[at].stages)
 
-    saves = []
-
-    def save(src, dst):
-        copy = pltpu.make_async_copy(src, dst, save_sem.at[len(saves)])
-        copy.start()
-        saves.append(copy)
-
-    hidden[...] = x_ref[...].astype(wide)
+    hidden[...] = both_hidden[0, pl.ds(0, tokens)].astype(wide)
+    vectors[...] = jnp.zeros(vectors.shape, wide)
     tops[...] = jnp.full(tops.shape, neg_large, wide)
     rows_copy.wait_recv()
     cols_copy.wait_recv()
@@ -521,26 +684,29 @@
 
         tiles(tokens // chunk, body)
 
-    def project(left, right, at, tile):
-        columns = dims.width
+    flying = [None, None]
+
+    def project(left, product, at):
+        slot = at % 2
+        if flying[slot] is not None:
+            flying[slot].wait_send()
+            settled.append(flying[slot])
 
         def far(j):
             cols = pl.ds(pl.multiple_of(j * tile, tile), tile)
-            away[at % 2, :, cols] = jnp.dot(
-                left[pl.ds(tokens, tokens)], right[:, cols], preferred_element_type=wide
-            ).astype(low)
+            away[slot, :, cols] = product(left[pl.ds(tokens, tokens)], cols).astype(low)
 
         def near(j):
             cols = pl.ds(pl.multiple_of(j * tile, tile), tile)
-            total[:, cols] = jnp.dot(left[pl.ds(0, tokens)], right[:, cols], preferred_element_type=wide)
-
-        tiles(columns // tile, far)
-        copy = to_mate(away.at[at % 2], back.at[at])
-        tiles(columns // tile, near)
-        return copy
-
+            total[:, cols] = product(left[pl.ds(0, tokens)], cols)
+
+        tiles(width // tile, far)
+        flying[slot] = to_mate(away.at[slot], back.at[at % (2 * dims.layers)])
+        tiles(width // tile, near)
+        return flying[slot]
+
+    settled = []
     tile = min(512, width)
-    waits = []
     for layer in range(dims.layers):
         prepare(4 * layer)
         hidden_copy.wait_recv()
@@ -582,11 +748,13 @@
         tiles(2 * lane_blocks, attend)
 
         prepare(4 * layer + 1)
-        if layer > 0:
-            waits[2 * layer - 2].wait_send()
-        copy = project(attended.at[layer], w_out.at[layer], 2 * layer, tile)
-        waits.append(copy)
-        copy.wait_recv()
+        project(
+            attended.at[layer],
+            lambda left, cols, layer=layer: jnp.dot(
+                left, w_out[layer, :, cols], preferred_element_type=wide
+            ),
+            2 * layer,
+        ).wait_recv()
 
         def first_rows(rows, value, layer=layer):
             first[rows] = value
@@ -621,11 +789,13 @@
         tiles(dims.kinds[2][2] // narrow, up_tile)
 
         prepare(4 * layer + 3)
-        if layer > 0:
-            waits[2 * layer - 1].wait_send()
-        copy = project(act.at[layer], w_down.at[layer], 2 * layer + 1, tile)
-        waits.append(copy)
-        copy.wait_recv()
+        project(
+            act.at[layer],
+            lambda left, cols, layer=layer: jnp.dot(
+                left, w_down[layer, :, cols], preferred_element_type=wide
+            ),
+            2 * layer + 1,
+        ).wait_recv()
         last = layer == dims.layers - 1
 
         def second_rows(rows, value, layer=layer, last=last):
@@ -651,181 +821,315 @@
                 both_hidden.at[layer + 1, pl.ds(0, tokens)],
                 both_hidden.at[layer + 1, pl.ds(tokens, tokens)],
             )
-        for src, dst in (
-            (both_hidden, out_hidden),
-            (qkv, out_qkv),
-            (attended, out_attended),
-            (probs, out_probs),
-            (norm1, out_norm1),
-            (both_first, out_first),
-            (act, out_act),
-            (slope, out_slope),
-            (norm2, out_norm2),
-            (rstd, out_rstd),
-            (w_qkv, out_qkv_w),
-            (w_out, out_out_w),
-            (w_up, out_up_w),
-            (w_down, out_down_w),
-        ):
-            save(src.at[layer], dst.at[layer])
+    reduces = {
+        (layer, kind): [
+            Reduce(
+                place,
+                layer,
+                kind,
+                part,
+                terms[kind],
+                [arrived[turn][kind] for turn in range(dims.bits)],
+                lines[kind],
+                done[kind],
+                swapped[kind // 2],
+                (reduce_send, reduce_recv),
+                (add_mine, add_other, load_sem, store_sem),
+            )
+            for part in range(2)
+        ]
+        for layer in range(dims.layers)
+        for kind in range(4)
+    }
+    queue = [
+        reduces[layer, kind] for layer in reversed(range(dims.layers)) for kind in (3, 2, 1, 0)
+    ]
+    stages = max(item.stages for pair in queue for item in pair)
+
+    def pump(step, ahead=2):
+        if step + ahead < len(queue):
+            for item in queue[step + ahead]:
+                item.reach(1)
+        for behind in reversed(range(stages - 1)):
+            at = step - behind
+            if 0 <= at < len(queue):
+                for item in queue[at]:
+                    item.reach(2 + behind)
+
+    def weight_terms(layer, kind, left, right):
+        _, held, columns, _ = dims.kinds[kind]
+        step = min(256, held)
+        wide_cols = columns if columns <= ring.shape[2] else columns // 2
+        across = columns // wide_cols
+        count = (held // step) * across
+        slots = ring.shape[0]
+
+        def store(j):
+            rows = pl.ds(pl.multiple_of((j // across) * step, step), step)
+            cols = pl.ds(pl.multiple_of((j % across) * wide_cols, 128), wide_cols)
+            return pltpu.make_async_copy(
+                ring.at[j % slots, pl.ds(0, step), pl.ds(0, wide_cols)],
+                terms[kind].at[layer, rows, cols],
+                ring_sem.at[j % slots],
+            )
+
+        def body(j):
+            @pl.when(j >= slots)
+            def _():
+                store(j - slots).wait()
+
+            rows = pl.ds(pl.multiple_of((j // across) * step, step), step)
+            cols = pl.ds(pl.multiple_of((j % across) * wide_cols, 128), wide_cols)
+            ring[j % slots, pl.ds(0, step), pl.ds(0, wide_cols)] = dot_first(
+                left[:, rows], right[:, cols]
+            ).astype(low)
+            store(j).start()
+
+        tiles(count, body)
+        for j in range(max(0, count - slots), count):
+            store(j).wait()
+
+    def count_up(layer, row, value, cols=None):
+        cols = pl.ds(0, value.shape[1]) if cols is None else cols
+        vectors[layer, pl.ds(row, 1), cols] += jnp.sum(value, axis=0, keepdims=True)
+
+    def norm_grad(value, normed, scale_row, gain_row):
+        grad = value * gain_row
+        inner = jnp.mean(grad * normed, axis=-1, keepdims=True)
+        return scale_row * (grad - jnp.mean(grad, axis=-1, keepdims=True) - normed * inner)
+
+    def back_rows(j):
+        return pl.ds(pl.multiple_of(j * chunk, chunk), chunk)
+
+    grad_copy = None
+    cotangent_copy.wait()
+    pumped = 0
+    for layer in reversed(range(dims.layers)):
+        newest = layer == dims.layers - 1
+        if grad_copy is not None:
+            grad_copy.wait_send()
+            settled.append(grad_copy)
+
+        def second_back(j, layer=layer, newest=newest):
+            rows = back_rows(j)
+            value = both_grad[rows].astype(wide) if newest else hidden[rows]
+            normed = norm2[layer, rows]
+            count_up(layer, 7, value * normed)
+            count_up(layer, 8, value)
+            grad = norm_grad(value, normed, rstd[layer, 1, rows, 0:1], small[layer, 6:7, :width])
+            first[rows] = grad
+            rounded = grad.astype(low)
+            both_grad[rows] = rounded
+            count_up(layer, 4, rounded.astype(wide))
+
+        tiles(tokens // chunk, second_back)
+        grad_copy = to_mate(both_grad.at[pl.ds(0, tokens)], both_grad.at[pl.ds(tokens, tokens)])
+        grad_copy.wait_recv()
+
+        weight_terms(layer, 3, act.at[layer], both_grad)
+        if newest:
+            for item in queue[0]:
+                item.reach(1)
+        else:
+            pump(pumped)
+            pumped += 1
+
+        def down_back(j, layer=layer):
+            cols = pl.ds(pl.multiple_of(j * narrow, narrow), narrow)
+            grad = dot_last(both_grad[...], w_down[layer, cols, :])
+            rounded = (grad * slope[layer, :, cols].astype(wide)).astype(low)
+            slope[layer, :, cols] = rounded
+            count_up(layer, 3, rounded.astype(wide), cols)
+
+        tiles(dims.hidden // 2 // narrow, down_back)
+        weight_terms(layer, 2, both_first.at[layer], slope.at[layer])
+        if newest:
+            for item in queue[1]:
+                item.reach(1)
+        else:
+            pump(pumped)
+            pumped += 1
+        exchange_at = 2 * (dims.layers - 1 - layer)
+        project(
+            slope.at[layer],
+            lambda left, cols, layer=layer: dot_last(left, w_up[layer, cols, :]),
+            2 * dims.layers + exchange_at,
+        ).wait_recv()
+        grad_copy.wait_send()
+        settled.append(grad_copy)
+
+        def first_back(j, layer=layer, exchange_at=exchange_at):
+            rows = back_rows(j)
+            value = first[rows] + total[rows] + back[exchange_at, rows].astype(wide)
+            normed = norm1[layer, rows]
+            count_up(layer, 5, value * normed)
+            count_up(layer, 6, value)
+            grad = norm_grad(value, normed, rstd[layer, 0, rows, 0:1], small[layer, 4:5, :width])
+            first[rows] = grad
+            rounded = grad.astype(low)
+            both_grad[rows] = rounded
+            count_up(layer, 2, rounded.astype(wide))
+
+        tiles(tokens // chunk, first_back)
+        grad_copy = to_mate(both_grad.at[pl.ds(0, tokens)], both_grad.at[pl.ds(tokens, tokens)])
+        grad_copy.wait_recv()
+        weight_terms(layer, 1, attended.at[layer], both_grad)
+
+        out_tile = min(256, dims.third)
+
+        def out_back(j, layer=layer):
+            cols = pl.ds(pl.multiple_of(j * out_tile, out_tile), out_tile)
+            attended[layer, :, cols] = dot_last(both_grad[...], w_out[layer, cols, :]).astype(low)
+
+        tiles(dims.third // out_tile, out_back)
+        if not newest:
+            pump(pumped)
+            pumped += 1
+
+        def attend_back(j, layer=layer):
+            s, block = j // lane_blocks, j % lane_blocks
+            rows = pl.ds(pl.multiple_of(s * tokens, tokens), tokens)
+            lanes = pl.ds(pl.multiple_of(block * 128, 128), 128)
+
+            def at(which):
+                return pl.ds(pl.multiple_of(which * dims.third + block * 128, 128), 128)
+
+            query, key_rows, value_rows = (qkv[layer, rows, at(which)] for which in range(3))
+            grad_out = attended[layer, rows, lanes]
+            grads = [[], [], []]
+            for e in range(heads_row):
+                part = slice(e * dims.head_dim, (e + 1) * dims.head_dim)
+                prob = probs[layer, s * (lane_blocks * heads_row) + block * heads_row + e]
+                grads[2].append(dot_first(prob, grad_out[:, part]))
+                prob = prob.astype(wide)
+                grad_prob = dot_last(grad_out[:, part], value_rows[:, part])
+                inner = jnp.sum(prob * grad_prob, axis=1, keepdims=True)
+                grad_score = (prob * (grad_prob - inner)).astype(low)
+                grads[0].append(
+                    jnp.dot(grad_score, key_rows[:, part], preferred_element_type=wide) * scale
+                )
+                grads[1].append(dot_first(grad_score, query[:, part]) * scale)
+            for which, row in ((0, 0), (1, None), (2, 1)):
+                rounded = jnp.concatenate(grads[which], axis=1).astype(low)
+                qkv[layer, rows, at(which)] = rounded
+                if row is not None:
+                    count_up(layer, row, rounded.astype(wide), lanes)
+
+        tiles(2 * lane_blocks, attend_back)
+        weight_terms(layer, 0, both_hidden.at[layer], qkv.at[layer])
+        project(
+            qkv.at[layer],
+            lambda left, cols, layer=layer: dot_last(left, w_qkv[layer, cols, :]),
+            2 * dims.layers + exchange_at + 1,
+        ).wait_recv()
+
+        def input_rows(j, exchange_at=exchange_at):
+            rows = back_rows(j)
+            hidden[rows] = first[rows] + total[rows] + back[exchange_at + 1, rows].astype(wide)
+
+        tiles(tokens // chunk, input_rows)
+        pump(pumped)
+        pumped += 1
+
+    grad_out_copy = pltpu.make_async_copy(hidden, input_grad, io_sem.at[0])
+    grad_out_copy.start()
+    while pumped < len(queue) + stages:
+        pump(pumped)
+        pumped += 1
 
     for copy in exchanges:
-        if not any(copy is other for other in waits[: 2 * dims.layers - 2]):
+        if not any(copy is other for other in settled):
             copy.wait_send()
     for gather in gathers:
         gather.finish_sends()
-    for copy in saves:
-        copy.wait()
-
-
-def run_forward(dims, x, segments, small, weights):
+    for pair in queue:
+        for item in pair:
+            item.finish_sends()
+    grad_out_copy.wait()
+
+
+def run_layers(dims, x, cotangent, segments, small, weights):
     layers, tokens, width = dims.layers, dims.tokens, dims.width
     both = 2 * tokens
-    held = [
-        jax.ShapeDtypeStruct((layers, rows, columns), low) for _, rows, columns, _ in dims.kinds
-    ]
-    states = [
-        ((layers, both, width), low),
-        ((layers, both, 3 * dims.third), low),
-        ((layers, both, dims.third), low),
-        ((layers, HEADS, tokens, tokens), low),
-        ((layers, tokens, width), wide),
-        ((layers, both, width), low),
-        ((layers, both, dims.hidden // 2), low),
-        ((layers, both, dims.hidden // 2), low),
-        ((layers, tokens, width), wide),
-        ((layers, 2, tokens, 128), wide),
-    ]
-    saved = held + [jax.ShapeDtypeStruct(shape, dtype) for shape, dtype in states]
+
+    def shape(dims_of, dtype):
+        return jax.ShapeDtypeStruct(dims_of, dtype)
+
+    held = [shape((layers, rows, columns), low) for _, rows, columns, _ in dims.kinds]
+    pair_rows = [rows * (2 if paired else 1) for rows, _, _, paired in dims.kinds]
+    columns = [kind[2] for kind in dims.kinds]
+    outs = (
+        [
+            shape((tokens, width), low),
+            shape((layers, HEADS // 2, 128), wide),
+            shape((layers, 16, dims.hidden // 2), wide),
+            shape((tokens, width), wide),
+        ]
+        + held * (1 + dims.bits)
+        + [shape((layers, dims.reps // 2, r, c), low) for r, c in zip(pair_rows, columns)]
+        + [shape((layers, r, c), low) for r, c in zip(pair_rows, columns)]
+        + [shape((layers, dims.rows, columns[kind]), low) for kind in (0, 2)]
+    )
     seg = segments.astype(wide)
     seg_row = jnp.broadcast_to(seg, (8, tokens))
     seg_col = jnp.broadcast_to(seg.reshape(tokens, 1), (tokens, 128))
     vmem = pl.BlockSpec(memory_space=pltpu.VMEM)
     anywhere = pl.BlockSpec(memory_space=pl.ANY)
-    outs = [
-        jax.ShapeDtypeStruct((tokens, width), low),
-        jax.ShapeDtypeStruct((layers, HEADS // 2, 128), wide),
-    ] + saved
     dma = pltpu.SemaphoreType.DMA
+    scratch = [pltpu.VMEM(item.shape, item.dtype) for item in held] + [
+        pltpu.VMEM(*item)
+        for item in (
+            ((layers, both, width), low),
+            ((layers, both, 3 * dims.third), low),
+            ((layers, both, dims.third), low),
+            ((layers, HEADS, tokens, tokens), low),
+            ((layers, tokens, width), wide),
+            ((layers, both, width), low),
+            ((layers, both, dims.hidden // 2), low),
+            ((layers, both, dims.hidden // 2), low),
+            ((layers, tokens, width), wide),
+            ((layers, 2, tokens, 128), wide),
+            ((tokens, width), wide),
+            ((tokens, width), wide),
+            ((tokens, width), wide),
+            ((2, tokens, width), low),
+            ((2 * layers, tokens, width), low),
+            ((2, tokens, tokens), wide),
+            ((both, width), low),
+            ((3, 256, 1024), low),
+            ((2, 256, 1024), low),
+            ((2, 256, 1024), low),
+            ((8, tokens), wide),
+            ((tokens, 128), wide),
+        )
+    ]
     slots = 2 + 2 * dims.bits
-    exchange_count = 3 + 4 * layers
-    scratch = (
-        [pltpu.VMEM(item.shape, item.dtype) for item in saved]
-        + [
-            pltpu.VMEM((tokens, width), wide),
-            pltpu.VMEM((tokens, width), wide),
-            pltpu.VMEM((tokens, width), wide),
-            pltpu.VMEM((2, tokens, width), low),
-            pltpu.VMEM((2 * layers, tokens, width), low),
-            pltpu.VMEM((2, tokens, tokens), wide),
-            pltpu.VMEM((8, tokens), wide),
-            pltpu.VMEM((tokens, 128), wide),
-        ]
-        + [
-            dma((4 * layers,)),
-            dma((4 * layers, slots)),
-            dma((4 * layers, slots)),
-            dma((exchange_count,)),
-            dma((exchange_count,)),
-            dma((len(saved) * layers,)),
-        ]
-    )
+    exchange_count = 3 + 8 * layers
+    reduce_slots = dims.bits + dims.reps
+    scratch = scratch + [
+        dma((4 * layers,)),
+        dma((4 * layers, slots)),
+        dma((4 * layers, slots)),
+        dma((exchange_count,)),
+        dma((exchange_count,)),
+        dma((8 * layers, reduce_slots)),
+        dma((8 * layers, reduce_slots)),
+        dma((2, 2)),
+        dma((2,)),
+        dma((3,)),
+        dma((2,)),
+    ]
     return pl.pallas_call(
-        functools.partial(forward_kernel, dims),
+        functools.partial(layers_kernel, dims),
         out_shape=outs,
-        in_specs=[vmem] * 4 + [anywhere] * 4,
-        out_specs=[vmem] * 2 + [anywhere] * len(saved),
+        in_specs=[anywhere] * 2 + [vmem] * 3 + [anywhere] * 4,
+        out_specs=[vmem] * 3 + [anywhere] * (len(outs) - 3),
         scratch_shapes=scratch,
         compiler_params=pltpu.CompilerParams(
-            collective_id=0, has_side_effects=True, vmem_limit_bytes=63 * 2**20
+            collective_id=0, has_side_effects=True, vmem_limit_bytes=63 * 2**20 + 2**19
         ),
-        name="forward",
-    )(x, seg_row, seg_col, small, *weights)
-
-
-def matmul_rows(left, right):
-    return jnp.einsum("ti,to->io", left, right, preferred_element_type=wide).astype(low)
-
-
-def matmul_back(left, right):
-    return jnp.einsum("to,io->ti", left, right, preferred_element_type=wide)
-
-
-def backward_layer(net, grad_out, weights, small, saved):
-    w_qkv, w_out, w_up, w_down = weights
-    gain_first, gain_second = small[4, : grad_out.shape[1]], small[6, : grad_out.shape[1]]
-    both_hidden, qkv, attended, probs, normed_one, both_first, activation, slope, normed_two, rstd = saved
-    rstd_one, rstd_two = rstd[0, :, :1], rstd[1, :, :1]
-    heads = HEADS // 2
-    third = w_qkv.shape[1] // 3
-    scale = 1.0 / math.sqrt(third // heads)
-    grad_gain_second = jnp.sum(grad_out * normed_two, axis=0)
-    grad_shift_second = jnp.sum(grad_out, axis=0)
-    grad_sum_two = norm_back(grad_out * gain_second, normed_two, rstd_two)
-    branch_two = grad_sum_two.astype(low)
-    grad_bias_down = column_sums(branch_two)
-    both_two = net.pair(branch_two)
-    grad_w_down = matmul_rows(activation, both_two)
-    branch_pre = (matmul_back(both_two, w_down) * slope.astype(wide)).astype(low)
-    grad_bias_up = column_sums(branch_pre)
-    grad_w_up = matmul_rows(both_first, branch_pre)
-    grad_first = grad_sum_two + net.join(matmul_back(branch_pre, w_up))
-    grad_gain_first = jnp.sum(grad_first * normed_one, axis=0)
-    grad_shift_first = jnp.sum(grad_first, axis=0)
-    grad_sum_one = norm_back(grad_first * gain_first, normed_one, rstd_one)
-    branch_one = grad_sum_one.astype(low)
-    grad_bias_out = column_sums(branch_one)
-    both_one = net.pair(branch_one)
-    grad_w_out = matmul_rows(attended, both_one)
-    grad_attended = split_heads(matmul_back(both_one, w_out).astype(low), heads)
-    query = split_heads(qkv[:, :third], heads)
-    key_rows = split_heads(qkv[:, third : 2 * third], heads)
-    value_rows = split_heads(qkv[:, 2 * third :], heads)
-    probs = probs.reshape((2, heads) + probs.shape[1:]).astype(wide)
-    grad_value = jnp.einsum(
-        "shqk,sqhd->skhd", probs.astype(low), grad_attended, preferred_element_type=wide
-    )
-    grad_probs = jnp.einsum("sqhd,skhd->shqk", grad_attended, value_rows, preferred_element_type=wide)
-    row_inner = jnp.sum(probs * grad_probs, axis=3, keepdims=True)
-    grad_scores = (probs * (grad_probs - row_inner)).astype(low)
-    grad_query = (
-        jnp.einsum("shqk,skhd->sqhd", grad_scores, key_rows, preferred_element_type=wide) * scale
-    )
-    grad_key = (
-        jnp.einsum("shqk,sqhd->skhd", grad_scores, query, preferred_element_type=wide) * scale
-    )
-    grad_qkv = jnp.concatenate(
-        [part.astype(low).reshape(qkv.shape[0], third) for part in (grad_query, grad_key, grad_value)],
-        axis=1,
-    )
-    grad_bias_query = column_sums(grad_qkv[:, :third])
-    grad_bias_value = column_sums(grad_qkv[:, 2 * third :])
-    grad_w_qkv = matmul_rows(both_hidden, grad_qkv)
-    grad_hidden = grad_sum_one + net.join(matmul_back(grad_qkv, w_qkv))
-    large = []
-    for value, paired in ((grad_w_qkv, True), (grad_w_out, False), (grad_w_up, True), (grad_w_down, False)):
-        columns = value.shape[1]
-        if paired:
-            value = net.rows_by_pair(value.reshape(net.shards, -1, columns))
-        large.append(scatter_weight(net, value.reshape(net.pairs, -1, columns)))
-    owned = (
-        swap_back(large[0], net, 3),
-        large[1],
-        swap_back(large[2], net, 1),
-        large[3],
-    )
-    terms = (
-        grad_bias_query,
-        grad_bias_value,
-        grad_bias_out,
-        grad_bias_up,
-        grad_bias_down,
-        grad_gain_first,
-        grad_shift_first,
-        grad_gain_second,
-        grad_shift_second,
-    )
-    return (grad_hidden, owned, terms)
+        name="layers",
+    )(x, cotangent, seg_row, seg_col, small, *weights)
 
 
 def shards(
@@ -900,15 +1204,16 @@
     small = jnp.stack(
         [jnp.stack([wide_row(row) for row in small_of(layer)]) for layer in range(layer_count)]
     )
-    results = run_forward(
+    results = run_layers(
         dims,
         inputs,
+        cotangent,
         segments,
         small,
         (by_half(w_qkv, net, 3), w_out, by_half(w_up, net, 1), w_down),
     )
-    output, tops = results[0], results[1]
-    weights_all, saved_all = results[2:6], results[6:]
+    output, tops, vector_terms, input_grad = results[:4]
+    done, swapped = results[-6:-2], results[-2:]
 
     local = tops[:, :, 0]
     local = net.in_order(local, net.over_core(local), net.core)
@@ -923,23 +1228,22 @@
         step *= 2
     peak = local
 
-    grad_flow = cotangent.astype(wide)
-    owned_all = [None] * layer_count
-    terms_all = [None] * layer_count
-    for layer_index in reversed(range(layer_count)):
-        grad_flow, owned, terms = backward_layer(
-            net,
-            grad_flow,
-            [weight[layer_index] for weight in weights_all],
-            small[layer_index],
-            [state[layer_index] for state in saved_all],
-        )
-        owned_all[layer_index] = owned
-        terms_all[layer_index] = terms
-    large = tuple(
-        jnp.stack([owned_all[layer_index][member].astype(wide) for layer_index in range(layer_count)])
-        for member in range(4)
+    def own_rows(value):
+        split = value.reshape(layer_count, 2, rows_here, value.shape[2])
+        return lax.dynamic_index_in_dim(split, net.core, 1, keepdims=False)
+
+    large = (
+        whole_columns(own_rows(done[0]), swapped[0], net, 3),
+        done[1].astype(wide),
+        whole_columns(own_rows(done[2]), swapped[1], net, 1),
+        done[3].astype(wide),
     )
+    half_width, half_hidden = width // 2, dims.hidden // 2
+    lengths_here = (half_width, half_width, width, half_hidden) + (width,) * 5
+    terms_all = [
+        [vector_terms[layer, row, :length] for row, length in enumerate(lengths_here)]
+        for layer in range(layer_count)
+    ]
 
     def placed(value, member):
         if member in (0, 1, 3):
@@ -978,7 +1282,7 @@
     start = lax.axis_index("shard") * rows_here
     scale_here = lax.dynamic_slice_in_dim(column_scale, start, rows_here, 1)
     clipped_bias_query = bias_query.astype(wide) * scale_here
-    return (output, grad_flow) + large + tuple(vector_grads) + (clipped_qk, clipped_bias_query)
+    return (output, input_grad) + large + tuple(vector_grads) + (clipped_qk, clipped_bias_query)
 
 
 def solution(mesh):

time: 888 us -> 618 us (0.70); the launches traced: 876 us -> 615 us
  Pallas kernels: 223 us -> 517 us
  waiting for transfers between devices: 220 us -> 20.9 us
  starting transfers between devices: 152 us -> 16.7 us
  local copies, waits for them, and re-layouts: 142 us -> 45.3 us
  other arithmetic: 78.4 us -> 13.8 us
  matrix products: 55.7 us -> 0 us
    pallas_call x1, Pallas kernels: 223 us -> 517 us  [run_layers(): pl.pallas_call(functools.partial(layers_kernel, dims), out_shape=outs, in...]
    ppermute x17 -> x1, waiting for transfers between devices: 135 us -> 6.68 us  [sum_reps(): got = lax.ppermute(total, 'rep', [(i + 1, i), (reps - 2 - i, reps - 1 - i)])]
    ppermute x17 -> x1, starting transfers between devices: 69.1 us -> 3.65 us  [sum_reps(): got = lax.ppermute(total, 'rep', [(i, i + 1), (reps - 1 - i, reps - 2 - i)])]
    ppermute x38 -> x6, waiting for transfers between devices: 61.7 us -> 5.76 us  [over_bit(): lax.ppermute(value, 'shard', [(i, i ^ step) for i in range(self.shards)])]
    dot_general x24 -> x0, matrix products: 55.7 us -> none  [the longest x8 28.1 us: matmul_back(): return jnp.einsum('to,io->ti', left, right, preferred_element_type=wide)]
    convert_element_type x67 -> x5, other arithmetic: 43.7 us -> 8.38 us  [the longest x1 4.12 us: shards(): done[3].astype(wide)]
    ppermute x38 -> x6, starting transfers between devices: 42.2 us -> 9.32 us  [over_bit(): lax.ppermute(value, 'shard', [(i, i ^ step) for i in range(self.shards)])]
    slice x21 -> x1, local copies, waits for them, and re-layouts: 24.4 us -> 1.09 us  [shards(): vector_terms[layer, row, :length]]
  transfers between devices with their start and end apart: 106 -> 14, of which waited for: 32 -> 8; matrix products, arithmetic and copies ran while one was open for 28% -> 7% of each run, Pallas kernels for 0% -> 0%
where the time goes in v3:
time: 618 us; the launch traced here: 615 us
  Pallas kernels  517 us (84%)
  local copies, waits for them, and re-layouts  45.3 us (7%)
  waiting for transfers between devices  20.9 us (3%)
  starting transfers between devices  16.7 us (3%)
  other arithmetic  13.8 us (2%)
    pallas_call x1, Pallas kernels, run_layers(): pl.pallas_call(functools.partial(layers_kernel, dims), out_shape=outs, in...  517 us
    unnamed x31, local copies, waits for them, and re-layouts  18 us
  transfers between devices with their start and end apart: 14, of which 8 were waited for; matrix products, arithmetic and copies ran while one was open for 7% of the time, Pallas kernels for 0%

profile of v3, /device:TPU:0, one launch (start us, length us, event | category | flops | bytes accessed | tf_op | source)
XLA Modules:
  0.0 615.2 jit_solution(18209027286612946489)
XLA Ops:
  0.7 0.7 constant_dynamic-update-slice_fusion.8
  1.3 0.7 constant_dynamic-update-slice_fusion.7
  2.0 0.7 constant_dynamic-update-slice_fusion.6
  2.6 0.7 constant_dynamic-update-slice_fusion.5
  3.3 0.7 constant_dynamic-update-slice_fusion.4
  4.0 0.7 constant_dynamic-update-slice_fusion.3
  4.7 0.7 constant_dynamic-update-slice_fusion.2
  5.3 0.7 constant_dynamic-update-slice_fusion.1
  6.0 0.7 constant_dynamic-update-slice_fusion
  6.6 0.5 collective-permute-start
  7.1 0.8 collective-permute-done
  8.0 2.9 collective-permute-start.1
  10.9 1.7 collective-permute-done.1
  12.6 2.1 collective-permute-start.2
  14.7 0.7 convert_element_type.177
  15.4 4.5 reshape.545
  19.9 2.4 copy.298
  22.3 2.8 reshape.546.refs_7_
  25.1 1.9 copy.223
  27.1 1.6 copy.226.refs_5_
  29.6 0.7 pad_maximum_fusion.refs_4_
  30.2 0.8 broadcast_in_dim.18.refs_3_
  31.0 0.6 broadcast_in_dim.17.refs_2_
  31.6 517.2 %layers.1 = (bf16[256,1024]{1,0:T(8,128)(2,1)}, f32[2,8,128]{2,1,0:T(8,128)}, f32[2,16,2048]{2,1,0:T(8,128)}, f32[256,1024]{1,0:T(8,128)}, bf16[2,1024,1536]{2,1...) custom-call(bf16[256,1024]{1,0:T(8,128)(2,1)} %refs_0_.1, ...), custom_call_target="tpu_custom_call" | custom-call | tf_op jit(solution)/shard_map/layers/pallas_call | solution.py:1122
  548.8 0.9 broadcast_select_fusion.9
  549.8 0.8 fusion.16
  550.6 1.1 fusion.20
  551.7 0.8 slice_reduce_fusion
  552.4 0.5 collective-permute-start.9
  553.5 1.3 constant_dynamic-slice_fusion.1
  554.9 0.7 copy.278
  555.5 0.5 copy.231
  556.1 0.8 reshape.552
  556.9 0.2 broadcast_select_fusion.1
  557.1 2.3 maximum_convert_fusion
  559.4 5.2 copy.235
  564.7 5.6 copy.262
  570.3 1.3 constant_dynamic-slice_fusion.2
  571.5 0.4 copy.277
  571.9 0.4 copy.228
  572.4 0.2 maximum_convert_fusion.1
  572.8 2.4 copy.261
  575.2 4.1 convert_element_type.207
  579.6 1.2 collective-permute-start.4
  580.8 0.9 collective-permute-start.10
  581.8 1.1 convert_element_type.204
  582.9 1.5 collective-permute-done.10
  584.4 1.0 collective-permute-start.11
  585.5 2.5 collective-permute-done.11
  588.0 3.6 collective-permute-done.12
  591.6 0.6 collective-permute-start.13
  592.2 1.2 collective-permute-start.5
  593.4 2.7 collective-permute-done.13
  596.2 3.7 collective-permute-start.6
  599.9 1.4 collective-permute-done.6
  601.3 0.8 collective-permute-start.7
  602.1 1.6 convert_multiply_fusion
  603.7 1.3 collective-permute-start.8
  605.0 0.6 fusion.18
  605.6 6.7 %collective-permute-done.8 = f32[2,12,128]{2,0,1:T(2,128)S(1)} collective-permute-done((f32[2,12,128]{2,0,1:T(2,128)S(1)}, f32[2,12,128]{2,0,1:T(2,128)S(1)}, u32[]{:S(2)}, u32[]{:S(2)}) %collective-permute-start.8) | collective-permute-done | bytes 12320 | tf_op jit(solution)/shard_map/ppermute | solution.py:95
  612.3 0.6 slice_bitcast_fusion.1
  612.9 0.6 slice_bitcast_fusion
  613.5 0.8 copy.310
  614.3 1.0 copy.311
  (109 shorter events, 2.2 us)
Async XLA Ops:
  6.6 1.3 collective-permute-start
  8.0 4.6 collective-permute-start.1
  12.6 16.1 %collective-permute-start.2 = (bf16[2,2,2,12,128]{4,2,3,1,0:T(2,128)(2,1)S(1)}, bf16[2,2,2,12,128]{4,2,3,1,0:T(2,128)(2,1)S(1)}, u32[]{:S(2)}, u32[]{:S(2)}) collective-permute-start(bf16[2,2,2,12,128]{4,2,3,1,0:T(2,128)(2,1)S(1)} %pad_maximum_fusion.2), channel_id=1, source_target_pairs={{0,4},{1,5},{2,6},{3,7},{4,0},{5,1},{6,2},{7,3},{8,12},{9,13},{10,... | collective-permute-start | bytes 73736 | tf_op jit(solution)/shard_map/ppermute | solution.py:41
  552.4 26.9 %collective-permute-start.9 = (f32[2,8]{1,0:T(2,128)S(1)}, f32[2,8]{1,0:T(2,128)S(1)}, u32[]{:S(2)}, u32[]{:S(2)}) collective-permute-start(f32[2,8]{1,0:T(2,128)S(1)} %slice_reduce_fusion), channel_id=1, source_target_pairs={{0,1},{1,0},{2,3},{3,2},{4,5},{5,4},{6,7},{7,6},{8,9},{9,8},{10,11... | collective-permute-start | bytes 200 | tf_op jit(solution)/shard_map/ppermute | solution.py:34
  553.5 26.0 %collective-permute-start.3 = (f32[4,1,2,12,128]{4,2,3,0,1:T(2,128)S(1)}, f32[4,1,2,12,128]{4,2,3,0,1:T(2,128)S(1)}, u32[]{:S(2)}, u32[]{:S(2)}) collective-permute-start(f32[4,1,2,12,128]{4,2,3,0,1:T(2,128)S(1)} %bitcast.209), channel_id=1, source_target_pairs={{0,1},{1,0},{2,3},{3,2},{4,5},{5,4},{6,7},{7,6},{8,9},{9,8},{10,11... | collective-permute-start | bytes 147464 | tf_op jit(solution)/shard_map/ppermute | solution.py:34
  554.9 1.2 copy-start.2
  570.3 1.6 copy-start.3
  575.2 6.6 %copy-start.4 = (bf16[2,128,1024]{2,1,0:T(8,128)(2,1)S(1)}, bf16[2,128,1024]{2,1,0:T(8,128)(2,1)}, u32[]{:S(2)}) copy-start(bf16[2,128,1024]{2,1,0:T(8,128)(2,1)} %get-tuple-element.31) | copy-start | bytes 1572868
  575.2 20.8 %copy-start.6 = (f32[2,16]{1,0:T(2,128)S(1)}, f32[2,16]{1,0:T(2,128)}, u32[]{:S(2)}) copy-start(f32[2,16]{1,0:T(2,128)} %param.33) | copy-start | bytes 388
  579.3 22.8 %copy-start = (bf16[2,128,3072]{2,1,0:T(8,128)(2,1)S(1)}, bf16[2,128,3072]{2,1,0:T(8,128)(2,1)}, u32[]{:S(2)}) copy-start(bf16[2,128,3072]{2,1,0:T(8,128)(2,1)} %param.20) | copy-start | bytes 4718596
  579.6 12.6 %collective-permute-start.4 = (f32[2,2,12,128]{3,1,2,0:T(2,128)S(1)}, f32[2,2,12,128]{3,1,2,0:T(2,128)S(1)}, u32[]{:S(2)}, u32[]{:S(2)}) collective-permute-start(f32[2,2,12,128]{3,1,2,0:T(2,128)S(1)} %dynamic-slice_bitcast_fusion), channel_id=1, source_target_pairs={{0,2},{1,3},{2,0},{3,1},{4,6},{5,7},{6,4},{7,5},{8,10},{9,11},{10,... | collective-permute-start | bytes 73736 | tf_op jit(solution)/shard_map/ppermute | solution.py:41
  580.8 3.6 collective-permute-start.10
  582.9 22.1 %copy-start.7 = (bf16[2,128]{1,0:T(2,128)(2,1)S(1)}, bf16[2,128]{1,0:T(2,128)(2,1)}, u32[]{:S(2)}) copy-start(bf16[2,128]{1,0:T(2,128)(2,1)} %param.24) | copy-start | bytes 1540
  582.9 30.6 %copy-start.5 = (bf16[256,1024]{1,0:T(8,128)(2,1)S(1)}, bf16[256,1024]{1,0:T(8,128)(2,1)}, u32[]{:S(2)}) copy-start(bf16[256,1024]{1,0:T(8,128)(2,1)} %get-tuple-element.189) | copy-start | bytes 1572868
  584.4 3.6 collective-permute-start.11
  588.0 3.6 collective-permute-start.12
  591.6 4.5 collective-permute-start.13
  592.2 4.0 collective-permute-start.5
  596.2 5.0 collective-permute-start.6
  601.3 13.0 %copy-start.1 = (f32[256,1024]{1,0:T(8,128)S(1)}, f32[256,1024]{1,0:T(8,128)}, u32[]{:S(2)}) copy-start(f32[256,1024]{1,0:T(8,128)} %get-tuple-element.190) | copy-start | bytes 3145732
  601.3 2.4 collective-permute-start.7
  603.7 8.6 %collective-permute-start.8 = (f32[2,12,128]{2,0,1:T(2,128)S(1)}, f32[2,12,128]{2,0,1:T(2,128)S(1)}, u32[]{:S(2)}, u32[]{:S(2)}) collective-permute-start(f32[2,12,128]{2,0,1:T(2,128)S(1)} %add.110), channel_id=1, source_target_pairs={{8,0},{16,24},{9,1},{17,25},{10,2},{18,26},{11,3},{19,27},{12,4},{... | collective-permute-start | bytes 36872 | tf_op jit(solution)/shard_map/ppermute | solution.py:95

commit v4 on v3

--- a/solution.py
+++ b/solution.py
@@ -10,6 +10,7 @@
 
 HEADS = 16
 MESH = pl.DeviceIdType.MESH
+LEAD = 0
 
 
 epsilon = 1e-05
@@ -159,6 +160,12 @@
             (self.rows, width, hidden // 2, True),
             (hidden // shards, hidden // 2, width, False),
         )
+        high = shards // (2 * step)
+        self.block = (width // (2 * high), None, hidden // (2 * high), None)
+        self.blocks = (3 * high, None, high, None)
+        self.lengths = (1, 1, 1, hidden // width, 1, 1, 1, 1, 1)
+        self.vector_rows = layers * sum(self.lengths)
+        self.direct = self.rows % 128 == 0 and step == 1
 
 
 def remote(src, dst, send, recv, where):
@@ -213,21 +220,40 @@
         if self.paired:
             mine = place.me * self.rows
             rows = pl.ds(pl.multiple_of(mine, 16), self.rows)
-            pltpu.make_async_copy(
-                self.source.at[self.layer, place.half], self.whole.at[self.layer, rows], self.local.at[self.at]
-            ).start()
-            remote(
-                self.source.at[self.layer, 1 - place.half],
-                self.whole.at[self.layer, rows],
-                self.send.at[self.at, 0],
-                self.recv.at[self.at, 0],
-                place.mate(),
-            ).start()
+            for theirs, ours in self.begin_blocks():
+                pltpu.make_async_copy(
+                    ours, self.whole.at[self.layer, rows, theirs[1]], self.local.at[self.at]
+                ).start()
+            for theirs, ours in self.begin_blocks():
+                remote(
+                    theirs[0],
+                    self.whole.at[self.layer, rows, theirs[1]],
+                    self.send.at[self.at, 0],
+                    self.recv.at[self.at, 0],
+                    place.mate(),
+                ).start()
         else:
             rows = pl.ds(pl.multiple_of(place.pair * self.rows, 16), self.rows)
             pltpu.make_async_copy(
                 self.source.at[self.layer], self.whole.at[self.layer, rows], self.local.at[self.at]
             ).start()
+
+    def begin_blocks(self):
+        place, width = self.place, self.dims.block[self.kind]
+        if not self.dims.direct:
+            every = pl.ds(0, self.columns)
+            yield (
+                (self.source.at[self.layer, 1 - place.half], every),
+                self.source.at[self.layer, place.half],
+            )
+            return
+        for block in range(self.dims.blocks[self.kind]):
+            to = pl.ds(block * width, width)
+            starts = [(2 * block + half) * width for half in (1 - place.half, place.half)]
+            theirs, ours = (
+                self.source.at[self.layer, :, pl.ds(pl.multiple_of(start, 128), width)] for start in starts
+            )
+            yield (theirs, to), ours
 
     def some(self, rows, columns):
         return self.whole.at[self.layer, pl.ds(0, rows), columns]
@@ -315,7 +341,7 @@
         self.place, self.dims = place, place.dims
         self.layer, self.kind, self.part = layer, kind, part
         self.terms, self.arrived, self.lines, self.done, self.swapped = terms, arrived, lines, done, swapped
-        self.send, self.recv = sems
+        self.send, self.recv, self.own_sem = sems
         self.mine, self.other, self.load_sem, self.store_sem = bufs
         self.rows, self.held, self.columns, self.paired = self.dims.kinds[kind]
         self.size = self.columns // 2
@@ -495,18 +521,50 @@
                     self.own if move < half - 1 else self.final,
                 )
 
-    def swap_copy(self):
-        rows = self.done.at[
-            self.layer,
-            pl.ds(pl.multiple_of((1 - self.place.half) * self.rows, 16), self.rows),
-            self.columns_here,
-        ]
-        return remote(
-            rows,
-            self.swapped.at[self.layer, pl.ds(0, self.rows), self.columns_here],
-            *self.sems(self.dims.bits + self.moves),
-            self.place.mate(),
-        )
+    def part_blocks(self):
+        width = self.dims.block[self.kind]
+        count = self.dims.blocks[self.kind] // 2
+        for block in range(self.part * count, (self.part + 1) * count):
+            place = (2 * block + self.place.half) * width
+            yield pl.ds(block * width, width), pl.ds(pl.multiple_of(place, 128), width)
+
+    def rows_done(self, half, columns):
+        start = pl.multiple_of(half * self.rows, 16)
+        return self.done.at[self.layer, pl.ds(start, self.rows), columns]
+
+    def start_swap(self):
+        slot = self.sems(self.dims.bits + self.moves)
+        if not self.dims.direct:
+            remote(
+                self.rows_done(1 - self.place.half, self.columns_here),
+                self.swapped.at[self.layer, pl.ds(0, self.rows), self.columns_here],
+                *slot,
+                self.place.mate(),
+            ).start()
+            return
+        for here, there in self.part_blocks():
+            remote(
+                self.rows_done(1 - self.place.half, here),
+                self.swapped.at[self.layer, pl.ds(0, self.rows), there],
+                *slot,
+                self.place.mate(),
+            ).start()
+        for here, there in self.part_blocks():
+            pltpu.make_async_copy(
+                self.rows_done(self.place.half, here),
+                self.swapped.at[self.layer, pl.ds(0, self.rows), there],
+                self.own_sem.at[self.at],
+            ).start()
+
+    def swap_bytes(self):
+        ref = self.done.at[self.layer, pl.ds(0, self.rows), self.columns_here]
+        return remote(ref, ref, *self.sems(self.dims.bits + self.moves), self.place.mate())
+
+    def finish_swap(self):
+        self.swap_bytes().wait_recv()
+        if self.dims.direct:
+            ref = self.done.at[self.layer, pl.ds(0, self.rows), self.columns_here]
+            pltpu.make_async_copy(ref, ref, self.own_sem.at[self.at]).wait()
 
     def advance(self):
         bits = self.dims.bits
@@ -524,9 +582,9 @@
         elif self.stage == bits + self.moves:
             self.finish_move(self.moves - 1)
             if self.paired:
-                self.swap_copy().start()
+                self.start_swap()
         else:
-            self.swap_copy().wait_recv()
+            self.finish_swap()
         self.stage += 1
 
     def reach(self, stage):
@@ -544,7 +602,7 @@
                 self.move_bytes(move).wait_send()
 
         if self.paired:
-            self.swap_copy().wait_send()
+            self.swap_bytes().wait_send()
 
 
 def when(condition):
@@ -561,6 +619,14 @@
     return {12: 8, 8: 6, 16: 10}.get(blocks, blocks - blocks // 3) * 128
 
 
+def few(count, body):
+    if count <= 8:
+        for index in range(count):
+            body(index)
+    else:
+        tiles(count, body)
+
+
 def gelu_and_slope(pre):
     cdf = 0.5 * (1.0 + lax.erf(pre * (1.0 / math.sqrt(2.0))))
     slope = cdf + pre * jnp.exp(-0.5 * pre * pre) * (1.0 / math.sqrt(2.0 * math.pi))
@@ -589,9 +655,10 @@
     def take(count):
         return [next(refs) for _ in range(count)]
 
-    x_ref, cotangent, seg_row, seg_col, small = take(5)
+    x_ref, cotangent, seg_row, vector_ref = take(4)
     src_qkv, src_out, src_up, src_down = take(4)
     output, tops, vectors, input_grad = take(4)
+    vector_out, peak_out = take(2) if dims.direct else (None, None)
     terms = take(4)
     arrived = [take(4) for _ in range(dims.bits)]
     lines, done = take(4), take(4)
@@ -599,22 +666,34 @@
     w_qkv, w_out, w_up, w_down = take(4)
     both_hidden, qkv, attended, probs, norm1, both_first, act, slope, norm2, rstd = take(10)
     hidden, first, total, away, back, bias, both_grad, ring, add_mine, add_other = take(10)
-    seg_rows, seg_cols = take(2)
+    seg_here, seg_rows = take(2)
+    if dims.direct:
+        vector_all, small, vector_away, vector_back, line_back = take(5)
+    else:
+        small = vector_ref
     gather_local, gather_send, gather_recv, mate_send, mate_recv = take(5)
-    reduce_send, reduce_recv, load_sem, store_sem, ring_sem, io_sem = take(6)
+    reduce_send, reduce_recv, own_sem, load_sem, store_sem, ring_sem, io_sem = take(7)
+    if dims.direct:
+        vector_send, vector_recv = take(2)
     place = Place(dims)
     tokens, width = dims.tokens, dims.width
     heads_row = 128 // dims.head_dim
     scale = 1.0 / math.sqrt(dims.head_dim)
 
     barrier = pltpu.get_barrier_semaphore()
-    others = [place.mate()] + [place.over_bit(bit) for bit in range(dims.bits)]
-    reps = dims.reps
-    groups = sorted({1 % reps, (reps - 1) % reps} - {0})
-    others += [((place.rep + step) % reps, place.me) for step in groups]
-    for other in others:
-        pl.semaphore_signal(barrier, 1, device_id=other, device_id_type=MESH)
-    pl.semaphore_wait(barrier, len(others))
+    reps, shards = dims.reps, dims.shards
+
+    def in_group(step):
+        return place.rep, (place.me + step) % shards
+
+    def greet(step):
+        pl.semaphore_signal(barrier, 1, device_id=in_group(step), device_id_type=MESH)
+
+    few(shards - 1, lambda index: greet(index + 1))
+    for step in range(1, reps):
+        line = (place.rep + step) % reps, place.me
+        pl.semaphore_signal(barrier, 1, device_id=line, device_id_type=MESH)
+    pl.semaphore_wait(barrier, shards + reps - 2)
 
     sources = (src_qkv, src_out, src_up, src_down)
     wholes = (w_qkv, w_out, w_up, w_down)
@@ -641,8 +720,26 @@
         exchanges.append(copy)
         return copy
 
-    rows_copy = to_mate(seg_row, seg_rows)
-    cols_copy = to_mate(seg_col, seg_cols)
+    seg_here[...] = jnp.broadcast_to(seg_row[...].astype(wide), seg_here.shape)
+    rows_copy = to_mate(seg_here, seg_rows)
+
+    def vector_bytes(buffer, slot, count):
+        ref = buffer.at[pl.ds(0, count)]
+        return remote(ref, ref, vector_send.at[slot], vector_recv.at[slot], place.mate())
+
+    if dims.direct:
+
+        def send_vector(index):
+            remote(
+                vector_ref,
+                vector_all.at[place.me],
+                vector_send.at[0],
+                vector_recv.at[0],
+                in_group(index + 1),
+            ).start()
+
+        vector_all[place.me] = vector_ref[...]
+        few(shards - 1, send_vector)
     x_copy = pltpu.make_async_copy(x_ref, both_hidden.at[0, pl.ds(0, tokens)], io_sem.at[0])
     cotangent_copy = pltpu.make_async_copy(cotangent, both_grad.at[pl.ds(0, tokens)], io_sem.at[1])
     x_copy.start()
@@ -651,23 +748,45 @@
     hidden_copy = to_mate(both_hidden.at[0, pl.ds(0, tokens)], both_hidden.at[0, pl.ds(tokens, tokens)])
     for gather in gathers:
         gather.begin()
-    for gather in gathers[:3]:
-        gather.reach(1)
+    turns = []
 
     def prepare(at):
-        for ahead in reversed(range(1, dims.bits + 2)):
-            if at + ahead < len(gathers):
-                gathers[at + ahead].reach(max(1, gathers[at + ahead].stages - ahead))
-        gathers[at].reach(gathers[at].stages)
+        while len(turns) < at + gathers[at].stages:
+            now = len(turns)
+            turns.append(now)
+            for number, gather in enumerate(gathers):
+                gather.reach(max(now - number + 1, 1 if number <= now + LEAD else 0))
 
     hidden[...] = both_hidden[0, pl.ds(0, tokens)].astype(wide)
     vectors[...] = jnp.zeros(vectors.shape, wide)
     tops[...] = jnp.full(tops.shape, neg_large, wide)
     rows_copy.wait_recv()
-    cols_copy.wait_recv()
-    for s, (row_ref, col_ref) in enumerate(((seg_row, seg_col), (seg_rows, seg_cols))):
-        same = col_ref[:, 0:1] == row_ref[0:1, :]
-        bias[s] = jnp.where(same, 0.0, neg_large)
+    for s, row_ref in enumerate((seg_here, seg_rows)):
+        row = row_ref[0:1, :]
+        column = jnp.broadcast_to(row, (128, tokens)).T[:, 0:1]
+        bias[s] = jnp.where(column == row, 0.0, neg_large)
+
+    if dims.direct:
+        vector_bytes(vector_all, 0, shards - 1).wait_recv()
+        starts = [sum(dims.lengths[:member]) for member in range(9)]
+        small[...] = jnp.zeros(small.shape, wide)
+        for layer in range(dims.layers):
+            base = layer * sum(dims.lengths)
+
+            def spread(row, member, shard, at, layer=layer, base=base):
+                for block in range(dims.lengths[member]):
+                    lanes = pl.ds(at + block * dims.rows, dims.rows)
+                    source = base + starts[member] + block
+                    small[layer, row : row + 1, lanes] = vector_all[shard, source : source + 1, :]
+
+            for shard in range(shards):
+                for row, member in ((1, 2), (3, 4), (4, 5), (5, 6), (6, 7), (7, 8)):
+                    spread(row, member, shard, shard * dims.rows)
+            for pair in range(dims.pairs):
+                shard = 2 * pair + place.half
+                spread(0, 0, shard, pair * dims.rows)
+                spread(0, 1, shard, 2 * dims.third + pair * dims.rows)
+                spread(2, 3, shard, pair * dims.rows * dims.lengths[3])
 
     chunk = 32 if tokens % 32 == 0 else tokens
 
@@ -833,7 +952,7 @@
                 lines[kind],
                 done[kind],
                 swapped[kind // 2],
-                (reduce_send, reduce_recv),
+                (reduce_send, reduce_recv, own_sem),
                 (add_mine, add_other, load_sem, store_sem),
             )
             for part in range(2)
@@ -1033,13 +1152,83 @@
 
     grad_out_copy = pltpu.make_async_copy(hidden, input_grad, io_sem.at[0])
     grad_out_copy.start()
+
+    if dims.direct:
+        count = dims.vector_rows
+        for shard in range(shards):
+            for layer in range(dims.layers):
+                at = layer * sum(dims.lengths)
+                for member, length in enumerate(dims.lengths):
+                    halved = member in (0, 1, 3)
+                    for block in range(length):
+                        first_lane = (shard // 2 if halved else shard) * length * dims.rows
+                        lanes = pl.ds(first_lane + block * dims.rows, dims.rows)
+                        value = vectors[layer, member : member + 1, lanes]
+                        if halved:
+                            value = jnp.where(place.half == shard % 2, value, 0.0)
+                        vector_away[shard, at : at + 1, :] = value
+                        at += 1
+                heads = HEADS // 2
+                vector_away[shard, pl.ds(count + layer * heads, heads)] = tops[layer]
+        vector_back[place.me] = vector_away[place.me]
+
+        def send_terms(index):
+            target = in_group(index + 1)
+            remote(
+                vector_away.at[target[1]],
+                vector_back.at[place.me],
+                vector_send.at[1],
+                vector_recv.at[1],
+                target,
+            ).start()
+
+        few(shards - 1, send_terms)
+    gathered = pumped + 1
     while pumped < len(queue) + stages:
         pump(pumped)
         pumped += 1
+        if dims.direct and pumped == gathered:
+            vector_bytes(vector_back, 1, shards - 1).wait_recv()
+            total_rows = vector_back[0, pl.ds(0, count)]
+            for shard in range(1, shards):
+                total_rows = total_rows + vector_back[shard, pl.ds(0, count)]
+            vector_out[...] = total_rows
+            heads = dims.layers * HEADS // 2
+            for half in range(2):
+                peak = vector_back[half, pl.ds(count, heads)]
+                for shard in range(2 + half, shards, 2):
+                    peak = jnp.maximum(peak, vector_back[shard, pl.ds(count, heads)])
+                peak_out[half] = peak
+            line_back[place.rep, pl.ds(0, count)] = vector_out[...]
+            for half in range(2):
+                line_back[place.rep, pl.ds(count + half * heads, heads)] = peak_out[half]
+            for step in range(1, reps):
+                remote(
+                    line_back.at[place.rep],
+                    line_back.at[place.rep],
+                    vector_send.at[2],
+                    vector_recv.at[2],
+                    ((place.rep + step) % reps, place.me),
+                ).start()
+    if dims.direct:
+        vector_bytes(line_back, 2, reps - 1).wait_recv()
+        total_rows = line_back[0, pl.ds(0, count)]
+        for other in range(1, reps):
+            total_rows = total_rows + line_back[other, pl.ds(0, count)]
+        vector_out[...] = total_rows
+        for half in range(2):
+            peak = line_back[0, pl.ds(count + half * heads, heads)]
+            for other in range(1, reps):
+                peak = jnp.maximum(peak, line_back[other, pl.ds(count + half * heads, heads)])
+            peak_out[half] = peak
 
     for copy in exchanges:
         if not any(copy is other for other in settled):
             copy.wait_send()
+    if dims.direct:
+        vector_bytes(vector_all, 0, shards - 1).wait_send()
+        vector_bytes(vector_back, 1, shards - 1).wait_send()
+        vector_bytes(line_back, 2, reps - 1).wait_send()
     for gather in gathers:
         gather.finish_sends()
     for pair in queue:
@@ -1048,7 +1237,7 @@
     grad_out_copy.wait()
 
 
-def run_layers(dims, x, cotangent, segments, small, weights):
+def run_layers(dims, x, cotangent, segments, vectors, weights):
     layers, tokens, width = dims.layers, dims.tokens, dims.width
     both = 2 * tokens
 
@@ -1058,6 +1247,13 @@
     held = [shape((layers, rows, columns), low) for _, rows, columns, _ in dims.kinds]
     pair_rows = [rows * (2 if paired else 1) for rows, _, _, paired in dims.kinds]
     columns = [kind[2] for kind in dims.kinds]
+    heads = HEADS // 2
+    summed = []
+    if dims.direct:
+        summed = [
+            shape((dims.vector_rows, dims.rows), wide),
+            shape((2, layers * heads, 128), wide),
+        ]
     outs = (
         [
             shape((tokens, width), low),
@@ -1065,14 +1261,15 @@
             shape((layers, 16, dims.hidden // 2), wide),
             shape((tokens, width), wide),
         ]
+        + summed
         + held * (1 + dims.bits)
         + [shape((layers, dims.reps // 2, r, c), low) for r, c in zip(pair_rows, columns)]
         + [shape((layers, r, c), low) for r, c in zip(pair_rows, columns)]
-        + [shape((layers, dims.rows, columns[kind]), low) for kind in (0, 2)]
+        + [
+            shape((layers, dims.rows, columns[kind] * (2 if dims.direct else 1)), low)
+            for kind in (0, 2)
+        ]
     )
-    seg = segments.astype(wide)
-    seg_row = jnp.broadcast_to(seg, (8, tokens))
-    seg_col = jnp.broadcast_to(seg.reshape(tokens, 1), (tokens, 128))
     vmem = pl.BlockSpec(memory_space=pltpu.VMEM)
     anywhere = pl.BlockSpec(memory_space=pl.ANY)
     dma = pltpu.SemaphoreType.DMA
@@ -1100,11 +1297,23 @@
             ((2, 256, 1024), low),
             ((2, 256, 1024), low),
             ((8, tokens), wide),
-            ((tokens, 128), wide),
+            ((8, tokens), wide),
         )
     ]
+    if dims.direct:
+        rows = dims.vector_rows
+        scratch += [
+            pltpu.VMEM(item, wide)
+            for item in (
+                (dims.shards, rows, dims.rows),
+                (layers, 8, dims.hidden // 2),
+                (dims.shards, rows + layers * heads, dims.rows),
+                (dims.shards, rows + layers * heads, dims.rows),
+                (dims.reps, rows + 2 * layers * heads, dims.rows),
+            )
+        ]
     slots = 2 + 2 * dims.bits
-    exchange_count = 3 + 8 * layers
+    exchange_count = 2 + 8 * layers
     reduce_slots = dims.bits + dims.reps
     scratch = scratch + [
         dma((4 * layers,)),
@@ -1114,22 +1323,101 @@
         dma((exchange_count,)),
         dma((8 * layers, reduce_slots)),
         dma((8 * layers, reduce_slots)),
+        dma((8 * layers,)),
         dma((2, 2)),
         dma((2,)),
         dma((3,)),
         dma((2,)),
     ]
+    if dims.direct:
+        scratch += [dma((3,)), dma((3,))]
     return pl.pallas_call(
         functools.partial(layers_kernel, dims),
         out_shape=outs,
-        in_specs=[anywhere] * 2 + [vmem] * 3 + [anywhere] * 4,
-        out_specs=[vmem] * 3 + [anywhere] * (len(outs) - 3),
+        in_specs=[anywhere] * 2 + [vmem] * 2 + [anywhere] * 4,
+        out_specs=[vmem] * 3 + [anywhere] + [vmem] * len(summed) + [anywhere] * (len(outs) - 4 - len(summed)),
         scratch_shapes=scratch,
         compiler_params=pltpu.CompilerParams(
             collective_id=0, has_side_effects=True, vmem_limit_bytes=63 * 2**20 + 2**19
         ),
         name="layers",
-    )(x, cotangent, seg_row, seg_col, small, *weights)
+    )(x, cotangent, segments, vectors, *weights)
+
+
+def own_rows(net, value):
+    layers, rows, columns = value.shape
+    split = value.reshape(layers, 2, rows // 2, columns)
+    return lax.dynamic_index_in_dim(split, net.core, 1, keepdims=False)
+
+
+def gathered_vectors(net, dims, packed):
+    lengths = dims.lengths
+    packed = net.in_order(packed, net.over_core(packed), net.core)
+    packed = net.rows_in_order(net.gather_chips(packed, list(range(net.bits))))
+
+    def whole(layer, member):
+        start = sum(lengths[:member])
+        return packed[:, layer, start : start + lengths[member]].astype(wide)
+
+    def of_core(layer, member):
+        split = whole(layer, member).reshape(net.high, 2, -1)
+        return lax.dynamic_index_in_dim(split, net.core, 1, keepdims=False).reshape(-1)
+
+    def wide_row(row):
+        return jnp.pad(row, (0, dims.hidden // 2 - row.shape[0]))
+
+    def rows(layer):
+        bias_q = of_core(layer, 0)
+        bias_qkv = jnp.concatenate([bias_q, jnp.zeros_like(bias_q), of_core(layer, 1)])
+        singles = [whole(layer, member).reshape(-1) for member in (2, 4, 5, 6, 7, 8)]
+        return [bias_qkv, singles[0], of_core(layer, 3)] + singles[1:]
+
+    return jnp.stack(
+        [jnp.stack([wide_row(row) for row in rows(layer)]) for layer in range(dims.layers)]
+    )
+
+
+def summed_vectors(net, dims, vectors, tops):
+    layers, lengths, rows = dims.layers, dims.lengths, dims.rows
+    half_width, half_hidden = dims.third, dims.hidden // 2
+    here = (half_width, half_width, dims.width, half_hidden) + (dims.width,) * 5
+
+    def placed(value, member):
+        if member in (0, 1, 3):
+            value = value.reshape(net.high, 1, net.step, lengths[member], rows)
+            zero = jnp.zeros_like(value)
+            first = net.core == 0
+            return jnp.concatenate(
+                [jnp.where(first, value, zero), jnp.where(first, zero, value)], axis=1
+            )
+        return value.reshape(net.high, 2, net.step, lengths[member], rows)
+
+    terms = jnp.stack(
+        [
+            jnp.concatenate(
+                [placed(vectors[layer, row, :size], row) for row, size in enumerate(here)], axis=3
+            )
+            for layer in range(layers)
+        ],
+        axis=3,
+    )
+    theirs = lax.dynamic_index_in_dim(terms, 1 - net.core, 1, keepdims=False)
+    ours = lax.dynamic_index_in_dim(terms, net.core, 1, keepdims=False)
+    terms = ours + net.over_core(theirs)
+    terms = terms.reshape((net.pairs,) + terms.shape[2:])
+    terms = net.sum_reps(net.scatter_chips(terms, list(range(net.bits))))
+
+    local = tops[:, :, 0]
+    local = net.in_order(local, net.over_core(local), net.core)
+    local = local.reshape(2, layers, net.high, -1).transpose(1, 2, 0, 3).reshape(layers, HEADS)
+    for bit in range(net.bits):
+        local = jnp.maximum(local, net.over_bit(local, bit))
+    step = 1
+    while step < net.reps:
+        swap = [(i, i ^ step) for i in range(net.reps)]
+        local = jnp.maximum(local, lax.ppermute(local, "rep", swap))
+        step *= 2
+    return terms, local
 
 
 def shards(
@@ -1175,106 +1463,34 @@
     packed = jnp.concatenate(
         [vector.reshape(layer_count, -1, rows_here) for vector in vectors], axis=1
     )
-    packed = net.in_order(packed, net.over_core(packed), net.core)
-    packed = net.rows_in_order(net.gather_chips(packed, list(range(net.bits))))
-
-    def whole(layer_index, member):
-        start = sum(lengths[:member])
-        return packed[:, layer_index, start : start + lengths[member]].astype(wide)
-
-    def of_core(layer_index, member):
-        split = whole(layer_index, member).reshape(net.high, 2, -1)
-        return lax.dynamic_index_in_dim(split, net.core, 1, keepdims=False).reshape(-1)
-
-    def small_of(layer_index):
-        bias_q = of_core(layer_index, 0)
-        bias_qkv = jnp.concatenate([bias_q, jnp.zeros_like(bias_q), of_core(layer_index, 1)])
-        return (
-            bias_qkv,
-            whole(layer_index, 2).reshape(-1),
-            of_core(layer_index, 3),
-        ) + tuple(whole(layer_index, member).reshape(-1) for member in (4, 5, 6, 7, 8))
-
     tokens = inputs.shape[0]
     dims = Dims(shard_count, rep_count, net.step, layer_count, tokens, width, w_up.shape[2])
-
-    def wide_row(row):
-        return jnp.pad(row, (0, dims.hidden // 2 - row.shape[0]))
-
-    small = jnp.stack(
-        [jnp.stack([wide_row(row) for row in small_of(layer)]) for layer in range(layer_count)]
-    )
-    results = run_layers(
-        dims,
-        inputs,
-        cotangent,
-        segments,
-        small,
-        (by_half(w_qkv, net, 3), w_out, by_half(w_up, net, 1), w_down),
-    )
+    if dims.direct:
+        vector_in = packed.reshape(dims.vector_rows, rows_here).astype(wide)
+        matrices = (w_qkv, w_out, w_up, w_down)
+    else:
+        vector_in = gathered_vectors(net, dims, packed)
+        matrices = (by_half(w_qkv, net, 3), w_out, by_half(w_up, net, 1), w_down)
+    results = run_layers(dims, inputs, cotangent, segments, vector_in, matrices)
     output, tops, vector_terms, input_grad = results[:4]
     done, swapped = results[-6:-2], results[-2:]
 
-    local = tops[:, :, 0]
-    local = net.in_order(local, net.over_core(local), net.core)
-    local = local.reshape(2, layer_count, net.high, -1).transpose(1, 2, 0, 3).reshape(layer_count, HEADS)
-    for bit in range(net.bits):
-        local = jnp.maximum(local, net.over_bit(local, bit))
-    step = 1
-    while step < net.reps:
-        local = jnp.maximum(
-            local, lax.ppermute(local, "rep", [(i, i ^ step) for i in range(net.reps)])
-        )
-        step *= 2
-    peak = local
-
-    def own_rows(value):
-        split = value.reshape(layer_count, 2, rows_here, value.shape[2])
-        return lax.dynamic_index_in_dim(split, net.core, 1, keepdims=False)
-
-    large = (
-        whole_columns(own_rows(done[0]), swapped[0], net, 3),
-        done[1].astype(wide),
-        whole_columns(own_rows(done[2]), swapped[1], net, 1),
-        done[3].astype(wide),
-    )
-    half_width, half_hidden = width // 2, dims.hidden // 2
-    lengths_here = (half_width, half_width, width, half_hidden) + (width,) * 5
-    terms_all = [
-        [vector_terms[layer, row, :length] for row, length in enumerate(lengths_here)]
-        for layer in range(layer_count)
+    if dims.direct:
+        vector_grads, peak = results[4:6]
+        vector_grads = vector_grads.reshape(layer_count, -1, rows_here)
+        peak = peak[:, :, 0].reshape(2, layer_count, net.high, -1)
+        peak = peak.transpose(1, 2, 0, 3).reshape(layer_count, HEADS)
+        full = swapped[0], done[1], swapped[1], done[3]
+    else:
+        vector_grads, peak = summed_vectors(net, dims, vector_terms, tops)
+        paired = [whole_columns(own_rows(net, done[k]), swapped[k // 2], net, 3 - k) for k in (0, 2)]
+        full = paired[0], done[1], paired[1], done[3]
+    large = tuple(value.astype(wide) for value in full)
+    ends = [sum(lengths[: member + 1]) for member in range(len(lengths))]
+    vector_grads = [
+        vector_grads[:, end - length : end].reshape(layer_count, -1)
+        for end, length in zip(ends, lengths)
     ]
-
-    def placed(value, member):
-        if member in (0, 1, 3):
-            value = value.reshape(net.high, 1, net.step, lengths[member], rows_here)
-            zero = jnp.zeros_like(value)
-            first = net.core == 0
-            return jnp.concatenate(
-                [jnp.where(first, value, zero), jnp.where(first, zero, value)], axis=1
-            )
-        return value.reshape(net.high, 2, net.step, lengths[member], rows_here)
-
-    terms = jnp.stack(
-        [
-            jnp.concatenate(
-                [placed(value, member) for member, value in enumerate(terms_all[layer_index])], axis=3
-            )
-            for layer_index in range(layer_count)
-        ],
-        axis=3,
-    )
-    theirs = lax.dynamic_index_in_dim(terms, 1 - net.core, 1, keepdims=False)
-    ours = lax.dynamic_index_in_dim(terms, net.core, 1, keepdims=False)
-    terms = ours + net.over_core(theirs)
-    terms = terms.reshape((net.pairs,) + terms.shape[2:])
-    terms = net.sum_reps(net.scatter_chips(terms, list(range(net.bits))))
-    vector_grads = []
-    start = 0
-    for length in lengths:
-        vector_grads.append(terms[:, start : start + length].reshape(layer_count, -1))
-        start += length
-
     factor = jnp.sqrt(tau / jnp.maximum(peak, tau))
     column_scale = jnp.repeat(factor, head_dim, axis=1)
     both_scale = jnp.concatenate([column_scale, column_scale], axis=1)

time: 618 us -> 514 us (0.83)
  local copies, waits for them, and re-layouts: 45.3 us -> 11.6 us
  Pallas kernels: 517 us -> 488 us
  waiting for transfers between devices: 20.9 us -> 0 us
  starting transfers between devices: 16.7 us -> 0 us
    pallas_call x1, Pallas kernels: 517 us -> 488 us  [run_layers(): pl.pallas_call(functools.partial(layers_kernel, dims), out_shape=outs, in...]
    ppermute x14 -> x0, waiting for transfers between devices: 20.9 us -> none  [the longest x1 6.68 us: sum_reps(): got = lax.ppermute(total, 'rep', [(i + 1, i), (reps - 2 - i, reps - 1 - i)])]
    ppermute x14 -> x0, starting transfers between devices: 16.7 us -> none  [the longest x6 9.32 us: over_bit(): lax.ppermute(value, 'shard', [(i, i ^ step) for i in range(self.shards)])]
    unnamed x31 -> x20, local copies, waits for them, and re-layouts: 18 us -> 2.4 us
    reshape x9 -> x11, local copies, waits for them, and re-layouts: 13.8 us -> 6.9 us  [the longest x9 5.96 us: shards(): vector.reshape(layer_count, -1, rows_here)]
  transfers between devices with their start and end apart: 14 -> 0, of which waited for: 8 -> 0; matrix products, arithmetic and copies ran while one was open for 7% -> 0% of each run, Pallas kernels for 0% -> 0%
where the time goes in v4:
time: 514 us; the launch traced here: 512 us
  Pallas kernels  488 us (95%)
  local copies, waits for them, and re-layouts  11.6 us (2%)
  other arithmetic  11.5 us (2%)
    pallas_call x1, Pallas kernels, run_layers(): pl.pallas_call(functools.partial(layers_kernel, dims), out_shape=outs, in...  488 us

profile of v4, /device:TPU:0, one launch (start us, length us, event | category | flops | bytes accessed | tf_op | source)
XLA Modules:
  0.0 512.2 jit_solution(3943113870072823587)
XLA Ops:
  0.7 0.7 reshape.104
  1.3 0.7 copy.51
  2.0 0.7 copy.52
  2.7 0.7 copy.53
  3.3 0.7 copy.54
  4.0 0.7 copy.55
  4.6 0.7 copy.56
  5.3 0.7 copy.57
  6.0 0.7 copy.58
  6.6 0.1 concatenate.6
  6.7 0.6 reshape.122.refs_3_
  7.3 0.0 copy-start.6
  7.3 0.0 copy-start.7
  7.3 488.4 %layers.1 = (bf16[256,1024]{1,0:T(8,128)(2,1)}, f32[2,8,128]{2,1,0:T(8,128)}, f32[2,16,2048]{2,1,0:T(8,128)}, f32[256,1024]{1,0:T(8,128)}, f32[24,128]{1,0:T(8,1...) custom-call(bf16[256,1024]{1,0:T(8,128)(2,1)} %refs_0_.1, ...), custom_call_target="tpu_custom_call" | custom-call | tf_op jit(solution)/shard_map/layers/pallas_call | solution.py:1334
  495.7 0.0 copy-start.1
  495.7 0.9 reshape.110
  496.5 0.6 fusion.1
  497.1 0.8 slice_reduce_fusion
  497.9 0.1 reshape_squeeze.3
  498.0 0.1 reshape.120
  498.1 0.0 copy-done.6
  498.1 0.1 broadcast_in_dim.4
  498.2 0.1 reshape.121
  498.3 0.0 copy-done.7
  498.3 0.6 dynamic-slice_multiply_fusion
  498.9 2.8 convert_multiply_fusion
  501.7 0.6 copy.62
  502.3 0.0 copy-done.1
  502.3 0.0 copy-start
  502.3 2.5 convert_element_type.27
  504.8 0.0 copy-done
  504.8 0.0 copy-start.2
  504.8 2.5 convert_element_type.28
  507.3 0.0 copy-done.2
  507.3 0.0 copy-start.4
  507.3 0.0 copy-start.5
  507.3 2.0 convert_element_type.25
  509.3 0.0 copy-start.3
  509.3 0.0 copy-done.4
  509.3 1.1 convert_element_type.26
  510.4 0.0 copy-done.5
  510.4 0.8 copy.65
  511.2 0.0 copy-done.3
  511.2 1.0 copy.66
  (4 shorter events, 0.0 us)
Async XLA Ops:
  7.3 490.8 %copy-start.6 = (f32[2,16]{1,0:T(2,128)S(1)}, f32[2,16]{1,0:T(2,128)}, u32[]{:S(2)}) copy-start(f32[2,16]{1,0:T(2,128)} %param.33) | copy-start | bytes 388
  7.3 491.0 %copy-start.7 = (bf16[2,128]{1,0:T(2,128)(2,1)S(1)}, bf16[2,128]{1,0:T(2,128)(2,1)}, u32[]{:S(2)}) copy-start(bf16[2,128]{1,0:T(2,128)(2,1)} %param.24) | copy-start | bytes 1540
  495.7 6.6 %copy-start.1 = (bf16[2,128,4096]{2,1,0:T(8,128)(2,1)S(1)}, bf16[2,128,4096]{2,1,0:T(8,128)(2,1)}, u32[]{:S(2)}) copy-start(bf16[2,128,4096]{2,1,0:T(8,128)(2,1)} %get-tuple-element.29) | copy-start | bytes 6291460
  502.3 2.5 copy-start
  504.8 2.5 copy-start.2
  507.3 2.0 copy-start.4
  507.3 3.1 copy-start.5
  509.3 1.9 copy-start.3

commit v5 on v4

--- a/solution.py
+++ b/solution.py
@@ -10,7 +10,12 @@
 
 HEADS = 16
 MESH = pl.DeviceIdType.MESH
-LEAD = 0
+LEAD = 1
+CUTS = 2
+AHEAD = 1
+GROUPS = ((0,), (1, 2, 3, 4, 5))
+IN_PLANE_FIRST = (11, 10, 10, 12)
+IN_PLANE = (11, 10, 10, 12)
 
 
 epsilon = 1e-05
@@ -166,6 +171,7 @@
         self.lengths = (1, 1, 1, hidden // width, 1, 1, 1, 1, 1)
         self.vector_rows = layers * sum(self.lengths)
         self.direct = self.rows % 128 == 0 and step == 1
+        self.cuts = tuple(CUTS if self.direct and kind != 1 else 1 for kind in range(4))
 
 
 def remote(src, dst, send, recv, where):
@@ -175,14 +181,17 @@
 
 
 class Gather:
-    def __init__(self, place, layer, kind, source, whole, sems, in_plane):
+    def __init__(self, place, layer, kind, cut, source, whole, sems, last):
         self.place, self.dims = place, place.dims
         self.layer, self.kind = layer, kind
         self.source, self.whole = source, whole
-        self.rows, self.held, self.columns, self.paired = self.dims.kinds[kind]
+        self.rows, self.held, columns, self.paired = self.dims.kinds[kind]
         self.local, self.send, self.recv = sems
-        self.at = layer * 4 + kind
-        self.in_plane = in_plane
+        self.cut, self.cuts = cut, self.dims.cuts[kind]
+        self.columns = columns // self.cuts
+        self.base = cut * self.columns
+        self.at = (layer * 4 + kind) * CUTS + cut
+        self.in_plane = in_plane = in_plane_columns(self.dims, layer, kind, self.columns, last)
         self.stage = 0
         self.stages = self.dims.bits + (2 if in_plane < self.columns else 1)
 
@@ -202,7 +211,7 @@
             offset = 0 if part == 0 else low_size
         else:
             offset = part * size
-        start = self.place.plane * (self.columns - self.in_plane) + offset
+        start = self.base + self.place.plane * (self.columns - self.in_plane) + offset
         return pl.ds(pl.multiple_of(start, 128), size), size
 
     def order(self, part):
@@ -234,8 +243,11 @@
                 ).start()
         else:
             rows = pl.ds(pl.multiple_of(place.pair * self.rows, 16), self.rows)
+            columns = pl.ds(self.base, self.columns)
             pltpu.make_async_copy(
-                self.source.at[self.layer], self.whole.at[self.layer, rows], self.local.at[self.at]
+                self.source.at[self.layer, :, columns],
+                self.whole.at[self.layer, rows, columns],
+                self.local.at[self.at],
             ).start()
 
     def begin_blocks(self):
@@ -247,7 +259,8 @@
                 self.source.at[self.layer, place.half],
             )
             return
-        for block in range(self.dims.blocks[self.kind]):
+        count = self.dims.blocks[self.kind] // self.cuts
+        for block in range(self.cut * count, (self.cut + 1) * count):
             to = pl.ds(block * width, width)
             starts = [(2 * block + half) * width for half in (1 - place.half, place.half)]
             theirs, ours = (
@@ -285,7 +298,7 @@
     def across(self):
         place = self.place
         size = self.columns - self.in_plane
-        columns = pl.ds(pl.multiple_of(place.plane * self.in_plane, 128), size)
+        columns = pl.ds(pl.multiple_of(self.base + place.plane * self.in_plane, 128), size)
         at = 1 + 2 * self.dims.bits
         for pair in self.subset(range(self.dims.bits))[1:]:
             starts, count = self.blocks(pair)
@@ -337,16 +350,18 @@
 
 
 class Reduce:
-    def __init__(self, place, layer, kind, part, terms, arrived, lines, done, swapped, sems, bufs):
+    def __init__(self, place, layer, kind, cut, part, terms, arrived, lines, done, swapped, sems, bufs):
         self.place, self.dims = place, place.dims
         self.layer, self.kind, self.part = layer, kind, part
         self.terms, self.arrived, self.lines, self.done, self.swapped = terms, arrived, lines, done, swapped
         self.send, self.recv, self.own_sem = sems
         self.mine, self.other, self.load_sem, self.store_sem = bufs
         self.rows, self.held, self.columns, self.paired = self.dims.kinds[kind]
-        self.size = self.columns // 2
-        self.columns_here = pl.ds(part * self.size, self.size)
-        self.at = (layer * 4 + kind) * 2 + part
+        cuts = self.dims.cuts[kind]
+        self.slice_at, self.slices = cut * 2 + part, 2 * cuts
+        self.size = self.columns // self.slices
+        self.columns_here = pl.ds(self.slice_at * self.size, self.size)
+        self.at = ((layer * 4 + kind) * CUTS + cut) * 2 + part
         bits = list(range(self.dims.bits))
         self.order = bits if part == 0 else bits[::-1]
         self.moves = self.dims.reps - 1
@@ -523,8 +538,8 @@
 
     def part_blocks(self):
         width = self.dims.block[self.kind]
-        count = self.dims.blocks[self.kind] // 2
-        for block in range(self.part * count, (self.part + 1) * count):
+        count = self.dims.blocks[self.kind] // self.slices
+        for block in range(self.slice_at * count, (self.slice_at + 1) * count):
             place = (2 * block + self.place.half) * width
             yield pl.ds(block * width, width), pl.ds(pl.multiple_of(place, 128), width)
 
@@ -587,6 +602,55 @@
             self.finish_swap()
         self.stage += 1
 
+    def additions(self, turn):
+        bits, half = self.dims.bits, self.dims.reps // 2
+        if turn < bits:
+            wholes = [
+                (
+                    self.block(self.terms, index, turn, False),
+                    self.block(self.arrived[turn], index, turn, False),
+                    self.block(self.terms, index, turn, False),
+                )
+                for index in range(self.count(turn))
+            ]
+        elif turn - bits < half:
+            move = turn - bits
+            result = self.own(0) if move < half - 1 else self.final(0)
+            wholes = [(self.own(0), self.line(move, 0), result)]
+        else:
+            wholes = []
+        step = min(self.piece, 256)
+        return [
+            tuple(ref.at[pl.ds(start, step)] for ref in refs)
+            for refs in wholes
+            for start in range(0, self.piece, step)
+        ]
+
+    def arrive(self, turn):
+        bits = self.dims.bits
+        if turn < bits:
+            self.turn_bytes(turn).wait_recv()
+        elif turn < bits + self.moves:
+            self.move_bytes(turn - bits).wait_recv()
+        else:
+            self.finish_swap()
+
+    def taking_part(self, turn):
+        bits = self.dims.bits
+        if not bits <= turn < bits + self.moves:
+            return True
+        receivers = self.roles(turn - bits)[1]
+        return jnp.logical_or(self.place.rep == receivers[0], self.place.rep == receivers[1])
+
+    def depart(self, turn):
+        bits = self.dims.bits
+        if turn < bits:
+            self.start_turn(turn)
+        elif turn < bits + self.moves:
+            self.start_move(turn - bits)
+        elif self.paired and turn == bits + self.moves:
+            self.start_swap()
+
     def reach(self, stage):
         while self.stage < min(stage, self.stages):
             self.advance()
@@ -611,12 +675,12 @@
     return pl.when(condition)
 
 
-def in_plane_columns(dims, layer, kind):
-    columns = dims.kinds[kind][2]
-    if dims.reps % 2:
+def in_plane_columns(dims, layer, kind, columns, last):
+    if dims.reps % 2 or last:
         return columns
     blocks = columns // 128
-    return {12: 8, 8: 6, 16: 10}.get(blocks, blocks - blocks // 3) * 128
+    share = IN_PLANE[kind] if layer else IN_PLANE_FIRST[kind]
+    return max(blocks * share // 16, blocks - blocks // 2) * 128
 
 
 def few(count, body):
@@ -655,7 +719,9 @@
     def take(count):
         return [next(refs) for _ in range(count)]
 
-    x_ref, cotangent, seg_row, vector_ref = take(4)
+    x_ref, cotangent, seg_row = take(3)
+    vector_refs = take(9) if dims.direct else None
+    vector_ref = None if dims.direct else take(1)[0]
     src_qkv, src_out, src_up, src_down = take(4)
     output, tops, vectors, input_grad = take(4)
     vector_out, peak_out = take(2) if dims.direct else (None, None)
@@ -668,13 +734,13 @@
     hidden, first, total, away, back, bias, both_grad, ring, add_mine, add_other = take(10)
     seg_here, seg_rows = take(2)
     if dims.direct:
-        vector_all, small, vector_away, vector_back, line_back = take(5)
+        vector_all, small, vector_away, vector_back, line_back, vector_here = take(6)
     else:
         small = vector_ref
     gather_local, gather_send, gather_recv, mate_send, mate_recv = take(5)
     reduce_send, reduce_recv, own_sem, load_sem, store_sem, ring_sem, io_sem = take(7)
     if dims.direct:
-        vector_send, vector_recv = take(2)
+        vector_send, vector_recv, pool_load, pool_store = take(4)
     place = Place(dims)
     tokens, width = dims.tokens, dims.width
     heads_row = 128 // dims.head_dim
@@ -702,13 +768,15 @@
             place,
             layer,
             kind,
+            cut,
             sources[kind],
             wholes[kind],
             (gather_local, gather_send, gather_recv),
-            in_plane_columns(dims, layer, kind),
+            layer == dims.layers - 1 and kind == 3 and cut == dims.cuts[kind] - 1,
         )
         for layer in range(dims.layers)
         for kind in range(4)
+        for cut in range(dims.cuts[kind])
     ]
 
     exchanges = []
@@ -731,14 +799,22 @@
 
         def send_vector(index):
             remote(
-                vector_ref,
+                vector_here,
                 vector_all.at[place.me],
                 vector_send.at[0],
                 vector_recv.at[0],
                 in_group(index + 1),
             ).start()
 
-        vector_all[place.me] = vector_ref[...]
+        at = 0
+        for layer in range(dims.layers):
+            for ref, length in zip(vector_refs, dims.lengths):
+                values = ref[...].astype(wide)
+                for block in range(length):
+                    lanes = slice(block * dims.rows, (block + 1) * dims.rows)
+                    vector_here[at : at + 1, :] = values[layer : layer + 1, lanes]
+                    at += 1
+        vector_all[place.me] = vector_here[...]
         few(shards - 1, send_vector)
     x_copy = pltpu.make_async_copy(x_ref, both_hidden.at[0, pl.ds(0, tokens)], io_sem.at[0])
     cotangent_copy = pltpu.make_async_copy(cotangent, both_grad.at[pl.ds(0, tokens)], io_sem.at[1])
@@ -750,12 +826,20 @@
         gather.begin()
     turns = []
 
+    def turn_on():
+        now = len(turns)
+        turns.append(now)
+        for number, gather in reversed(list(enumerate(gathers))):
+            gather.reach(max(now - number + 1, 1 if number <= now + LEAD else 0))
+
     def prepare(at):
-        while len(turns) < at + gathers[at].stages:
-            now = len(turns)
-            turns.append(now)
-            for number, gather in enumerate(gathers):
-                gather.reach(max(now - number + 1, 1 if number <= now + LEAD else 0))
+        last = max(
+            number
+            for number, gather in enumerate(gathers)
+            if gather.layer * 4 + gather.kind == at
+        )
+        while len(turns) < last + gathers[last].stages:
+            turn_on()
 
     hidden[...] = both_hidden[0, pl.ds(0, tokens)].astype(wide)
     vectors[...] = jnp.zeros(vectors.shape, wide)
@@ -864,7 +948,10 @@
                 outs, axis=1
             ).astype(low)
 
-        tiles(2 * lane_blocks, attend)
+        turn_on()
+        tiles(lane_blocks, attend)
+        turn_on()
+        tiles(lane_blocks, lambda j, attend=attend: attend(j + lane_blocks))
 
         prepare(4 * layer + 1)
         project(
@@ -940,12 +1027,15 @@
                 both_hidden.at[layer + 1, pl.ds(0, tokens)],
                 both_hidden.at[layer + 1, pl.ds(tokens, tokens)],
             )
-    reduces = {
-        (layer, kind): [
+    for gather in gathers:
+        gather.finish_sends()
+    queue = [
+        [
             Reduce(
                 place,
                 layer,
                 kind,
+                cut,
                 part,
                 terms[kind],
                 [arrived[turn][kind] for turn in range(dims.bits)],
@@ -957,15 +1047,84 @@
             )
             for part in range(2)
         ]
-        for layer in range(dims.layers)
-        for kind in range(4)
-    }
-    queue = [
-        reduces[layer, kind] for layer in reversed(range(dims.layers)) for kind in (3, 2, 1, 0)
+        for layer in reversed(range(dims.layers))
+        for kind in ((3, 2, 1, 0) if layer else (3, 2, 0, 1))
+        for cut in range(dims.cuts[kind])
     ]
     stages = max(item.stages for pair in queue for item in pair)
 
-    def pump(step, ahead=2):
+    pools = [
+        (ref, row, column)
+        for ref in (w_down, w_up, act, slope, w_qkv)
+        for row in range(0, ref.shape[1] - 255, 256)
+        for column in range(0, ref.shape[2] - 1023, 1024)
+    ]
+
+    def together(items):
+        work, used = [], 0
+        for item in items:
+            turn = item.stage - 1
+            pieces = []
+            for own, other, result in item.additions(turn):
+                rows, cols = own.shape
+                pair = []
+                for ref in (own, other):
+                    pool, row, column = pools[used]
+                    slot = pool.at[dims.layers - 1, pl.ds(row, rows), pl.ds(column, cols)]
+                    pair.append((slot, pltpu.make_async_copy(ref, slot, pool_load.at[used])))
+                    used += 1
+                back_copy = pltpu.make_async_copy(pair[0][0], result, pool_store.at[used // 2 - 1])
+                pieces.append((pair, back_copy))
+            work.append((item, turn, pieces))
+        for item, turn, pieces in work:
+
+            @when(item.taking_part(turn))
+            def _(item=item, turn=turn, pieces=pieces):
+                item.arrive(turn)
+                for pair, _ in pieces:
+                    for _, copy in pair:
+                        copy.start()
+
+        for item, turn, pieces in work:
+
+            @when(item.taking_part(turn))
+            def _(pieces=pieces):
+                for pair, back_copy in pieces:
+                    for _, copy in pair:
+                        copy.wait()
+                    one, two = pair[0][0], pair[1][0]
+                    one[...] = one[...] + two[...]
+                    back_copy.start()
+
+        for item, turn, pieces in work:
+
+            @when(item.taking_part(turn))
+            def _(pieces=pieces):
+                for _, back_copy in pieces:
+                    back_copy.wait()
+
+            item.depart(turn + 1)
+            item.stage += 1
+
+    def pump_together(step, ahead):
+        if step + ahead < len(queue):
+            for item in queue[step + ahead]:
+                item.reach(1)
+        for group in GROUPS:
+            together(
+                [
+                    item
+                    for behind in group
+                    if 0 <= step - behind < len(queue)
+                    for item in queue[step - behind]
+                    if item.stage < min(2 + behind, item.stages)
+                ]
+            )
+
+    def pump(step, ahead=AHEAD):
+        if dims.direct:
+            pump_together(step, ahead)
+            return
         if step + ahead < len(queue):
             for item in queue[step + ahead]:
                 item.reach(1)
@@ -1047,7 +1206,7 @@
 
         weight_terms(layer, 3, act.at[layer], both_grad)
         if newest:
-            for item in queue[0]:
+            for item in queue[0] + queue[1]:
                 item.reach(1)
         else:
             pump(pumped)
@@ -1063,7 +1222,7 @@
         tiles(dims.hidden // 2 // narrow, down_back)
         weight_terms(layer, 2, both_first.at[layer], slope.at[layer])
         if newest:
-            for item in queue[1]:
+            for item in queue[2]:
                 item.reach(1)
         else:
             pump(pumped)
@@ -1101,9 +1260,8 @@
             attended[layer, :, cols] = dot_last(both_grad[...], w_out[layer, cols, :]).astype(low)
 
         tiles(dims.third // out_tile, out_back)
-        if not newest:
-            pump(pumped)
-            pumped += 1
+        pump(pumped)
+        pumped += 1
 
         def attend_back(j, layer=layer):
             s, block = j // lane_blocks, j % lane_blocks
@@ -1135,6 +1293,8 @@
                     count_up(layer, row, rounded.astype(wide), lanes)
 
         tiles(2 * lane_blocks, attend_back)
+        pump(pumped)
+        pumped += 1
         weight_terms(layer, 0, both_hidden.at[layer], qkv.at[layer])
         project(
             qkv.at[layer],
@@ -1229,8 +1389,6 @@
         vector_bytes(vector_all, 0, shards - 1).wait_send()
         vector_bytes(vector_back, 1, shards - 1).wait_send()
         vector_bytes(line_back, 2, reps - 1).wait_send()
-    for gather in gathers:
-        gather.finish_sends()
     for pair in queue:
         for item in pair:
             item.finish_sends()
@@ -1310,38 +1468,39 @@
                 (dims.shards, rows + layers * heads, dims.rows),
                 (dims.shards, rows + layers * heads, dims.rows),
                 (dims.reps, rows + 2 * layers * heads, dims.rows),
+                (rows, dims.rows),
             )
         ]
     slots = 2 + 2 * dims.bits
     exchange_count = 2 + 8 * layers
     reduce_slots = dims.bits + dims.reps
     scratch = scratch + [
-        dma((4 * layers,)),
-        dma((4 * layers, slots)),
-        dma((4 * layers, slots)),
+        dma((4 * layers * CUTS,)),
+        dma((4 * layers * CUTS, slots)),
+        dma((4 * layers * CUTS, slots)),
         dma((exchange_count,)),
         dma((exchange_count,)),
-        dma((8 * layers, reduce_slots)),
-        dma((8 * layers, reduce_slots)),
-        dma((8 * layers,)),
+        dma((8 * layers * CUTS, reduce_slots)),
+        dma((8 * layers * CUTS, reduce_slots)),
+        dma((8 * layers * CUTS,)),
         dma((2, 2)),
         dma((2,)),
         dma((3,)),
         dma((2,)),
     ]
     if dims.direct:
-        scratch += [dma((3,)), dma((3,))]
+        scratch += [dma((3,)), dma((3,)), dma((32,)), dma((16,))]
     return pl.pallas_call(
         functools.partial(layers_kernel, dims),
         out_shape=outs,
-        in_specs=[anywhere] * 2 + [vmem] * 2 + [anywhere] * 4,
+        in_specs=[anywhere] * 2 + [vmem] * (1 + len(vectors)) + [anywhere] * 4,
         out_specs=[vmem] * 3 + [anywhere] + [vmem] * len(summed) + [anywhere] * (len(outs) - 4 - len(summed)),
         scratch_shapes=scratch,
         compiler_params=pltpu.CompilerParams(
             collective_id=0, has_side_effects=True, vmem_limit_bytes=63 * 2**20 + 2**19
         ),
         name="layers",
-    )(x, cotangent, segments, vectors, *weights)
+    )(x, cotangent, segments, *vectors, *weights)
 
 
 def own_rows(net, value):
@@ -1460,16 +1619,16 @@
         norm2_bias,
     )
     lengths = [vector.shape[1] // rows_here for vector in vectors]
-    packed = jnp.concatenate(
-        [vector.reshape(layer_count, -1, rows_here) for vector in vectors], axis=1
-    )
     tokens = inputs.shape[0]
     dims = Dims(shard_count, rep_count, net.step, layer_count, tokens, width, w_up.shape[2])
     if dims.direct:
-        vector_in = packed.reshape(dims.vector_rows, rows_here).astype(wide)
+        vector_in = vectors
         matrices = (w_qkv, w_out, w_up, w_down)
     else:
-        vector_in = gathered_vectors(net, dims, packed)
+        packed = jnp.concatenate(
+            [vector.reshape(layer_count, -1, rows_here) for vector in vectors], axis=1
+        )
+        vector_in = (gathered_vectors(net, dims, packed),)
         matrices = (by_half(w_qkv, net, 3), w_out, by_half(w_up, net, 1), w_down)
     results = run_layers(dims, inputs, cotangent, segments, vector_in, matrices)
     output, tops, vector_terms, input_grad = results[:4]

time: 514 us -> 462 us (0.90)
  Pallas kernels: 488 us -> 444 us
  local copies, waits for them, and re-layouts: 11.6 us -> 5 us
    pallas_call x1, Pallas kernels: 488 us -> 444 us  [run_layers(): pl.pallas_call(functools.partial(layers_kernel, dims), out_shape=outs, in...]
    reshape x9 -> x0, local copies, waits for them, and re-layouts: 5.96 us -> none  [shards(): vector.reshape(layer_count, -1, rows_here)]
where the time goes in v5:
time: 462 us; the launch traced here: 461 us
  Pallas kernels  444 us (96%)
  other arithmetic  11.5 us (2%)
  local copies, waits for them, and re-layouts  5 us (1%)
    pallas_call x1, Pallas kernels, run_layers(): pl.pallas_call(functools.partial(layers_kernel, dims), out_shape=outs, in...  444 us

profile of v5, /device:TPU:0, one launch (start us, length us, event | category | flops | bytes accessed | tf_op | source)
XLA Modules:
  0.0 460.8 jit_solution(14961236367387430680)
XLA Ops:
  0.7 0.0 copy-start.6
  0.7 0.0 copy-start.7
  0.7 443.5 %layers.1 = (bf16[256,1024]{1,0:T(8,128)(2,1)}, f32[2,8,128]{2,1,0:T(8,128)}, f32[2,16,2048]{2,1,0:T(8,128)}, f32[256,1024]{1,0:T(8,128)}, f32[24,128]{1,0:T(8,1...) custom-call(bf16[256,1024]{1,0:T(8,128)(2,1)} %refs_0_.1, ...), custom_call_target="tpu_custom_call" | custom-call | tf_op jit(solution)/shard_map/layers/pallas_call | solution.py:1493
  444.2 0.0 copy-start.1
  444.2 0.9 reshape.71
  445.1 0.6 fusion.1
  445.7 0.8 slice_reduce_fusion
  446.5 0.1 reshape_squeeze.3
  446.6 0.1 reshape.81
  446.7 0.0 copy-done.7
  446.7 0.1 broadcast_in_dim.4
  446.8 0.1 reshape.82
  446.9 0.0 copy-done.6
  446.9 0.6 dynamic-slice_multiply_fusion
  447.5 2.8 convert_multiply_fusion
  450.3 0.6 copy.46
  450.9 0.0 copy-done.1
  450.9 0.0 copy-start
  450.9 2.5 convert_element_type.20
  453.4 0.0 copy-done
  453.4 0.0 copy-start.2
  453.4 2.5 convert_element_type.21
  455.9 0.0 copy-done.2
  455.9 0.0 copy-start.4
  455.9 0.0 copy-start.5
  455.9 2.0 convert_element_type.18
  457.9 0.0 copy-start.3
  457.9 0.0 copy-done.4
  457.9 1.1 convert_element_type.19
  459.0 0.0 copy-done.5
  459.0 0.8 copy.49
  459.8 0.0 copy-done.3
  459.8 1.0 copy.50
  (4 shorter events, 0.0 us)
Async XLA Ops:
  0.7 446.2 %copy-start.6 = (bf16[2,128]{1,0:T(2,128)(2,1)S(1)}, bf16[2,128]{1,0:T(2,128)(2,1)}, u32[]{:S(2)}) copy-start(bf16[2,128]{1,0:T(2,128)(2,1)} %refs_3_.1) | copy-start | bytes 1540
  0.7 446.0 %copy-start.7 = (f32[2,16]{1,0:T(2,128)S(1)}, f32[2,16]{1,0:T(2,128)}, u32[]{:S(2)}) copy-start(f32[2,16]{1,0:T(2,128)} %param.33) | copy-start | bytes 388
  444.2 6.6 %copy-start.1 = (bf16[2,128,4096]{2,1,0:T(8,128)(2,1)S(1)}, bf16[2,128,4096]{2,1,0:T(8,128)(2,1)}, u32[]{:S(2)}) copy-start(bf16[2,128,4096]{2,1,0:T(8,128)(2,1)} %get-tuple-element.29) | copy-start | bytes 6291460
  450.9 2.5 copy-start
  453.4 2.5 copy-start.2
  455.9 2.0 copy-start.4
  455.9 3.1 copy-start.5
  457.9 1.9 copy-start.3

commit v6 on v5

--- a/solution.py
+++ b/solution.py
@@ -1047,8 +1047,9 @@
             )
             for part in range(2)
         ]
+        for kinds in ((3, 2), (0,), (1,))
         for layer in reversed(range(dims.layers))
-        for kind in ((3, 2, 1, 0) if layer else (3, 2, 0, 1))
+        for kind in kinds
         for cut in range(dims.cuts[kind])
     ]
     stages = max(item.stages for pair in queue for item in pair)
@@ -1221,10 +1222,7 @@
 
         tiles(dims.hidden // 2 // narrow, down_back)
         weight_terms(layer, 2, both_first.at[layer], slope.at[layer])
-        if newest:
-            for item in queue[2]:
-                item.reach(1)
-        else:
+        if not newest:
             pump(pumped)
             pumped += 1
         exchange_at = 2 * (dims.layers - 1 - layer)

time: 462 us -> 444 us (0.961)
  Pallas kernels: 444 us -> 426 us
    pallas_call x1, Pallas kernels: 444 us -> 426 us  [run_layers(): pl.pallas_call(functools.partial(layers_kernel, dims), out_shape=outs, in...]
where the time goes in v6:
time: 444 us; the launch traced here: 443 us
  Pallas kernels  426 us (96%)
  other arithmetic  11.5 us (3%)
  local copies, waits for them, and re-layouts  5 us (1%)
    pallas_call x1, Pallas kernels, run_layers(): pl.pallas_call(functools.partial(layers_kernel, dims), out_shape=outs, in...  426 us

profile of v6, /device:TPU:0, one launch (start us, length us, event | category | flops | bytes accessed | tf_op | source)
XLA Modules:
  0.0 443.2 jit_solution(11432855097321479690)
XLA Ops:
  0.7 0.0 copy-start.6
  0.7 0.0 copy-start.7
  0.7 426.0 %layers.1 = (bf16[256,1024]{1,0:T(8,128)(2,1)}, f32[2,8,128]{2,1,0:T(8,128)}, f32[2,16,2048]{2,1,0:T(8,128)}, f32[256,1024]{1,0:T(8,128)}, f32[24,128]{1,0:T(8,1...) custom-call(bf16[256,1024]{1,0:T(8,128)(2,1)} %refs_0_.1, ...), custom_call_target="tpu_custom_call" | custom-call | tf_op jit(solution)/shard_map/layers/pallas_call | solution.py:1491
  426.7 0.0 copy-start.1
  426.7 0.9 reshape.71
  427.5 0.6 fusion.1
  428.1 0.8 slice_reduce_fusion
  428.9 0.1 reshape_squeeze.3
  429.0 0.1 reshape.81
  429.1 0.0 copy-done.7
  429.2 0.1 broadcast_in_dim.4
  429.2 0.1 reshape.82
  429.3 0.0 copy-done.6
  429.3 0.6 dynamic-slice_multiply_fusion
  429.9 2.8 convert_multiply_fusion
  432.7 0.6 copy.46
  433.3 0.0 copy-done.1
  433.3 0.0 copy-start
  433.3 2.5 convert_element_type.20
  435.8 0.0 copy-done
  435.8 0.0 copy-start.2
  435.8 2.5 convert_element_type.21
  438.3 0.0 copy-done.2
  438.3 0.0 copy-start.4
  438.3 0.0 copy-start.5
  438.3 2.0 convert_element_type.18
  440.3 0.0 copy-start.3
  440.3 0.0 copy-done.4
  440.4 1.1 convert_element_type.19
  441.4 0.0 copy-done.5
  441.4 0.8 copy.49
  442.2 0.0 copy-done.3
  442.2 1.0 copy.50
  (4 shorter events, 0.0 us)
Async XLA Ops:
  0.7 428.7 %copy-start.6 = (bf16[2,128]{1,0:T(2,128)(2,1)S(1)}, bf16[2,128]{1,0:T(2,128)(2,1)}, u32[]{:S(2)}) copy-start(bf16[2,128]{1,0:T(2,128)(2,1)} %refs_3_.1) | copy-start | bytes 1540
  0.7 428.5 %copy-start.7 = (f32[2,16]{1,0:T(2,128)S(1)}, f32[2,16]{1,0:T(2,128)}, u32[]{:S(2)}) copy-start(f32[2,16]{1,0:T(2,128)} %param.33) | copy-start | bytes 388
  426.7 6.6 %copy-start.1 = (bf16[2,128,4096]{2,1,0:T(8,128)(2,1)S(1)}, bf16[2,128,4096]{2,1,0:T(8,128)(2,1)}, u32[]{:S(2)}) copy-start(bf16[2,128,4096]{2,1,0:T(8,128)(2,1)} %get-tuple-element.29) | copy-start | bytes 6291460
  433.3 2.5 copy-start
  435.8 2.5 copy-start.2
  438.3 2.0 copy-start.4
  438.3 3.1 copy-start.5
  440.3 1.9 copy-start.3

commit v7 on v6

--- a/solution.py
+++ b/solution.py
@@ -1107,10 +1107,16 @@
             item.depart(turn + 1)
             item.stage += 1
 
+    ready = set()
+
+    def start_ready(last):
+        for items in queue[: last + 1]:
+            for item in items:
+                if (item.layer, item.kind) in ready:
+                    item.reach(1)
+
     def pump_together(step, ahead):
-        if step + ahead < len(queue):
-            for item in queue[step + ahead]:
-                item.reach(1)
+        start_ready(step + ahead)
         for group in GROUPS:
             together(
                 [
@@ -1118,7 +1124,7 @@
                     for behind in group
                     if 0 <= step - behind < len(queue)
                     for item in queue[step - behind]
-                    if item.stage < min(2 + behind, item.stages)
+                    if 0 < item.stage < min(2 + behind, item.stages)
                 ]
             )
 
@@ -1126,16 +1132,16 @@
         if dims.direct:
             pump_together(step, ahead)
             return
-        if step + ahead < len(queue):
-            for item in queue[step + ahead]:
-                item.reach(1)
+        start_ready(step + ahead)
         for behind in reversed(range(stages - 1)):
             at = step - behind
             if 0 <= at < len(queue):
                 for item in queue[at]:
-                    item.reach(2 + behind)
+                    if item.stage:
+                        item.reach(2 + behind)
 
     def weight_terms(layer, kind, left, right):
+        ready.add((layer, kind))
         _, held, columns, _ = dims.kinds[kind]
         step = min(256, held)
         wide_cols = columns if columns <= ring.shape[2] else columns // 2
@@ -1207,8 +1213,7 @@
 
         weight_terms(layer, 3, act.at[layer], both_grad)
         if newest:
-            for item in queue[0] + queue[1]:
-                item.reach(1)
+            start_ready(1)
         else:
             pump(pumped)
             pumped += 1

time: 444 us -> 444 us (level)
  no operation moved by 1% of the time
where the time goes in v7:
time: 444 us; the launch traced here: 443 us
  Pallas kernels  426 us (96%)
  other arithmetic  11.5 us (3%)
  local copies, waits for them, and re-layouts  5 us (1%)
    pallas_call x1, Pallas kernels, run_layers(): pl.pallas_call(functools.partial(layers_kernel, dims), out_shape=outs, in...  426 us

profile of v7, /device:TPU:0, one launch (start us, length us, event | category | flops | bytes accessed | tf_op | source)
XLA Modules:
  0.0 443.2 jit_solution(11432855097321479690)
XLA Ops:
  0.7 0.0 copy-start.6
  0.7 0.0 copy-start.7
  0.7 426.0 %layers.1 = (bf16[256,1024]{1,0:T(8,128)(2,1)}, f32[2,8,128]{2,1,0:T(8,128)}, f32[2,16,2048]{2,1,0:T(8,128)}, f32[256,1024]{1,0:T(8,128)}, f32[24,128]{1,0:T(8,1...) custom-call(bf16[256,1024]{1,0:T(8,128)(2,1)} %refs_0_.1, ...), custom_call_target="tpu_custom_call" | custom-call | tf_op jit(solution)/shard_map/layers/pallas_call | solution.py:1496
  426.7 0.0 copy-start.1
  426.7 0.9 reshape.71
  427.5 0.6 fusion.1
  428.1 0.8 slice_reduce_fusion
  428.9 0.1 reshape_squeeze.3
  429.0 0.1 reshape.81
  429.1 0.0 copy-done.7
  429.2 0.1 broadcast_in_dim.4
  429.2 0.1 reshape.82
  429.3 0.0 copy-done.6
  429.3 0.6 dynamic-slice_multiply_fusion
  429.9 2.8 convert_multiply_fusion
  432.7 0.6 copy.46
  433.3 0.0 copy-done.1
  433.3 0.0 copy-start
  433.3 2.5 convert_element_type.20
  435.8 0.0 copy-done
  435.8 0.0 copy-start.2
  435.8 2.5 convert_element_type.21
  438.3 0.0 copy-done.2
  438.3 0.0 copy-start.4
  438.3 0.0 copy-start.5
  438.3 2.0 convert_element_type.18
  440.3 0.0 copy-start.3
  440.3 0.0 copy-done.4
  440.4 1.1 convert_element_type.19
  441.4 0.0 copy-done.5
  441.4 0.8 copy.49
  442.2 0.0 copy-done.3
  442.2 1.0 copy.50
  (4 shorter events, 0.0 us)
Async XLA Ops:
  0.7 428.7 %copy-start.6 = (bf16[2,128]{1,0:T(2,128)(2,1)S(1)}, bf16[2,128]{1,0:T(2,128)(2,1)}, u32[]{:S(2)}) copy-start(bf16[2,128]{1,0:T(2,128)(2,1)} %refs_3_.1) | copy-start | bytes 1540
  0.7 428.5 %copy-start.7 = (f32[2,16]{1,0:T(2,128)S(1)}, f32[2,16]{1,0:T(2,128)}, u32[]{:S(2)}) copy-start(f32[2,16]{1,0:T(2,128)} %param.33) | copy-start | bytes 388
  426.7 6.6 %copy-start.1 = (bf16[2,128,4096]{2,1,0:T(8,128)(2,1)S(1)}, bf16[2,128,4096]{2,1,0:T(8,128)(2,1)}, u32[]{:S(2)}) copy-start(bf16[2,128,4096]{2,1,0:T(8,128)(2,1)} %get-tuple-element.29) | copy-start | bytes 6291460
  433.3 2.5 copy-start
  435.8 2.5 copy-start.2
  438.3 2.0 copy-start.4
  438.3 3.1 copy-start.5
  440.3 1.9 copy-start.3
